TPU v7x, 32 devices: a whole 2x2x4 slice. The times are simulated.
32 devices in a mesh: cp: 8 (over y, x, core), tp: 4 (over z).
Axes of the slice: x: 2, y: 2, z: 4, core: 2. Of those that a mesh axis runs over, the one named last changes fastest.
Arguments:
- layer_input: bfloat16 [4096, 2048], P('cp'), may hold values from -6 to 6
- seq_lengths: int32 [3], replicated, may hold values from 1024 to 2048, as said below
- active_until: int32 [3], replicated, may hold values from 896 to 2048, as said below
- ln_gains: float32 [2, 2048], replicated, may hold values from 0.1 to 1.9
- ln_shifts: float32 [2, 2048], replicated, may hold values from -1.75 to 1.75
- query_key_value_weight: bfloat16 [2048, 3, 2048], P(None, None, 'tp'), may hold values from -0.125 to 0.125
- b_qv: float32 [2, 2048], P(None, 'tp'), may hold values from -0.625 to 0.625
- w_out: bfloat16 [2048, 2048], P('tp'), may hold values from -1.5 to 1.5
- b_outs: float32 [2, 2048], replicated, may hold values from -1.75 to 1.75
- w_up: bfloat16 [2048, 8192], P(None, 'tp'), may hold values from -0.125 to 0.125
- b_up: float32 [8192], P('tp'), may hold values from -3 to 3
- w_down: bfloat16 [8192, 2048], P('tp'), may hold values from -0.0625 to 0.0625
- d_out: bfloat16 [4096, 2048], P('cp'), may hold values from -6 to 6
Outputs:
- out: float32 [4096, 2048], P('cp')
- g_x: float32 [4096, 2048], P('cp')
- g_ln_gains: float32 [2, 2048], replicated
- g_ln_shifts: float32 [2, 2048], replicated
- g_qkv: float32 [2048, 3, 2048], P('cp', None, 'tp')
- g_bqv: float32 [2, 2048], P(None, 'tp')
- g_out: float32 [2048, 2048], P('tp', 'cp')
- g_bouts: float32 [2, 2048], replicated
- g_up: float32 [2048, 8192], P('cp', 'tp')
- g_bup: float32 [8192], P('tp')
- g_down: float32 [8192, 2048], P('tp', 'cp')
Inputs may be any that keep to these rules, and one draw needn't show every extreme that they name: `seq_lengths`: two sequences have 2048 // 2 tokens and all others 2048, in an order drawn from the seed; the lengths sum to 4096. `active_until`: entry s lies between the length of sequence s minus an eighth of it (rounded down) and that length.
All inputs are finite; a program needn't handle non-finite values.
Results may differ from a plain program's by a relative error of at most 0.02.
Values may be sent and summed in bfloat16 or wider, within the bound.
A program may use at most 192 MiB of HBM per device.

v0:
```python
import jax
import jax.numpy as jnp
from jax import lax
from jax.sharding import PartitionSpec as P

HD = 64
LONG = 2048


EPS = 1e-05
NEG = -1e30


def passed_along(value, axis, steps):
    count = lax.axis_size(axis)
    first, last = (max(0, -steps), min(count, count - steps))
    return lax.ppermute(value, axis, [(source, source + steps) for source in range(first, last)])


def layer_norm(v, gain, shift):
    mean = jnp.mean(v, axis=-1, keepdims=True)
    centred = v - mean
    var = jnp.mean(centred * centred, axis=-1, keepdims=True)
    return centred * lax.rsqrt(var + EPS) * gain + shift


def gelu_tanh(v):
    return jax.nn.gelu(v, approximate=True)


def row_info(seq_lengths, active_until, first, count):
    ends = jnp.cumsum(seq_lengths)
    starts = ends - seq_lengths
    rows = first + jnp.arange(count)
    inside = (rows[:, None] >= starts[None, :]) & (rows[:, None] < ends[None, :])
    numbers = jnp.arange(seq_lengths.shape[0])
    segment = jnp.sum(jnp.where(inside, numbers[None, :] + 1, 0), axis=1) - 1
    position = rows - jnp.sum(jnp.where(inside, starts[None, :], 0), axis=1)
    limit = jnp.sum(jnp.where(inside, active_until[None, :], 0), axis=1)
    active = (position < limit).astype(jnp.float32)
    return (rows, segment, active)


def block_scores(query_h, key_h, query_rows, query_seg, key_rows, key_seg, scale):
    scores = jnp.einsum("qhd,khd->hqk", query_h, key_h, preferred_element_type=jnp.float32) * scale
    allowed = (
        (key_rows[None, :] <= query_rows[:, None])
        & (key_seg[None, :] == query_seg[:, None])
        & (key_seg[None, :] >= 0)
    )
    return (jnp.where(allowed[None], scores, NEG), allowed)


def keep_carry(acc):
    return acc


def shards(
    layer_input,
    seq_lengths,
    active_until,
    ln_gains,
    ln_shifts,
    query_key_value_weight,
    b_qv,
    w_out,
    b_outs,
    w_up,
    b_up,
    w_down,
    d_out,
):
    rows = layer_input.shape[0]
    width = query_key_value_weight.shape[2]
    heads = width // HD
    scale = HD ** (-0.5)
    bands = lax.axis_size("cp")
    total_rows = rows * bands
    reach = min(LONG, total_rows // 2) // rows - 1
    first = lax.axis_index("cp") * rows
    my_rows, my_seg, active = row_info(seq_lengths, active_until, first, rows)
    gate = active[:, None]
    input_full = layer_input.astype(jnp.float32)
    first_norm_output, ln1_pull = jax.vjp(layer_norm, input_full, ln_gains[0], ln_shifts[0])
    first_norm_lowered = first_norm_output.astype(jnp.bfloat16)
    projected_rows = jnp.einsum(
        "oa,amh->omh",
        first_norm_lowered,
        query_key_value_weight,
        preferred_element_type=jnp.float32,
    )
    q_b = (projected_rows[:, 0] + b_qv[0]).astype(jnp.bfloat16)
    k_b = projected_rows[:, 1].astype(jnp.bfloat16)
    v_b = (projected_rows[:, 2] + b_qv[1]).astype(jnp.bfloat16)
    q_h = q_b.reshape(rows, heads, HD)
    kv_own = jnp.concatenate([k_b, v_b], axis=1)

    def pass_step(index, state):
        stored, current = state
        current = passed_along(current, "cp", 1)
        return (lax.dynamic_update_index_in_dim(stored, current, index, 0), current)

    stored0 = jnp.zeros((reach + 1, rows, 2 * width), jnp.bfloat16).at[0].set(kv_own)
    kept, unused_last = lax.fori_loop(1, reach + 1, pass_step, (stored0, kv_own))

    def block_of(index):
        block = lax.dynamic_index_in_dim(kept, index, 0, keepdims=False)
        return (
            block[:, :width].reshape(rows, heads, HD),
            block[:, width:].reshape(rows, heads, HD),
        )

    def stats_step(index, acc):
        key_start = first - index * rows

        def stats_work(acc):
            keys3, unused_vals = block_of(index)
            key_rows, key_seg, unused = row_info(seq_lengths, active_until, key_start, rows)
            masked, allowed = block_scores(q_h, keys3, my_rows, my_seg, key_rows, key_seg, scale)
            top, total = acc
            new_top = jnp.maximum(top, jnp.max(masked, axis=-1))
            total = total * jnp.exp(top - new_top) + jnp.sum(
                jnp.where(allowed[None], jnp.exp(masked - new_top[:, :, None]), 0.0), axis=-1
            )
            return (new_top, total)

        return lax.cond(key_start >= 0, stats_work, keep_carry, acc)

    start_top = jnp.full((heads, rows), NEG, jnp.float32)
    start_total = jnp.zeros((heads, rows), jnp.float32)
    top, total = lax.fori_loop(0, reach + 1, stats_step, (start_top, start_total))
    lse = top + jnp.log(total)

    def value_step(index, acc):
        key_start = first - index * rows

        def value_work(acc):
            keys3, vals3 = block_of(index)
            key_rows, key_seg, unused = row_info(seq_lengths, active_until, key_start, rows)
            masked, allowed = block_scores(q_h, keys3, my_rows, my_seg, key_rows, key_seg, scale)
            probs = jnp.where(allowed[None], jnp.exp(masked - lse[:, :, None]), 0.0)
            probs_low = probs.astype(jnp.bfloat16)
            rest = (probs - probs_low.astype(jnp.float32)).astype(jnp.bfloat16)
            upper = acc[0] + jnp.einsum(
                "hqk,khd->qhd", probs_low, vals3, preferred_element_type=jnp.float32
            )
            lower = acc[1] + jnp.einsum(
                "hqk,khd->qhd", rest, vals3, preferred_element_type=jnp.float32
            )
            return (upper, lower)

        return lax.cond(key_start >= 0, value_work, keep_carry, acc)

    zero_q = jnp.zeros((rows, heads, HD), jnp.float32)
    upper, lower = lax.fori_loop(0, reach + 1, value_step, (zero_q, zero_q))
    attended_low = upper.reshape(rows, width).astype(jnp.bfloat16)
    combined = upper + lower
    attn = (
        lax.psum(
            jnp.dot(attended_low, w_out, preferred_element_type=jnp.float32).astype(jnp.bfloat16),
            "tp",
        ).astype(jnp.float32)
        + b_outs[0]
    )
    hidden_state = input_full + gate * attn
    norm2, ln2_pull = jax.vjp(layer_norm, hidden_state, ln_gains[1], ln_shifts[1])
    norm2_low = norm2.astype(jnp.bfloat16)
    pre = jnp.dot(norm2_low, w_up, preferred_element_type=jnp.float32) + b_up
    act, gelu_pull = jax.vjp(gelu_tanh, pre)
    act_low = act.astype(jnp.bfloat16)
    ffn = (
        lax.psum(
            jnp.dot(act_low, w_down, preferred_element_type=jnp.float32).astype(jnp.bfloat16), "tp"
        ).astype(jnp.float32)
        + b_outs[1]
    )
    out = hidden_state + gate * ffn
    grad_out = d_out.astype(jnp.float32)
    g_ffn = (gate * grad_out).astype(jnp.bfloat16)
    g_act = jnp.einsum("td,fd->tf", g_ffn, w_down, preferred_element_type=jnp.float32)
    g_pre = gelu_pull(g_act)[0].astype(jnp.bfloat16)
    down_term = jnp.einsum("tf,td->fd", act_low, g_ffn, preferred_element_type=jnp.float32)
    up_term = jnp.einsum("td,tf->df", norm2_low, g_pre, preferred_element_type=jnp.float32)
    bup_term = jnp.sum(g_pre.astype(jnp.float32), axis=0)
    g_norm2 = lax.psum(
        jnp.einsum("tf,df->td", g_pre, w_up, preferred_element_type=jnp.float32).astype(
            jnp.bfloat16
        ),
        "tp",
    ).astype(jnp.float32)
    from_norm2, gain2_term, shift2_term = ln2_pull(g_norm2)
    g_hidden = grad_out + from_norm2
    g_attn = (gate * g_hidden).astype(jnp.bfloat16)
    g_attended = jnp.einsum("td,ed->te", g_attn, w_out, preferred_element_type=jnp.float32).astype(
        jnp.bfloat16
    )
    out_term = jnp.einsum("te,td->ed", attended_low, g_attn, preferred_element_type=jnp.float32)
    bouts_term = jnp.stack(
        [jnp.sum(g_attn.astype(jnp.float32), axis=0), jnp.sum(g_ffn.astype(jnp.float32), axis=0)]
    )
    g_att_h = g_attended.reshape(rows, heads, HD)
    delta = jnp.einsum("qhd,qhd->hq", g_att_h.astype(jnp.float32), combined)
    zero_kv = jnp.zeros((rows, 2 * width), jnp.float32)

    def grad_terms(index):
        key_start = first - index * rows

        def grad_work(unused_arg):
            keys3, vals3 = block_of(index)
            key_rows, key_seg, unused = row_info(seq_lengths, active_until, key_start, rows)
            masked, allowed = block_scores(q_h, keys3, my_rows, my_seg, key_rows, key_seg, scale)
            probs = jnp.where(allowed[None], jnp.exp(masked - lse[:, :, None]), 0.0)
            g_probs = jnp.einsum("qhd,khd->hqk", g_att_h, vals3, preferred_element_type=jnp.float32)
            g_scores = (probs * (g_probs - delta[:, :, None])).astype(jnp.bfloat16)
            g_q = (
                jnp.einsum("hqk,khd->qhd", g_scores, keys3, preferred_element_type=jnp.float32)
                * scale
            )
            probs_low = probs.astype(jnp.bfloat16)
            g_k = (
                jnp.einsum("hqk,qhd->khd", g_scores, q_h, preferred_element_type=jnp.float32)
                * scale
            )
            g_v = jnp.einsum("hqk,qhd->khd", probs_low, g_att_h, preferred_element_type=jnp.float32)
            return (
                g_q,
                jnp.concatenate([g_k.reshape(rows, width), g_v.reshape(rows, width)], axis=1),
            )

        def no_terms(unused_arg):
            return (zero_q, zero_kv)

        return lax.cond(key_start >= 0, grad_work, no_terms, 0)

    last_q, last_kv = grad_terms(reach)

    def return_step(step, state):
        g_q_acc, kv_acc = state
        index = reach - 1 - step
        kv_acc = passed_along(kv_acc.astype(jnp.bfloat16), "cp", -1).astype(kv_acc.dtype)
        term_q, term_kv = grad_terms(index)
        return (g_q_acc + term_q, kv_acc + term_kv)

    g_q_sum, kv_sum = lax.fori_loop(0, reach, return_step, (last_q, last_kv))
    g_q_b = g_q_sum.reshape(rows, width).astype(jnp.bfloat16)
    g_k_b = kv_sum[:, :width].astype(jnp.bfloat16)
    g_v_b = kv_sum[:, width:].astype(jnp.bfloat16)
    projection_gradient = jnp.stack([g_q_b, g_k_b, g_v_b], axis=1)
    query_key_value_term = jnp.einsum(
        "hm,hwz->mwz", first_norm_lowered, projection_gradient, preferred_element_type=jnp.float32
    )
    bqv_term = jnp.stack(
        [jnp.sum(g_q_b.astype(jnp.float32), axis=0), jnp.sum(g_v_b.astype(jnp.float32), axis=0)]
    )
    g_norm1 = lax.psum(
        jnp.einsum(
            "wzb,gzb->wg",
            projection_gradient,
            query_key_value_weight,
            preferred_element_type=jnp.float32,
        ).astype(jnp.bfloat16),
        "tp",
    ).astype(jnp.float32)
    from_norm1, gain1_term, shift1_term = ln1_pull(g_norm1)
    g_x = g_hidden + from_norm1
    g_qkv, g_out, g_up, g_down = (
        lax.psum_scatter(
            query_key_value_term.astype(jnp.bfloat16), "cp", scatter_dimension=0, tiled=True
        ).astype(jnp.float32),
        lax.psum_scatter(
            out_term.astype(jnp.bfloat16), "cp", scatter_dimension=1, tiled=True
        ).astype(jnp.float32),
        lax.psum_scatter(
            up_term.astype(jnp.bfloat16), "cp", scatter_dimension=0, tiled=True
        ).astype(jnp.float32),
        lax.psum_scatter(
            down_term.astype(jnp.bfloat16), "cp", scatter_dimension=1, tiled=True
        ).astype(jnp.float32),
    )
    g_ln_gains, g_ln_shifts, g_bqv, g_bup, g_bouts = (
        lax.psum(jnp.stack([gain1_term, gain2_term]).astype(jnp.bfloat16), "cp").astype(
            jnp.float32
        ),
        lax.psum(jnp.stack([shift1_term, shift2_term]).astype(jnp.bfloat16), "cp").astype(
            jnp.float32
        ),
        lax.psum(bqv_term.astype(jnp.bfloat16), "cp").astype(jnp.float32),
        lax.psum(bup_term.astype(jnp.bfloat16), "cp").astype(jnp.float32),
        lax.psum(bouts_term.astype(jnp.bfloat16), "cp").astype(jnp.float32),
    )
    return (out, g_x, g_ln_gains, g_ln_shifts, g_qkv, g_bqv, g_out, g_bouts, g_up, g_bup, g_down)


def solution(mesh):
    return jax.shard_map(
        shards,
        mesh=mesh,
        in_specs=(
            P("cp", None),
            P(),
            P(),
            P(),
            P(),
            P(None, None, "tp"),
            P(None, "tp"),
            P("tp", None),
            P(),
            P(None, "tp"),
            P("tp"),
            P("tp", None),
            P("cp", None),
        ),
        out_specs=(
            P("cp", None),
            P("cp", None),
            P(),
            P(),
            P("cp", None, "tp"),
            P(None, "tp"),
            P("tp", "cp"),
            P(),
            P("cp", "tp"),
            P("tp"),
            P("tp", "cp"),
        ),
        check_vma=False,
    )
```

profile of v0, /device:TPU:0, one launch (start us, length us, event | category | flops | bytes accessed | tf_op | source)
XLA Modules:
  0.0 888.3 jit_solution(2700710955240549495)
XLA Ops:
  12.9 6.0 fusion.79
  29.0 3.8 scatter.4.clone
  32.8 51.5 %while.67 = (s32[]{:T(128)}, bf16[4,512,1024]{2,1,0:T(8,128)(2,1)}, bf16[512,1024]{1,0:T(8,128)(2,1)}, s32[]{:T(128)}, s32[]{:T(128)}, /*index=5*/s32[]{:T(128)}) while((s32[]{:T(128)}, bf16[4,512,1024]{2,1,0:T(8,128)(2,1)}, bf16[512,1024]{1,0:T(8,128)(2,1)}, s32[]{:T(128)}, s32[]{:T(128)}, /*index=5*/s32[]{:T(128)}) %tuple.230), condition=%wide.region_6.7_spmd, body=%wide.region_5.6_spmd.sunk | while | flops 5 | bytes 8388763 | solution.py:104
  32.8 3.3 collective-permute-start
  42.3 14.9 %collective-permute-start = (bf16[512,1024]{1,0:T(8,128)(2,1)}, bf16[512,1024]{1,0:T(8,128)(2,1)}, u32[]{:S(2)}, u32[]{:S(2)}) collective-permute-start(bf16[512,1024]{1,0:T(8,128)(2,1)} %get-tuple-element.1387), channel_id=1, source_target_pairs={{0,4},{4,8},{8,12},{12,16},{16,20},{20,24},{24,28},{1,5},{5,9},{9,... | collective-permute-start | bytes 3145736 | tf_op jit(solution)/shard_map/while/body/eval_jaxpr/ppermute | solution.py:17
  63.4 14.8 %collective-permute-start = (bf16[512,1024]{1,0:T(8,128)(2,1)}, bf16[512,1024]{1,0:T(8,128)(2,1)}, u32[]{:S(2)}, u32[]{:S(2)}) collective-permute-start(bf16[512,1024]{1,0:T(8,128)(2,1)} %get-tuple-element.1387), channel_id=1, source_target_pairs={{0,4},{4,8},{8,12},{12,16},{16,20},{20,24},{24,28},{1,5},{5,9},{9,... | collective-permute-start | bytes 3145736 | tf_op jit(solution)/shard_map/while/body/eval_jaxpr/ppermute | solution.py:17
  84.3 6.2 copy.63
  92.6 5.8 while.68
  92.6 5.5 conditional.14
  100.5 9.7 %while.69 = (s32[]{:T(128)}, f32[512,8,64]{0,2,1:T(8,128)}, f32[512,8,64]{0,2,1:T(8,128)}, s32[]{:T(128)}, bf16[4,512,1024]{1,2,0:T(8,128)(2,1)}, /*index=5*/s32...) while((s32[]{:T(128)}, f32[512,8,64]{0,2,1:T(8,128)}, ...), condition=%wide.region_21.22_spmd.clone.clone, body=%wide.region_16.21_spmd.clone.clone.sunk | while | flops 834151936 | bytes 53276200 | solution.py:155
  100.5 9.4 %conditional.15 = ((f32[512,8,64]{0,2,1:T(8,128)}, f32[512,8,64]{0,2,1:T(8,128)})) conditional(s32[]{:T(128)} %convert_element_type.456, (f32[512,8,64]{0,2,1:T(8,128)}, f32[512,8,64]{0,2,1:T(8,128)}) %tuple.219, (s32[]{:T(128)}, bf16[4,512,1024]{1,2,0:T(8,128)(2,1)}, s32[]{:T(128)}, s32[]{:T(128)}, s32[3]{0:T(128)S(1)}, ...), branch_computations={%region_17.17_spmd, %region_18.20_spmd} | conditional | flops 834151936 | bytes 53273896 | solution.py:152
  103.9 2.7 fusion.23
  111.6 2.6 convolution_convert_fusion.6
  114.9 146.6 %all-reduce.7.cloned.1.call-done = bf16[512,2048]{1,0:T(8,128)(2,1)} async-done(((bf16[512,2048]{1,0:T(8,128)(2,1)}), bf16[512,2048]{1,0:T(8,128)(2,1)}) %all-reduce.7.cloned.1.call-update) | async-done | bytes 2097168 | tf_op jit(solution)/shard_map/psum | solution.py:159
  261.6 3.3 fusion.95
  266.4 10.3 %fusion.94 = f32[512,2048]{1,0:T(8,128)} fusion(bf16[2048,2048]{1,0:T(8,128)(2,1)} %param.40, f32[2048]{0:T(1024)S(1)} %bitcast.229, f32[2048]{0:T(1024)S(1)} %bitcast.220, f32[512]{0:T(512)S(1)} %fusion.84, f32[512]{0:T(512)S(1)} %broadcast_multiply_fusion, bf16[512,2048]{1,0:T(8,128)(2,1)S(1)} %copy-done.3, bf16[512,2048]{1,0:T(8,128)(2,1)S(1)} %copy-done.6, ...), kind=kOutput, calls=%fused_computation.189 | convolution fusion | flops 4305453056 | bytes 16807936 | tf_op jit(solution)/shard_map/dot_general | solution.py:168
  276.7 9.9 %fusion.105 = (bf16[2048]{0:T(1024)(128)(2,1)}, bf16[512,2048]{1,0:T(8,128)(2,1)S(1)}) fusion(f32[512,2048]{1,0:T(8,128)} %fusion.94, f32[2048]{0:T(1024)S(1)} %copy-done.60, bf16[2048,2048]{1,0:T(8,128)(2,1)S(1)} %bitcast.238, bf16[512,2048]{1,0:T(8,128)(2,1)S(1)} %copy-done.11, f32[512]{0:T(512)S(1)} %fusion.82), kind=kOutput, calls=%fused_computation.200 | convolution fusion | flops 4321179648 | bytes 16791552 | tf_op jit(solution)/shard_map/td,fd->tf/dot_general | solution.py:180
  288.0 5.8 convolution_convert_fusion.4
  293.8 85.6 %all-reduce.9.cloned.1.call-done = bf16[512,2048]{1,0:T(8,128)(2,1)} async-done(((bf16[512,2048]{1,0:T(8,128)(2,1)}), bf16[512,2048]{1,0:T(8,128)(2,1)}) %all-reduce.9.cloned.1.call-update) | async-done | bytes 2097168 | tf_op jit(solution)/shard_map/psum | solution.py:185
  379.4 15.5 %fusion.62 = (bf16[2048]{0:T(1024)(128)(2,1)}, f32[512]{0:T(512)S(1)}) fusion(bf16[512,2048]{1,0:T(8,128)(2,1)} %all-reduce.9.cloned.1.call-done, f32[512]{0:T(512)S(1)} %fusion.84, f32[512]{0:T(512)S(1)} %broadcast_multiply_fusion, f32[2048]{0:T(1024)S(1)} %bitcast.206, bf16[512,2048]{1,0:T(8,128)(2,1)} %all-reduce.7.cloned.1.call-done, ...), kind=kLoop, calls=%fused_computation.119 | loop fusion | flops 13628928 | bytes 6320128 | tf_op jit(solution)/shard_map/transpose(jvp())/reduce_sum | solution.py:24
  400.7 2.6 convolution_convert_fusion.3
  403.4 11.3 %convolution_convert_fusion.5 = bf16[512,2048]{1,0:T(8,128)(2,1)} fusion(bf16[2048,2048]{1,0:T(8,128)(2,1)} %param.42, f32[512,2048]{1,0:T(8,128)} %fusion.94, f32[2048]{0:T(1024)S(1)} %copy-done.60), kind=kOutput, calls=%fused_computation.139 | convolution fusion | flops 4306501632 | bytes 14688256 | tf_op jit(solution)/shard_map/dot_general | solution.py:173
  416.0 2.5 conditional.4
  418.6 50.7 %while.70 = (s32[]{:T(128)}, f32[512,8,64]{0,2,1:T(8,128)}, bf16[512,1024]{0,1:T(8,128)(2,1)}, s32[]{:T(128)}, bf16[4,512,1024]{1,2,0:T(8,128)(2,1)}, /*index=5*...) while((s32[]{:T(128)}, f32[512,8,64]{0,2,1:T(8,128)}, ...), condition=%wide.region_38.39_spmd.clone.clone, body=%wide.region_33.38_spmd.clone.clone.sunk | while | flops 1371284992 | bytes 65351152 | solution.py:244
  421.3 2.7 add.657
  424.0 2.5 convert_add_fusion.6
  429.2 2.7 add.657
  431.9 15.3 %collective-permute-done.1 = bf16[512,1024]{0,1:T(8,128)(2,1)} collective-permute-done((bf16[512,1024]{0,1:T(8,128)(2,1)}, bf16[512,1024]{0,1:T(8,128)(2,1)}, u32[]{:S(2)}, u32[]{:S(2)}) %collective-permute-start.1) | collective-permute-done | bytes 1048608 | tf_op jit(solution)/shard_map/while/body/eval_jaxpr/ppermute | solution.py:17
  447.3 2.5 convert_add_fusion.6
  451.1 12.3 %conditional.16 = (f32[512,8,64]{0,2,1:T(8,128)}, f32[512,1024]{0,1:T(8,128)S(1)}) conditional(s32[]{:T(128)} %convert_element_type.458, () %tuple.222, (s32[]{:T(128)}, bf16[4,512,1024]{1,2,0:T(8,128)(2,1)}, s32[]{:T(128)}, s32[]{:T(128)}, s32[3]{0:T(128)S(1)}, /*index=5*/s32[512]{0:T(512)S(1)}, bf16[512,8,64]{0,2,1:T(8,128)(2,1)S(1)}, ...), branch_computations={%region_34.34_spmd, %region_35.37_spmd} | conditional | flops 1369449984 | bytes 53814448 | solution.py:233
  454.5 3.3 fusion.38
  463.4 2.7 add.657
  466.7 2.5 convert_add_fusion.6
  473.3 7.4 bitcast_convert_fusion
  482.4 6.7 convolution_convert_fusion.2
  489.8 10.7 %convolution_convert_fusion.1 = bf16[2048,2048]{1,0:T(8,128)(2,1)} fusion(bf16[512,2048]{1,0:T(8,128)(2,1)} %copy-done.62, f32[2048]{0:T(1024)S(1)} %bitcast.230, f32[2048]{0:T(1024)S(1)} %bitcast.223, f32[512]{0:T(512)S(1)} %copy-done.42, f32[512]{0:T(512)S(1)} %copy-done.35, bf16[512,2048]{1,0:T(8,128)(2,1)S(1)} %copy-done.5, ...), kind=kOutput, calls=%fused_computation.92 | convolution fusion | flops 4309647360 | bytes 14710784 | tf_op jit(solution)/shard_map/td,tf->df/dot_general | solution.py:183
  501.2 11.8 %convolution_convert_fusion = bf16[2048,2048]{1,0:T(8,128)(2,1)} fusion(bf16[512,2048]{1,0:T(8,128)(2,1)} %param.43, f32[512]{0:T(512)S(1)} %copy-done.29, f32[512,2048]{1,0:T(8,128)} %fusion.94, f32[2048]{0:T(1024)S(1)} %copy-done.61), kind=kOutput, calls=%fused_computation.91 | convolution fusion | flops 4312793088 | bytes 14690304 | tf_op jit(solution)/shard_map/tf,td->fd/dot_general | solution.py:182
  513.8 2.5 reduce.5
  518.2 146.5 %all-reduce.11.cloned.1.call-done = (bf16[512,2048]{1,0:T(8,128)(2,1)}, bf16[512,2048]{1,0:T(8,128)(2,1)}) async-done(((bf16[512,2048]{1,0:T(8,128)(2,1)}, bf16[512,2048]{1,0:T(8,128)(2,1)}), (bf16[512,2048]{1,0:T(8,128)(2,1)}, bf16[512,2048]{1,0:T(8,128)(2,1)})) %all-reduce.11.cloned.1.call-update) | async-done | bytes 4194320 | tf_op jit(solution)/shard_map/psum | solution.py:172
  666.7 2.7 fusion.72
  671.7 24.3 %all-reduce.1 = (bf16[2,2048]{1,0:T(2,128)(2,1)S(1)}, bf16[2,2048]{1,0:T(2,128)(2,1)S(1)}, bf16[2,512]{1,0:T(2,128)(2,1)S(1)}, bf16[2,2048]{1,0:T(2,128)(2,1)S(1)}, bf16[2048]{0:T(1024)(128)(2,1)S(1)}) all-reduce(bf16[2,2048]{1,0:T(2,128)(2,1)S(1)} %pad_maximum_fusion.6, ...), channel_id=1, replica_groups=mesh['cp'=8,'tp'=4] {'cp'}, use_global_device_ids=true, to_apply=%region_44.45 | all-reduce | flops 15360 | bytes 61440 | tf_op jit(solution)/shard_map/psum | solution.py:281
  699.0 9.3 %add_add_fusion.2 = (f32[512,2048]{1,0:T(8,128)}, f32[512,2048]{1,0:T(8,128)}) fusion(bf16[512,2048]{1,0:T(8,128)(2,1)} %param.31, bf16[512,2048]{1,0:T(8,128)(2,1)} %get-tuple-element.1114, f32[512,2048]{1,0:T(8,128)} %copy-done.8, bf16[512,2048]{1,0:T(8,128)(2,1)} %param.43, f32[512]{0:T(512)S(1)} %negate_multiply_fusion, ...), kind=kLoop, calls=%fused_computation.131 | loop fusion | flops 22020096 | bytes 23105536 | tf_op jit(solution)/shard_map/add | solution.py:265
  708.3 20.5 %reduce-scatter.5.cloned.1.call-done = bf16[256,3,512]{2,0,1:T(8,128)(2,1)} async-done(((bf16[2048,3,512]{2,0,1:T(8,128)(2,1)}), bf16[256,3,512]{2,0,1:T(8,128)(2,1)}) %reduce-scatter.5.cloned.1.call-update) | async-done | bytes 786448 | tf_op jit(solution)/shard_map/reduce_scatter | solution.py:267
  728.7 2.5 convert_element_type.238
  731.2 72.5 %reduce-scatter.9.cloned.1.call-done = bf16[256,2048]{1,0:T(8,128)(2,1)} async-done(((bf16[2048,2048]{1,0:T(8,128)(2,1)}), bf16[256,2048]{1,0:T(8,128)(2,1)}) %reduce-scatter.9.cloned.1.call-update) | async-done | bytes 1048592 | tf_op jit(solution)/shard_map/reduce_scatter | solution.py:273
  803.8 2.8 convert_element_type.248
  806.6 72.0 %reduce-scatter.11.cloned.1.call-done = bf16[2048,256]{1,0:T(8,128)(2,1)} async-done(((bf16[2048,2048]{1,0:T(8,128)(2,1)}), bf16[2048,256]{1,0:T(8,128)(2,1)}) %reduce-scatter.11.cloned.1.call-update) | async-done | bytes 1048592 | tf_op jit(solution)/shard_map/reduce_scatter | solution.py:276
  878.5 2.7 convert_element_type.251
  (291 shorter events, 100.3 us)
Async XLA Ops:
  7.2 104.4 %copy-start = (bf16[512,2048]{1,0:T(8,128)(2,1)S(1)}, bf16[512,2048]{1,0:T(8,128)(2,1)}, u32[]{:S(2)}) copy-start(bf16[512,2048]{1,0:T(8,128)(2,1)} %param.38) | copy-start | bytes 6291460
  7.2 5.1 copy-start.49
  7.2 5.1 copy-start.50
  7.2 254.4 %all-reduce.7.cloned.1.call-start = ((), (), s32[]{:S(2)}) async-start(), calls=%async_computation.4 | async-start | bytes 4194304 | tf_op jit(solution)/shard_map/psum | solution.py:159
  7.3 5.7 copy-start.2
  9.4 3.0 copy-start.32
  12.3 382.6 %copy-start.30 = (f32[1,2048]{1,0:T(1,128)}, f32[1,2048]{1,0:T(1,128)S(1)}, u32[]{:S(2)}) copy-start(f32[1,2048]{1,0:T(1,128)S(1)} %get-tuple-element.1154) | copy-start | bytes 24580
  12.3 254.0 %copy-start.53 = (f32[1,2048]{1,0:T(1,128)}, f32[1,2048]{1,0:T(1,128)S(1)}, u32[]{:S(2)}) copy-start(f32[1,2048]{1,0:T(1,128)S(1)} %get-tuple-element.1156) | copy-start | bytes 24580
  12.9 8.7 copy-start.58
  32.8 5.0 collective-permute-start
  42.3 16.5 %collective-permute-start = (bf16[512,1024]{1,0:T(8,128)(2,1)}, bf16[512,1024]{1,0:T(8,128)(2,1)}, u32[]{:S(2)}, u32[]{:S(2)}) collective-permute-start(bf16[512,1024]{1,0:T(8,128)(2,1)} %get-tuple-element.1387), channel_id=1, source_target_pairs={{0,4},{4,8},{8,12},{12,16},{16,20},{20,24},{24,28},{1,5},{5,9},{9,... | collective-permute-start | bytes 3145736 | tf_op jit(solution)/shard_map/while/body/eval_jaxpr/ppermute | solution.py:17
  63.4 16.4 %collective-permute-start = (bf16[512,1024]{1,0:T(8,128)(2,1)}, bf16[512,1024]{1,0:T(8,128)(2,1)}, u32[]{:S(2)}, u32[]{:S(2)}) collective-permute-start(bf16[512,1024]{1,0:T(8,128)(2,1)} %get-tuple-element.1387), channel_id=1, source_target_pairs={{0,4},{4,8},{8,12},{12,16},{16,20},{20,24},{24,28},{1,5},{5,9},{9,... | collective-permute-start | bytes 3145736 | tf_op jit(solution)/shard_map/while/body/eval_jaxpr/ppermute | solution.py:17
  84.3 6.3 copy-start.25
  84.3 6.5 copy-start.59
  103.9 2.8 copy-start.13
  114.2 265.2 %all-reduce.9.cloned.1.call-start = ((), (), s32[]{:S(2)}) async-start(), calls=%async_computation.5 | async-start | bytes 4194304 | tf_op jit(solution)/shard_map/psum | solution.py:185
  114.3 283.0 %copy-start.28 = (f32[512]{0:T(512)}, f32[512]{0:T(512)S(1)}, u32[]{:S(2)}) copy-start(f32[512]{0:T(512)S(1)} %fusion.82) | copy-start | bytes 6148
  114.9 280.0 %copy-start.23 = (f32[1,2048]{1,0:T(1,128)}, f32[1,2048]{1,0:T(1,128)S(1)}, u32[]{:S(2)}) copy-start(f32[1,2048]{1,0:T(1,128)S(1)} %get-tuple-element.1152) | copy-start | bytes 24580
  261.6 3.3 copy-start.3
  261.6 3.5 copy-start.6
  261.6 15.1 %slice-start.2 = ((s8[8388608]{0:T(1024)(128)(4,1)}), s8[4194304]{0:T(1024)(128)(4,1)S(1)}, s32[]{:S(2)}) async-start(s8[8388608]{0:T(1024)(128)(4,1)} %bitcast.237), calls=%async_computation.13 | async-start | bytes 8388608
  265.1 129.9 %copy-start.34 = (f32[512]{0:T(512)}, f32[512]{0:T(512)S(1)}, u32[]{:S(2)}) copy-start(f32[512]{0:T(512)S(1)} %broadcast_multiply_fusion) | copy-start | bytes 6148
  266.3 128.6 %copy-start.41 = (f32[512]{0:T(512)}, f32[512]{0:T(512)S(1)}, u32[]{:S(2)}) copy-start(f32[512]{0:T(512)S(1)} %fusion.84) | copy-start | bytes 6148
  266.3 10.4 %copy-start.11 = (bf16[512,2048]{1,0:T(8,128)(2,1)S(1)}, bf16[512,2048]{1,0:T(8,128)(2,1)}, u32[]{:S(2)}) copy-start(bf16[512,2048]{1,0:T(8,128)(2,1)} %param.43) | copy-start | bytes 6291460
  266.3 10.4 %slice-start.3 = ((s8[8388608]{0:T(1024)(128)(4,1)}), s8[4194304]{0:T(1024)(128)(4,1)S(1)}, s32[]{:S(2)}) async-start(s8[8388608]{0:T(1024)(128)(4,1)} %bitcast.237), calls=%async_computation.14 | async-start | bytes 8388608
  266.4 10.3 %copy-start.60 = (f32[2048]{0:T(1024)S(1)}, f32[2048]{0:T(1024)}, u32[]{:S(2)}) copy-start(f32[2048]{0:T(1024)} %param.41) | copy-start | bytes 24580
  266.4 21.6 %slice-start = ((s8[8388608]{0:T(1024)(128)(4,1)}), s8[4194304]{0:T(1024)(128)(4,1)S(1)}, s32[]{:S(2)}) async-start(s8[8388608]{0:T(1024)(128)(4,1)} %bitcast.235), calls=%async_computation.11 | async-start | bytes 8388608
  276.7 11.3 %slice-start.1 = ((s8[8388608]{0:T(1024)(128)(4,1)}), s8[4194304]{0:T(1024)(128)(4,1)S(1)}, s32[]{:S(2)}) async-start(s8[8388608]{0:T(1024)(128)(4,1)} %bitcast.235), calls=%async_computation.12 | async-start | bytes 8388608
  293.8 222.7 %reduce-scatter.7.cloned.1.call-start = ((), (), s32[]{:S(2)}) async-start(), calls=%async_computation.7 | async-start | bytes 2359296 | tf_op jit(solution)/shard_map/reduce_scatter | solution.py:270
  379.4 15.5 %copy-start.4 = (bf16[512,2048]{1,0:T(8,128)(2,1)S(1)}, bf16[512,2048]{1,0:T(8,128)(2,1)}, u32[]{:S(2)}) copy-start(bf16[512,2048]{1,0:T(8,128)(2,1)} %param.31) | copy-start | bytes 6291460
  379.4 15.6 %copy-start.7 = (bf16[512,2048]{1,0:T(8,128)(2,1)S(1)}, bf16[512,2048]{1,0:T(8,128)(2,1)}, u32[]{:S(2)}) copy-start(bf16[512,2048]{1,0:T(8,128)(2,1)} %all-reduce.7.cloned.1.call-done) | copy-start | bytes 6291460
  379.4 15.6 %copy-start.10 = (bf16[512,2048]{1,0:T(8,128)(2,1)S(1)}, bf16[512,2048]{1,0:T(8,128)(2,1)}, u32[]{:S(2)}) copy-start(bf16[512,2048]{1,0:T(8,128)(2,1)} %all-reduce.9.cloned.1.call-done) | copy-start | bytes 6291460
  403.3 261.4 %all-reduce.11.cloned.1.call-start = ((), (), s32[]{:S(2)}) async-start(), calls=%async_computation.10 | async-start | bytes 8388608 | tf_op jit(solution)/shard_map/psum | solution.py:172
  403.4 11.3 %copy-start.15 = (f32[512,8,64]{0,2,1:T(8,128)S(1)}, f32[512,8,64]{0,2,1:T(8,128)}, u32[]{:S(2)}) copy-start(f32[512,8,64]{0,2,1:T(8,128)} %get-tuple-element.753) | copy-start | bytes 3145732
  403.4 11.3 %copy-start.18 = (bf16[512,2048]{1,0:T(8,128)(2,1)S(1)}, bf16[512,2048]{1,0:T(8,128)(2,1)}, u32[]{:S(2)}) copy-start(bf16[512,2048]{1,0:T(8,128)(2,1)} %copy-done.17) | copy-start | bytes 6291460
  403.4 11.3 %copy-start.21 = (f32[512,8,64]{0,2,1:T(8,128)S(1)}, f32[512,8,64]{0,2,1:T(8,128)}, u32[]{:S(2)}) copy-start(f32[512,8,64]{0,2,1:T(8,128)} %get-tuple-element.754) | copy-start | bytes 3145732
  418.6 5.4 collective-permute-start.1
  426.5 20.7 %collective-permute-start.1 = (bf16[512,1024]{0,1:T(8,128)(2,1)}, bf16[512,1024]{0,1:T(8,128)(2,1)}, u32[]{:S(2)}, u32[]{:S(2)}) collective-permute-start(bf16[512,1024]{0,1:T(8,128)(2,1)} %get-tuple-element.1487), channel_id=1, source_target_pairs={{4,0},{8,4},{12,8},{16,12},{20,16},{24,20},{28,24},{5,1},{9,5},{13... | collective-permute-start | bytes 3145736 | tf_op jit(solution)/shard_map/while/body/eval_jaxpr/ppermute | solution.py:17
  449.8 16.9 %collective-permute-start.1 = (bf16[512,1024]{0,1:T(8,128)(2,1)}, bf16[512,1024]{0,1:T(8,128)(2,1)}, u32[]{:S(2)}, u32[]{:S(2)}) collective-permute-start(bf16[512,1024]{0,1:T(8,128)(2,1)} %get-tuple-element.1487), channel_id=1, source_target_pairs={{4,0},{8,4},{12,8},{16,12},{20,16},{24,20},{28,24},{5,1},{9,5},{13... | collective-permute-start | bytes 3145736 | tf_op jit(solution)/shard_map/while/body/eval_jaxpr/ppermute | solution.py:17
  480.8 247.9 %reduce-scatter.5.cloned.1.call-start = ((), (), s32[]{:S(2)}) async-start(), calls=%async_computation.6 | async-start | bytes 7077888 | tf_op jit(solution)/shard_map/reduce_scatter | solution.py:267
  489.2 314.6 %reduce-scatter.9.cloned.1.call-start = ((), (), s32[]{:S(2)}) async-start(), calls=%async_computation.8 | async-start | bytes 9437184 | tf_op jit(solution)/shard_map/reduce_scatter | solution.py:273
  500.6 378.0 %reduce-scatter.11.cloned.1.call-start = ((), (), s32[]{:S(2)}) async-start(), calls=%async_computation.9 | async-start | bytes 9437184 | tf_op jit(solution)/shard_map/reduce_scatter | solution.py:276
  513.0 3.4 copy-start.52
  513.8 155.6 %copy-start.46 = (f32[512]{0:T(512)S(1)}, f32[512]{0:T(512)}, u32[]{:S(2)}) copy-start(f32[512]{0:T(512)} %copy-done.45) | copy-start | bytes 6148
  666.7 5.0 copy-start.57
  666.7 32.3 %copy-start.36 = (f32[1,2048]{1,0:T(1,128)S(1)}, f32[1,2048]{1,0:T(1,128)}, u32[]{:S(2)}) copy-start(f32[1,2048]{1,0:T(1,128)} %get-tuple-element.1151) | copy-start | bytes 24580
  666.7 32.3 %copy-start.40 = (f32[512]{0:T(512)S(1)}, f32[512]{0:T(512)}, u32[]{:S(2)}) copy-start(f32[512]{0:T(512)} %copy-done.39) | copy-start | bytes 6148
  699.0 182.2 %copy-start.1 = (bf16[512,2048]{1,0:T(8,128)(2,1)S(1)}, bf16[512,2048]{1,0:T(8,128)(2,1)}, u32[]{:S(2)}) copy-start(bf16[512,2048]{1,0:T(8,128)(2,1)} %param.38) | copy-start | bytes 6291460
  (32 other events, 40.3 us)
Sparse Core Ops, SparseCore 0:
  114.4 147.1 all-reduce.6
  293.9 85.4 all-reduce.8
  403.5 42.1 reduce-scatter.6
  480.9 183.7 all-reduce.10
  667.9 60.7 reduce-scatter.4
  732.5 71.2 reduce-scatter.8
  807.2 71.2 reduce-scatter.10
where the time goes:
time: 894 us; the launch traced here: 888 us
  waiting for transfers between devices  565 us (63%)
  matrix products  104 us (12%)
  other arithmetic  87.4 us (10%)
  local copies, waits for them, and re-layouts  54 us (6%)
  starting transfers between devices  37.4 us (4%)
  blocking collectives  24.3 us (3%)
  between operations  15.1 us (2%)
    psum x1, waiting for transfers between devices, shards(): lax.psum(jnp.dot(attended_low, w_out, preferred_element_type=jnp.float32)...  147 us
    psum x1, waiting for transfers between devices, shards(): lax.psum(jnp.dot(act_low, w_down, preferred_element_type=jnp.float32).ast...  146 us
    psum x1, waiting for transfers between devices, shards(): lax.psum(jnp.einsum('tf,df->td', g_pre, w_up, preferred_element_type=jnp....  85.6 us
    reduce_scatter x1, waiting for transfers between devices, shards(): lax.psum_scatter(up_term.astype(jnp.bfloat16), 'cp', scatter_dimension=0,...  72.5 us
    reduce_scatter x1, waiting for transfers between devices, shards(): lax.psum_scatter(down_term.astype(jnp.bfloat16), 'cp', scatter_dimension=...  72 us
    ppermute x6, starting transfers between devices, passed_along(): lax.ppermute(value, axis, [(source, source + steps) for source in range(f...  36.9 us
    reduce_sum x5, other arithmetic, layer_norm(): return centred * lax.rsqrt(var + EPS) * gain + shift  24.9 us
    psum x1, blocking collectives, shards(): lax.psum(jnp.stack([gain1_term, gain2_term]).astype(jnp.bfloat16), 'cp')  24.3 us
  transfers between devices with their start and end apart: 13, of which 11 were waited for; matrix products, arithmetic and copies ran while one was open for 13% of the time, Pallas kernels for 0%

commit v1 on v0

--- a/solution.py
+++ b/solution.py
@@ -1,14 +1,391 @@
+import functools
+
 import jax
 import jax.numpy as jnp
 from jax import lax
+from jax.experimental import pallas as pl
+from jax.experimental.pallas import tpu as pltpu
 from jax.sharding import PartitionSpec as P
 
 HD = 64
 LONG = 2048
-
-
 EPS = 1e-05
 NEG = -1e30
+MESH = pl.DeviceIdType.MESH
+F32 = jnp.float32
+BF16 = jnp.bfloat16
+ANY = pl.BlockSpec(memory_space=pl.ANY)
+IN_VMEM = pl.BlockSpec(memory_space=pltpu.VMEM)
+IN_SMEM = pl.BlockSpec(memory_space=pltpu.SMEM)
+SUB = 32
+CHUNK = 256
+
+
+def dot(a, b):
+    return jnp.dot(a, b, preferred_element_type=F32)
+
+
+def dot_nt(a, b):
+    return lax.dot_general(a, b, (((1,), (1,)), ((), ())), preferred_element_type=F32)
+
+
+def dot_tn(a, b):
+    return lax.dot_general(a, b, (((0,), (0,)), ((), ())), preferred_element_type=F32)
+
+
+def rows_of(index, size):
+    return pl.ds(pl.multiple_of(index * size, size), size)
+
+
+def place():
+    cp = lax.axis_index("cp")
+    tp = lax.axis_index("tp")
+    return cp, tp, lax.rem(cp, 2), lax.div(cp, 2)
+
+
+def greet(cp, tp, others):
+    barrier = pltpu.get_barrier_semaphore()
+    edge = (tp == 0) | (tp == 3)
+    for other in [*others, (cp, line_near(tp))]:
+        pl.semaphore_signal(barrier, inc=1, device_id=other, device_id_type=MESH)
+
+    @pl.when(jnp.logical_not(edge))
+    def _():
+        pl.semaphore_signal(barrier, inc=1, device_id=(cp, 3 - tp), device_id_type=MESH)
+
+    pl.semaphore_wait(barrier, len(others) + jnp.where(edge, 1, 2))
+
+
+def line_near(tp):
+    return jnp.where(tp == 0, 1, jnp.where(tp == 1, 0, jnp.where(tp == 2, 3, 2)))
+
+
+class LineSum:
+    def __init__(self, part, slot_a, slot_b, total, send, recv):
+        self.cp, self.tp, _, _ = place()
+        self.edge = (self.tp == 0) | (self.tp == 3)
+        self.refs = (part, slot_a, slot_b, total)
+        self.send, self.recv = send, recv
+
+    def copy(self, kind, s):
+        part, slot_a, slot_b, total = self.refs
+        src, dst = ((part, slot_a), (part, slot_b), (total, total))[kind]
+        other = (self.cp, 3 - self.tp if kind == 1 else line_near(self.tp))
+        rows = rows_of(s, SUB)
+        return pltpu.make_async_remote_copy(
+            src_ref=src.at[rows],
+            dst_ref=dst.at[rows],
+            send_sem=self.send.at[kind, s],
+            recv_sem=self.recv.at[kind, s],
+            device_id=other,
+            device_id_type=MESH,
+        )
+
+    def push(self, s):
+        @pl.when(self.edge)
+        def _():
+            self.copy(0, s).start()
+
+    def relay_in(self, s):
+        part, slot_a, _, _ = self.refs
+
+        @pl.when(jnp.logical_not(self.edge))
+        def _():
+            rows = rows_of(s, SUB)
+            self.copy(0, s).wait_recv()
+            part[rows] = (part[rows].astype(F32) + slot_a[rows].astype(F32)).astype(BF16)
+            self.copy(1, s).start()
+
+    def relay_out(self, s):
+        part, _, slot_b, total = self.refs
+
+        @pl.when(jnp.logical_not(self.edge))
+        def _():
+            rows = rows_of(s, SUB)
+            self.copy(1, s).wait_recv()
+            total[rows] = (part[rows].astype(F32) + slot_b[rows].astype(F32)).astype(BF16)
+            self.copy(2, s).start()
+
+    def get(self, s):
+        @pl.when(self.edge)
+        def _():
+            self.copy(2, s).wait_recv()
+
+    def drain(self, s):
+        @pl.when(self.edge)
+        def _():
+            self.copy(0, s).wait_send()
+
+        @pl.when(jnp.logical_not(self.edge))
+        def _():
+            self.copy(1, s).wait_send()
+            self.copy(2, s).wait_send()
+
+    def run(self, first, last):
+        def step(s, carry):
+            @pl.when(s < last)
+            def _():
+                self.relay_in(s)
+
+            @pl.when(s > first)
+            def _():
+                self.relay_out(s - 1)
+                self.get(s - 1)
+
+            return carry
+
+        lax.fori_loop(first, last + 1, step, 0)
+
+    def drain_all(self, count):
+        def step(s, carry):
+            self.drain(s)
+            return carry
+
+        lax.fori_loop(0, count, step, 0)
+
+
+def line_scratch(rows, width, with_part=True):
+    count = rows // SUB
+    return [pltpu.VMEM((rows, width), BF16)] * 4 + [
+        pltpu.SemaphoreType.DMA((3, count)),
+        pltpu.SemaphoreType.DMA((3, count)),
+    ]
+
+
+def band_info(lengths_ref, until_ref, first):
+    start = jnp.int32(0)
+    begin = jnp.int32(0)
+    until = jnp.int32(0)
+    for i in range(lengths_ref.shape[0]):
+        length = lengths_ref[i]
+        inside = (first >= start) & (first < start + length)
+        begin = jnp.where(inside, start, begin)
+        until = jnp.where(inside, until_ref[i], until)
+        start = start + length
+    return begin, until + begin - first
+
+
+def loop(count, body):
+    def step(i, carry):
+        body(i)
+        return carry
+
+    lax.fori_loop(0, count, step, 0)
+
+
+def attend_kernel(
+    x_hbm, lengths_ref, until_ref, gains, shifts, wqkv_hbm, bqv, wout_hbm,
+    sum_hbm, norm_hbm, q_hbm, kv_hbm, att_hbm, att_t_hbm, lse_out,
+    x_v, norm_v, w_v, wout_v, q_v, kv, q_t, v_t, s_v, p_v, att_t, att_v,
+    part, slot_a, slot_b, total, ar_send, ar_recv, kv_send, kv_recv, load_sem, store_sem,
+):
+    cp, tp, core, chip = place()
+    bands = lax.axis_size("cp")
+    chips = bands // 2
+    rows, depth = x_v.shape
+    width = q_v.shape[1]
+    heads = width // HD
+    near = (cp + 1 - 2 * core, tp)
+    after = (lax.rem(cp + 2, bands), tp)
+    before = (lax.rem(cp + bands - 2, bands), tp)
+    loads = [
+        pltpu.make_async_copy(x_hbm, x_v, load_sem.at[0]),
+        pltpu.make_async_copy(wqkv_hbm.at[1], w_v.at[1], load_sem.at[1]),
+        pltpu.make_async_copy(wqkv_hbm.at[2], w_v.at[2], load_sem.at[2]),
+        pltpu.make_async_copy(wqkv_hbm.at[0], w_v.at[0], load_sem.at[3]),
+        pltpu.make_async_copy(wout_hbm, wout_v, load_sem.at[4]),
+    ]
+    for item in loads:
+        item.start()
+    greet(cp, tp, [near, after, before])
+    begin, _ = band_info(lengths_ref, until_ref, cp * rows)
+    has_before = begin < chip * 2 * rows
+    loads[0].wait()
+
+    @functools.partial(loop, rows // 64)
+    def _(i):
+        part_rows = rows_of(i, 64)
+        v = x_v[part_rows].astype(F32)
+        mean = jnp.mean(v, axis=-1, keepdims=True)
+        centred = v - mean
+        var = jnp.mean(centred * centred, axis=-1, keepdims=True)
+        norm_v[part_rows] = (centred * lax.rsqrt(var + EPS) * gains[0:1] + shifts[0:1]).astype(BF16)
+
+    stores = [pltpu.make_async_copy(norm_v, norm_hbm, store_sem.at[0])]
+    stores[0].start()
+    own = 2 + core
+
+    for load, column in ((1, 0), (2, 1)):
+        loads[load].wait()
+
+        @functools.partial(loop, rows // CHUNK)
+        def _(i):
+            value = dot(norm_v[rows_of(i, CHUNK)], w_v[load])
+            if column:
+                value = value + bqv[1:2]
+            target = pl.ds(pl.multiple_of(own * rows + i * CHUNK, CHUNK), CHUNK)
+            kv[target, column * width : (column + 1) * width] = value.astype(BF16)
+
+    def kv_copy(kind, slot, device):
+        block = kv.at[rows_of(slot, rows)]
+        to = kv.at[rows_of(core, rows)] if kind == 0 else block
+        return pltpu.make_async_remote_copy(
+            src_ref=block, dst_ref=to, send_sem=kv_send.at[kind], recv_sem=kv_recv.at[kind],
+            device_id=device, device_id_type=MESH,
+        )
+
+    to_next = kv_copy(0, own, after)
+    to_near = kv_copy(1, own, near)
+    forward = kv_copy(2, core, near)
+
+    @pl.when(chip < chips - 1)
+    def _():
+        to_next.start()
+
+    to_near.start()
+
+    @pl.when(chip == 0)
+    def _():
+        @functools.partial(loop, 2 * rows // 64)
+        def _(i):
+            kv[rows_of(i, 64)] = jnp.zeros((64, 2 * width), BF16)
+
+    loads[3].wait()
+
+    @functools.partial(loop, rows // CHUNK)
+    def _(i):
+        part_rows = rows_of(i, CHUNK)
+        value = (dot(norm_v[part_rows], w_v[0]) + bqv[0:1]).astype(BF16)
+        q_v[part_rows] = value
+        turned = (value.astype(F32) * (HD ** -0.5)).T
+        upper = lax.broadcasted_iota(jnp.int32, (2 * HD, CHUNK), 0) < HD
+        for h in range(heads):
+            both = turned[(h // 2) * 2 * HD : (h // 2 + 1) * 2 * HD]
+            q_t[h, :, part_rows] = jnp.where(upper == (h % 2 == 0), both, 0.0).astype(BF16)
+
+    stores.append(pltpu.make_async_copy(q_v, q_hbm, store_sem.at[1]))
+    stores[1].start()
+    to_near.wait_recv()
+
+    def turn_values(slot):
+        v_t[:, rows_of(slot, rows)] = kv[rows_of(slot, rows), width:].astype(F32).T.astype(BF16)
+
+    turn_values(2)
+    turn_values(3)
+
+    @pl.when(chip > 0)
+    def _():
+        to_next.wait_recv()
+        forward.start()
+        forward.wait_recv()
+
+    stores.append(pltpu.make_async_copy(kv, kv_hbm, store_sem.at[2]))
+    stores[2].start()
+    turn_values(0)
+    turn_values(1)
+    loads[4].wait()
+    line = LineSum(part, slot_a, slot_b, total, ar_send, ar_recv)
+    bias = jnp.where(has_before, 0.0, NEG)
+    keys = 4 * rows
+
+    for c in range(rows // CHUNK):
+        columns = slice(c * CHUNK, (c + 1) * CHUNK)
+
+        def head(h, parity, c=c, columns=columns):
+            lanes = pl.ds(pl.multiple_of(lax.div(h, 2) * 2 * HD, 2 * HD), 2 * HD)
+            query = q_t[h, :, columns]
+            top = jnp.full((1, CHUNK), NEG, F32)
+            for b in range(4):
+                s = dot(kv[b * rows : (b + 1) * rows, lanes], query)
+                if b < 2:
+                    s = s + bias
+                else:
+                    key = lax.broadcasted_iota(jnp.int32, (rows, CHUNK), 0) + (b - 2) * rows
+                    row = lax.broadcasted_iota(jnp.int32, (rows, CHUNK), 1) + c * CHUNK
+                    s = jnp.where(key <= row + core * rows, s, NEG)
+                s_v[b * rows : (b + 1) * rows] = s
+                top = jnp.maximum(top, jnp.max(s, axis=0, keepdims=True))
+            mass = jnp.zeros((1, CHUNK), F32)
+            for b in range(4):
+                p = jnp.exp(s_v[b * rows : (b + 1) * rows] - top)
+                mass = mass + jnp.sum(p, axis=0, keepdims=True)
+                p_v[b * rows : (b + 1) * rows] = p.astype(BF16)
+            feature = pl.ds(pl.multiple_of(h * HD, HD), HD)
+            att_t[feature, columns] = dot(v_t[feature], p_v[...]) / mass
+            lse_out[pl.ds(h, 1), columns] = top + jnp.log(mass)
+
+        loop(heads, lambda h: head(h, 0))
+        att_v[columns] = att_t[:, columns].T.astype(BF16)
+
+        @functools.partial(loop, depth // 512)
+        def _(t):
+            lanes = rows_of(t, 512)
+            part[columns, lanes] = dot(att_v[columns], wout_v[:, lanes]).astype(BF16)
+
+        loop(CHUNK // SUB, lambda s, c=c: line.push(s + c * (CHUNK // SUB)))
+
+    stores.append(pltpu.make_async_copy(att_v, att_hbm, store_sem.at[3]))
+    stores.append(pltpu.make_async_copy(att_t, att_t_hbm, store_sem.at[4]))
+    stores[3].start()
+    stores[4].start()
+    line.run(0, rows // SUB)
+    stores.append(pltpu.make_async_copy(total, sum_hbm, store_sem.at[5]))
+    stores[5].start()
+    line.drain_all(rows // SUB)
+
+    @pl.when(chip < chips - 1)
+    def _():
+        to_next.wait_send()
+
+    @pl.when(chip > 0)
+    def _():
+        forward.wait_send()
+
+    to_near.wait_send()
+    for item in stores:
+        item.wait()
+
+
+def attend(x, lengths, until, gains, shifts, wqkv, bqv, wout):
+    rows, depth = x.shape
+    width = wqkv.shape[2]
+    heads = width // HD
+    shape = jax.ShapeDtypeStruct
+    return pl.pallas_call(
+        attend_kernel,
+        out_shape=(
+            shape((rows, depth), BF16),
+            shape((rows, depth), BF16),
+            shape((rows, width), BF16),
+            shape((4 * rows, 2 * width), BF16),
+            shape((rows, width), BF16),
+            shape((width, rows), F32),
+            shape((heads, rows), F32),
+        ),
+        in_specs=[ANY, IN_SMEM, IN_SMEM, IN_VMEM, IN_VMEM, ANY, IN_VMEM, ANY],
+        out_specs=(ANY,) * 6 + (IN_VMEM,),
+        scratch_shapes=[
+            pltpu.VMEM((rows, depth), BF16),
+            pltpu.VMEM((rows, depth), BF16),
+            pltpu.VMEM((3, depth, width), BF16),
+            pltpu.VMEM((width, depth), BF16),
+            pltpu.VMEM((rows, width), BF16),
+            pltpu.VMEM((4 * rows, 2 * width), BF16),
+            pltpu.VMEM((heads, 2 * HD, rows), BF16),
+            pltpu.VMEM((width, 4 * rows), BF16),
+            pltpu.VMEM((4 * rows, CHUNK), F32),
+            pltpu.VMEM((4 * rows, CHUNK), BF16),
+            pltpu.VMEM((width, rows), F32),
+            pltpu.VMEM((rows, width), BF16),
+            *line_scratch(rows, depth),
+            pltpu.SemaphoreType.DMA((3,)),
+            pltpu.SemaphoreType.DMA((3,)),
+            pltpu.SemaphoreType.DMA((5,)),
+            pltpu.SemaphoreType.DMA((6,)),
+        ],
+        compiler_params=pltpu.CompilerParams(collective_id=0, has_side_effects=True, vmem_limit_bytes=56 * 2**20),
+        name="attend",
+    )(x, lengths, until, gains, shifts, wqkv, bqv, wout)
 
 
 def passed_along(value, axis, steps):
@@ -29,7 +406,8 @@
 
 
 def row_info(seq_lengths, active_until, first, count):
-    ends = jnp.cumsum(seq_lengths)
+    index = jnp.arange(seq_lengths.shape[0])
+    ends = jnp.sum(jnp.where(index[None, :] <= index[:, None], seq_lengths[None, :], 0), axis=1)
     starts = ends - seq_lengths
     rows = first + jnp.arange(count)
     inside = (rows[:, None] >= starts[None, :]) & (rows[:, None] < ends[None, :])
@@ -49,10 +427,6 @@
         & (key_seg[None, :] >= 0)
     )
     return (jnp.where(allowed[None], scores, NEG), allowed)
-
-
-def keep_carry(acc):
-    return acc
 
 
 def shards(
@@ -82,86 +456,23 @@
     gate = active[:, None]
     input_full = layer_input.astype(jnp.float32)
     first_norm_output, ln1_pull = jax.vjp(layer_norm, input_full, ln_gains[0], ln_shifts[0])
-    first_norm_lowered = first_norm_output.astype(jnp.bfloat16)
-    projected_rows = jnp.einsum(
-        "oa,amh->omh",
-        first_norm_lowered,
-        query_key_value_weight,
-        preferred_element_type=jnp.float32,
-    )
-    q_b = (projected_rows[:, 0] + b_qv[0]).astype(jnp.bfloat16)
-    k_b = projected_rows[:, 1].astype(jnp.bfloat16)
-    v_b = (projected_rows[:, 2] + b_qv[1]).astype(jnp.bfloat16)
+    (attn_sum, first_norm_lowered, q_b, kv_all, attended_low, attended_t, lse) = attend(
+        layer_input, seq_lengths, active_until, ln_gains, ln_shifts,
+        jnp.transpose(query_key_value_weight, (1, 0, 2)), b_qv, w_out,
+    )
     q_h = q_b.reshape(rows, heads, HD)
-    kv_own = jnp.concatenate([k_b, v_b], axis=1)
-
-    def pass_step(index, state):
-        stored, current = state
-        current = passed_along(current, "cp", 1)
-        return (lax.dynamic_update_index_in_dim(stored, current, index, 0), current)
-
-    stored0 = jnp.zeros((reach + 1, rows, 2 * width), jnp.bfloat16).at[0].set(kv_own)
-    kept, unused_last = lax.fori_loop(1, reach + 1, pass_step, (stored0, kv_own))
+    core = lax.rem(lax.axis_index("cp"), 2)
 
     def block_of(index):
-        block = lax.dynamic_index_in_dim(kept, index, 0, keepdims=False)
+        block = lax.dynamic_slice_in_dim(kv_all, jnp.maximum(2 + core - index, 0) * rows, rows, 0)
         return (
             block[:, :width].reshape(rows, heads, HD),
             block[:, width:].reshape(rows, heads, HD),
         )
 
-    def stats_step(index, acc):
-        key_start = first - index * rows
-
-        def stats_work(acc):
-            keys3, unused_vals = block_of(index)
-            key_rows, key_seg, unused = row_info(seq_lengths, active_until, key_start, rows)
-            masked, allowed = block_scores(q_h, keys3, my_rows, my_seg, key_rows, key_seg, scale)
-            top, total = acc
-            new_top = jnp.maximum(top, jnp.max(masked, axis=-1))
-            total = total * jnp.exp(top - new_top) + jnp.sum(
-                jnp.where(allowed[None], jnp.exp(masked - new_top[:, :, None]), 0.0), axis=-1
-            )
-            return (new_top, total)
-
-        return lax.cond(key_start >= 0, stats_work, keep_carry, acc)
-
-    start_top = jnp.full((heads, rows), NEG, jnp.float32)
-    start_total = jnp.zeros((heads, rows), jnp.float32)
-    top, total = lax.fori_loop(0, reach + 1, stats_step, (start_top, start_total))
-    lse = top + jnp.log(total)
-
-    def value_step(index, acc):
-        key_start = first - index * rows
-
-        def value_work(acc):
-            keys3, vals3 = block_of(index)
-            key_rows, key_seg, unused = row_info(seq_lengths, active_until, key_start, rows)
-            masked, allowed = block_scores(q_h, keys3, my_rows, my_seg, key_rows, key_seg, scale)
-            probs = jnp.where(allowed[None], jnp.exp(masked - lse[:, :, None]), 0.0)
-            probs_low = probs.astype(jnp.bfloat16)
-            rest = (probs - probs_low.astype(jnp.float32)).astype(jnp.bfloat16)
-            upper = acc[0] + jnp.einsum(
-                "hqk,khd->qhd", probs_low, vals3, preferred_element_type=jnp.float32
-            )
-            lower = acc[1] + jnp.einsum(
-                "hqk,khd->qhd", rest, vals3, preferred_element_type=jnp.float32
-            )
-            return (upper, lower)
-
-        return lax.cond(key_start >= 0, value_work, keep_carry, acc)
-
     zero_q = jnp.zeros((rows, heads, HD), jnp.float32)
-    upper, lower = lax.fori_loop(0, reach + 1, value_step, (zero_q, zero_q))
-    attended_low = upper.reshape(rows, width).astype(jnp.bfloat16)
-    combined = upper + lower
-    attn = (
-        lax.psum(
-            jnp.dot(attended_low, w_out, preferred_element_type=jnp.float32).astype(jnp.bfloat16),
-            "tp",
-        ).astype(jnp.float32)
-        + b_outs[0]
-    )
+    combined = attended_t.T.reshape(rows, heads, HD)
+    attn = attn_sum.astype(jnp.float32) + b_outs[0]
     hidden_state = input_full + gate * attn
     norm2, ln2_pull = jax.vjp(layer_norm, hidden_state, ln_gains[1], ln_shifts[1])
     norm2_low = norm2.astype(jnp.bfloat16)

time: 894 us -> 765 us (0.86)
  waiting for transfers between devices: 565 us -> 440 us
  Pallas kernels: 0 us -> 92.1 us
  starting transfers between devices: 37.4 us -> 4.1 us
  local copies, waits for them, and re-layouts: 54 us -> 23.4 us
  other arithmetic: 87.4 us -> 63.5 us
  matrix products: 104 us -> 90.3 us
    psum x1 -> x0, waiting for transfers between devices: 147 us -> none  [shards(): lax.psum(jnp.dot(attended_low, w_out, preferred_element_type=jnp.float32)...]
    pallas_call x0 -> x1, Pallas kernels: none -> 92.1 us  [attend(): pl.pallas_call(attend_kernel, out_shape=(shape((rows, depth), BF16), shap...]
    ppermute x6 -> x3, starting transfers between devices: 36.9 us -> 3.85 us  [passed_along(): lax.ppermute(value, axis, [(source, source + steps) for source in range(f...]
    psum x1, waiting for transfers between devices: 85.6 us -> 108 us  [shards(): lax.psum(jnp.einsum('tf,df->td', g_pre, w_up, preferred_element_type=jnp....]
    dot_general x4 -> x0, matrix products: 13.6 us -> none  [the longest x1 5.96 us: shards(): jnp.einsum('oa,amh->omh', first_norm_lowered, query_key_value_weight, pre...]
    reduce_sum x5 -> x4, other arithmetic: 24.9 us -> 11.5 us  [layer_norm(): return centred * lax.rsqrt(var + EPS) * gain + shift]
    while x4 -> x12, local copies, waits for them, and re-layouts: 9.05 us -> 0.02 us
    unnamed x128 -> x83, local copies, waits for them, and re-layouts: 18.6 us -> 12.8 us
  transfers between devices with their start and end apart: 13 -> 9, of which waited for: 11 -> 8; matrix products, arithmetic and copies ran while one was open for 13% -> 16% of each run, Pallas kernels for 0% -> 0%
where the time goes in v1:
time: 765 us; the launch traced here: 754 us
  waiting for transfers between devices  440 us (58%)
  Pallas kernels  92.1 us (12%)
  matrix products  90.3 us (12%)
  other arithmetic  63.5 us (8%)
  blocking collectives  24.7 us (3%)
  local copies, waits for them, and re-layouts  23.4 us (3%)
  between operations  15.1 us (2%)
    psum x1, waiting for transfers between devices, shards(): lax.psum(jnp.dot(act_low, w_down, preferred_element_type=jnp.float32).ast...  148 us
    psum x1, waiting for transfers between devices, shards(): lax.psum(jnp.einsum('tf,df->td', g_pre, w_up, preferred_element_type=jnp....  108 us
    pallas_call x1, Pallas kernels, attend(): pl.pallas_call(attend_kernel, out_shape=(shape((rows, depth), BF16), shap...  92.1 us
    reduce_scatter x1, waiting for transfers between devices, shards(): lax.psum_scatter(up_term.astype(jnp.bfloat16), 'cp', scatter_dimension=0,...  72.3 us
    reduce_scatter x1, waiting for transfers between devices, shards(): lax.psum_scatter(down_term.astype(jnp.bfloat16), 'cp', scatter_dimension=...  72.1 us
    psum x1, blocking collectives, shards(): lax.psum(jnp.stack([gain1_term, gain2_term]).astype(jnp.bfloat16), 'cp')  24.7 us
    reduce_scatter x1, waiting for transfers between devices, shards(): lax.psum_scatter(query_key_value_term.astype(jnp.bfloat16), 'cp', scatter...  20.9 us
    ppermute x3, waiting for transfers between devices, passed_along(): lax.ppermute(value, axis, [(source, source + steps) for source in range(f...  18.7 us
  transfers between devices with their start and end apart: 9, of which 8 were waited for; matrix products, arithmetic and copies ran while one was open for 16% of the time, Pallas kernels for 0%

profile of v1, /device:TPU:0, one launch (start us, length us, event | category | flops | bytes accessed | tf_op | source)
XLA Modules:
  0.0 753.7 jit_solution(9158643586777637370)
XLA Ops:
  13.0 92.1 %attend.1 = (bf16[512,2048]{1,0:T(8,128)(2,1)}, bf16[512,2048]{1,0:T(8,128)(2,1)}, bf16[512,512]{1,0:T(8,128)(2,1)}, bf16[2048,1024]{1,0:T(8,128)(2,1)}, bf16[51...) custom-call(bf16[512,2048]{1,0:T(8,128)(2,1)} %x_hbm.1, s32[3]{0:T(128)} %lengths_ref.1, s32[3]{0:T(128)} %until_ref.1, ...), custom_call_target="tpu_custom_call" | custom-call | tf_op jit(solution)/shard_map/attend/pallas_call | solution.py:354
  105.2 2.7 fusion.61
  109.2 7.9 %fusion.60 = f32[512,2048]{1,0:T(8,128)S(1)} fusion(bf16[2048,2048]{1,0:T(8,128)(2,1)} %param.28, f32[2048]{0:T(1024)S(1)} %bitcast.137, f32[2048]{0:T(1024)S(1)} %bitcast.132, f32[512]{0:T(512)S(1)} %fusion.50, f32[512]{0:T(512)S(1)} %broadcast_multiply_fusion.1, bf16[512,2048]{1,0:T(8,128)(2,1)S(1)} %copy-done, bf16[512,2048]{1,0:T(8,128)(2,1)S(1)} %copy-done.2, ...), kind=kOutput, calls=%fused_computation.137 | convolution fusion | flops 4305453056 | bytes 16807936 | tf_op jit(solution)/shard_map/dot_general | solution.py:479
  117.1 11.6 %fusion.69 = (bf16[2048]{0:T(1024)(128)(2,1)}, bf16[512,2048]{1,0:T(8,128)(2,1)S(1)}) fusion(f32[512,2048]{1,0:T(8,128)S(1)} %fusion.60, f32[2048]{0:T(1024)S(1)} %copy-done.36, bf16[2048,2048]{1,0:T(8,128)(2,1)} %param.30, bf16[512,2048]{1,0:T(8,128)(2,1)S(1)} %copy-done.7, f32[512]{0:T(512)S(1)} %fusion.49), kind=kOutput, calls=%fused_computation.146 | convolution fusion | flops 4321179648 | bytes 16791552 | tf_op jit(solution)/shard_map/td,fd->tf/dot_general | solution.py:491
  130.1 6.0 convolution_convert_fusion.4
  136.1 107.7 %all-reduce.5.cloned.1.call-done = bf16[512,2048]{1,0:T(8,128)(2,1)} async-done(((bf16[512,2048]{1,0:T(8,128)(2,1)}), bf16[512,2048]{1,0:T(8,128)(2,1)}) %all-reduce.5.cloned.1.call-update) | async-done | bytes 2097168 | tf_op jit(solution)/shard_map/psum | solution.py:496
  243.8 5.4 fusion.35
  249.3 2.3 fusion.64
  251.6 2.0 fusion.62
  255.0 2.6 convolution_convert_fusion.3
  257.7 11.1 %convolution_convert_fusion.5 = bf16[512,2048]{1,0:T(8,128)(2,1)} fusion(bf16[2048,2048]{1,0:T(8,128)(2,1)} %param.30, f32[512,2048]{1,0:T(8,128)} %copy-done.39, f32[2048]{0:T(1024)S(1)} %copy-done.36), kind=kOutput, calls=%fused_computation.98 | convolution fusion | flops 4306501632 | bytes 14688256 | tf_op jit(solution)/shard_map/dot_general | solution.py:484
  269.8 7.0 copy.57
  276.9 3.5 fusion.48
  280.4 2.2 conditional.2
  282.5 51.8 %while.17 = (s32[]{:T(128)}, f32[512,8,64]{0,2,1:T(8,128)}, bf16[512,1024]{0,1:T(8,128)(2,1)}, s32[]{:T(128)}, s32[]{:T(128)}, /*index=5*/bf16[2048,1024]{0,1:T(...) while((s32[]{:T(128)}, f32[512,8,64]{0,2,1:T(8,128)}, ...), condition=%wide.region_19.20_spmd.clone.clone, body=%wide.region_14.19_spmd.clone.clone.sunk | while | flops 1371284992 | bytes 67448432 | solution.py:555
  284.4 2.4 add.409
  287.6 2.5 convert_add_fusion.6
  291.9 2.4 add.409
  294.3 14.3 %collective-permute-done = bf16[512,1024]{0,1:T(8,128)(2,1)} collective-permute-done((bf16[512,1024]{0,1:T(8,128)(2,1)}, bf16[512,1024]{0,1:T(8,128)(2,1)}, u32[]{:S(2)}, u32[]{:S(2)}) %collective-permute-start) | collective-permute-done | bytes 1048608 | tf_op jit(solution)/shard_map/while/body/eval_jaxpr/ppermute | solution.py:394
  308.6 2.5 convert_add_fusion.6
  312.5 13.3 %conditional.6 = (f32[512,8,64]{0,2,1:T(8,128)S(1)}, f32[512,1024]{0,1:T(8,128)S(1)}) conditional(s32[]{:T(128)} %convert_element_type.352, () %tuple.90, (s32[]{:T(128)}, s32[]{:T(128)}, bf16[2048,1024]{0,1:T(8,128)(2,1)}, s32[]{:T(128)}, s32[]{:T(128)}, /*index=5*/s32[3]{0:T(128)S(1)}, s32[512]{0:T(512)S(1)}, bf16[512,8,64]{0,2,1:T(8,128)(2,1)}, ...), branch_computations={%region_15.15_spmd, %region_16.18_spmd} | conditional | flops 1369449984 | bytes 51717352 | solution.py:544
  314.3 2.3 fusion.71
  316.7 2.3 fusion.19
  319.0 3.4 fusion.14
  322.4 2.4 convolution_multiply_fusion.2
  325.8 2.4 add.409
  328.2 3.6 collective-permute-done
  331.8 2.5 convert_add_fusion.6
  337.6 7.4 bitcast_convert_fusion
  345.1 7.0 convolution_convert_fusion.2
  352.2 1.5 copy-done.9
  353.7 11.3 %convolution_convert_fusion = bf16[2048,2048]{1,0:T(8,128)(2,1)} fusion(bf16[512,2048]{1,0:T(8,128)(2,1)S(1)} %copy-done.9, f32[512]{0:T(512)S(1)} %copy-done.17, f32[512,2048]{1,0:T(8,128)} %copy-done.39, f32[2048]{0:T(1024)S(1)} %copy-done.36), kind=kOutput, calls=%fused_computation.53 | convolution fusion | flops 4312793088 | bytes 14690304 | tf_op jit(solution)/shard_map/tf,td->fd/dot_general | solution.py:493
  365.1 1.5 copy-done.1
  366.6 10.7 %convolution_convert_fusion.1 = bf16[2048,2048]{1,0:T(8,128)(2,1)} fusion(bf16[512,2048]{1,0:T(8,128)(2,1)} %copy-done.40, f32[2048]{0:T(1024)S(1)} %bitcast.138, f32[2048]{0:T(1024)S(1)} %bitcast.135, f32[512]{0:T(512)S(1)} %copy-done.24, f32[512]{0:T(512)S(1)} %copy-done.21, bf16[512,2048]{1,0:T(8,128)(2,1)S(1)} %copy-done.1, ...), kind=kOutput, calls=%fused_computation.54 | convolution fusion | flops 4309647360 | bytes 14710784 | tf_op jit(solution)/shard_map/td,tf->df/dot_general | solution.py:494
  377.3 2.0 reduce.3
  379.6 1.8 convert_element_type.190
  381.4 148.1 %all-reduce.7.cloned.1.call-done = (bf16[512,2048]{1,0:T(8,128)(2,1)}, bf16[512,2048]{1,0:T(8,128)(2,1)}) async-done(((bf16[512,2048]{1,0:T(8,128)(2,1)}, bf16[512,2048]{1,0:T(8,128)(2,1)}), (bf16[512,2048]{1,0:T(8,128)(2,1)}, bf16[512,2048]{1,0:T(8,128)(2,1)})) %all-reduce.7.cloned.1.call-update) | async-done | bytes 4194320 | tf_op jit(solution)/shard_map/psum | solution.py:483
  529.6 2.0 reduce.2
  531.6 3.0 fusion.44
  534.6 2.2 fusion.36
  536.9 24.7 %all-reduce = (bf16[2,2048]{1,0:T(2,128)(2,1)S(1)}, bf16[2,2048]{1,0:T(2,128)(2,1)S(1)}, bf16[2,512]{1,0:T(2,128)(2,1)S(1)}, bf16[2,2048]{1,0:T(2,128)(2,1)S(1)}, bf16[2048]{0:T(1024)(128)(2,1)S(1)}) all-reduce(bf16[2,2048]{1,0:T(2,128)(2,1)S(1)} %get-tuple-element.510, ...), channel_id=1, replica_groups=mesh['cp'=8,'tp'=4] {'cp'}, use_global_device_ids=true, to_apply=%region_27.28 | all-reduce | flops 15360 | bytes 61440 | tf_op jit(solution)/shard_map/psum | solution.py:592
  564.6 8.5 %add_add_fusion.2 = (f32[512,2048]{1,0:T(8,128)}, f32[512,2048]{1,0:T(8,128)}) fusion(bf16[512,2048]{1,0:T(8,128)(2,1)S(1)} %copy-done.1, bf16[512,2048]{1,0:T(8,128)(2,1)} %get-tuple-element.481, f32[512,2048]{1,0:T(8,128)} %copy-done.4, bf16[512,2048]{1,0:T(8,128)(2,1)} %param.31, f32[512]{0:T(512)S(1)} %negate_multiply_fusion, ...), kind=kLoop, calls=%fused_computation.90 | loop fusion | flops 22020096 | bytes 23105536 | tf_op jit(solution)/shard_map/add | solution.py:576
  573.1 20.9 %reduce-scatter.5.cloned.1.call-done = bf16[256,3,512]{2,0,1:T(8,128)(2,1)} async-done(((bf16[2048,3,512]{2,0,1:T(8,128)(2,1)}), bf16[256,3,512]{2,0,1:T(8,128)(2,1)}) %reduce-scatter.5.cloned.1.call-update) | async-done | bytes 786448 | tf_op jit(solution)/shard_map/reduce_scatter | solution.py:578
  594.0 2.5 convert_element_type.185
  596.5 72.1 %reduce-scatter.11.cloned.1.call-done = bf16[2048,256]{1,0:T(8,128)(2,1)} async-done(((bf16[2048,2048]{1,0:T(8,128)(2,1)}), bf16[2048,256]{1,0:T(8,128)(2,1)}) %reduce-scatter.11.cloned.1.call-update) | async-done | bytes 1048592 | tf_op jit(solution)/shard_map/reduce_scatter | solution.py:587
  668.5 2.7 convert_element_type.198
  671.2 72.3 %reduce-scatter.9.cloned.1.call-done = bf16[256,2048]{1,0:T(8,128)(2,1)} async-done(((bf16[2048,2048]{1,0:T(8,128)(2,1)}), bf16[256,2048]{1,0:T(8,128)(2,1)}) %reduce-scatter.9.cloned.1.call-update) | async-done | bytes 1048592 | tf_op jit(solution)/shard_map/reduce_scatter | solution.py:584
  743.6 2.8 convert_element_type.195
  (171 shorter events, 28.8 us)
Async XLA Ops:
  7.2 236.6 %all-reduce.5.cloned.1.call-start = ((), (), s32[]{:S(2)}) async-start(), calls=%async_computation.4 | async-start | bytes 4194304 | tf_op jit(solution)/shard_map/psum | solution.py:496
  9.4 99.7 %copy-start.31 = (f32[1,2048]{1,0:T(1,128)}, f32[1,2048]{1,0:T(1,128)S(1)}, u32[]{:S(2)}) copy-start(f32[1,2048]{1,0:T(1,128)S(1)} %slice.37) | copy-start | bytes 24580
  10.8 238.4 %copy-start.13 = (f32[1,2048]{1,0:T(1,128)}, f32[1,2048]{1,0:T(1,128)S(1)}, u32[]{:S(2)}) copy-start(f32[1,2048]{1,0:T(1,128)S(1)} %get-tuple-element.503) | copy-start | bytes 24580
  12.2 237.0 %copy-start.18 = (f32[1,2048]{1,0:T(1,128)}, f32[1,2048]{1,0:T(1,128)S(1)}, u32[]{:S(2)}) copy-start(f32[1,2048]{1,0:T(1,128)S(1)} %get-tuple-element.501) | copy-start | bytes 24580
  13.0 238.6 %copy-start.16 = (f32[512]{0:T(512)}, f32[512]{0:T(512)S(1)}, u32[]{:S(2)}) copy-start(f32[512]{0:T(512)S(1)} %fusion.49) | copy-start | bytes 6148
  13.0 92.2 %copy-start = (bf16[512,2048]{1,0:T(8,128)(2,1)S(1)}, bf16[512,2048]{1,0:T(8,128)(2,1)}, u32[]{:S(2)}) copy-start(bf16[512,2048]{1,0:T(8,128)(2,1)} %x_hbm.1) | copy-start | bytes 6291460
  105.2 2.7 copy-start.2
  107.9 141.4 %copy-start.20 = (f32[512]{0:T(512)}, f32[512]{0:T(512)S(1)}, u32[]{:S(2)}) copy-start(f32[512]{0:T(512)S(1)} %broadcast_multiply_fusion.1) | copy-start | bytes 6148
  109.1 140.1 %copy-start.23 = (f32[512]{0:T(512)}, f32[512]{0:T(512)S(1)}, u32[]{:S(2)}) copy-start(f32[512]{0:T(512)S(1)} %fusion.50) | copy-start | bytes 6148
  109.1 7.9 %copy-start.7 = (bf16[512,2048]{1,0:T(8,128)(2,1)S(1)}, bf16[512,2048]{1,0:T(8,128)(2,1)}, u32[]{:S(2)}) copy-start(bf16[512,2048]{1,0:T(8,128)(2,1)} %param.31) | copy-start | bytes 6291460
  109.1 7.9 %copy-start.36 = (f32[2048]{0:T(1024)S(1)}, f32[2048]{0:T(1024)}, u32[]{:S(2)}) copy-start(f32[2048]{0:T(1024)} %param.29) | copy-start | bytes 24580
  109.2 20.9 %slice-start = ((s8[8388608]{0:T(1024)(128)(4,1)}), s8[4194304]{0:T(1024)(128)(4,1)S(1)}, s32[]{:S(2)}) async-start(s8[8388608]{0:T(1024)(128)(4,1)} %bitcast.139), calls=%async_computation.10 | async-start | bytes 8388608
  117.1 11.6 %copy-start.39 = (f32[512,2048]{1,0:T(8,128)}, f32[512,2048]{1,0:T(8,128)S(1)}, u32[]{:S(2)}) copy-start(f32[512,2048]{1,0:T(8,128)S(1)} %fusion.60) | copy-start | bytes 12582916
  117.1 12.9 %slice-start.1 = ((s8[8388608]{0:T(1024)(128)(4,1)}), s8[4194304]{0:T(1024)(128)(4,1)S(1)}, s32[]{:S(2)}) async-start(s8[8388608]{0:T(1024)(128)(4,1)} %bitcast.139), calls=%async_computation.11 | async-start | bytes 8388608
  136.0 243.5 %reduce-scatter.7.cloned.1.call-start = ((), (), s32[]{:S(2)}) async-start(), calls=%async_computation.6 | async-start | bytes 2359296 | tf_op jit(solution)/shard_map/reduce_scatter | solution.py:581
  243.8 5.4 copy-start.3
  243.8 5.4 copy-start.6
  249.3 2.4 copy-start.8
  251.6 2.1 copy-start.4
  251.6 2.1 copy-start.25
  251.6 3.4 copy-start.35
  257.6 11.2 %copy-start.12 = (bf16[512,512]{1,0:T(8,128)(2,1)S(1)}, bf16[512,512]{1,0:T(8,128)(2,1)}, u32[]{:S(2)}) copy-start(bf16[512,512]{1,0:T(8,128)(2,1)} %get-tuple-element.302) | copy-start | bytes 1572868
  257.6 271.9 %all-reduce.7.cloned.1.call-start = ((), (), s32[]{:S(2)}) async-start(), calls=%async_computation.9 | async-start | bytes 8388608 | tf_op jit(solution)/shard_map/psum | solution.py:483
  269.8 7.0 copy-start.10
  276.9 3.5 copy-start.34
  282.7 4.9 collective-permute-start
  286.8 3.3 copy-start.38
  290.1 18.5 %collective-permute-start = (bf16[512,1024]{0,1:T(8,128)(2,1)}, bf16[512,1024]{0,1:T(8,128)(2,1)}, u32[]{:S(2)}, u32[]{:S(2)}) collective-permute-start(bf16[512,1024]{0,1:T(8,128)(2,1)} %get-tuple-element.615), channel_id=1, source_target_pairs={{4,0},{8,4},{12,8},{16,12},{20,16},{24,20},{28,24},{5,1},{9,5},{13... | collective-permute-start | bytes 3145736 | tf_op jit(solution)/shard_map/while/body/eval_jaxpr/ppermute | solution.py:394
  294.3 16.9 %copy-start.38 = (bf16[512,8,64]{0,2,1:T(8,128)(2,1)S(1)}, bf16[512,8,64]{0,2,1:T(8,128)(2,1)}, u32[]{:S(2)}) copy-start(bf16[512,8,64]{0,2,1:T(8,128)(2,1)} %copy-done.37) | copy-start | bytes 1572868 | tf_op jit(solution)/shard_map/while
  311.1 20.7 %collective-permute-start = (bf16[512,1024]{0,1:T(8,128)(2,1)}, bf16[512,1024]{0,1:T(8,128)(2,1)}, u32[]{:S(2)}, u32[]{:S(2)}) collective-permute-start(bf16[512,1024]{0,1:T(8,128)(2,1)} %get-tuple-element.615), channel_id=1, source_target_pairs={{4,0},{8,4},{12,8},{16,12},{20,16},{24,20},{28,24},{5,1},{9,5},{13... | collective-permute-start | bytes 3145736 | tf_op jit(solution)/shard_map/while/body/eval_jaxpr/ppermute | solution.py:394
  328.2 6.2 copy-start.38
  345.1 248.9 %reduce-scatter.5.cloned.1.call-start = ((), (), s32[]{:S(2)}) async-start(), calls=%async_computation.5 | async-start | bytes 7077888 | tf_op jit(solution)/shard_map/reduce_scatter | solution.py:578
  352.1 1.6 copy-start.9
  352.1 1.6 copy-start.17
  352.1 316.4 %reduce-scatter.11.cloned.1.call-start = ((), (), s32[]{:S(2)}) async-start(), calls=%async_computation.8 | async-start | bytes 9437184 | tf_op jit(solution)/shard_map/reduce_scatter | solution.py:587
  365.0 1.6 copy-start.14
  365.0 1.6 copy-start.19
  365.0 1.6 copy-start.21
  365.0 378.5 %reduce-scatter.9.cloned.1.call-start = ((), (), s32[]{:S(2)}) async-start(), calls=%async_computation.7 | async-start | bytes 9437184 | tf_op jit(solution)/shard_map/reduce_scatter | solution.py:584
  377.3 2.0 copy-start.27
  377.3 2.0 copy-start.29
  377.3 2.1 copy-start.28
  377.3 2.2 copy-start.30
  377.3 154.2 %copy-start.15 = (f32[1,2048]{1,0:T(1,128)S(1)}, f32[1,2048]{1,0:T(1,128)}, u32[]{:S(2)}) copy-start(f32[1,2048]{1,0:T(1,128)} %get-tuple-element.500) | copy-start | bytes 24580
  531.5 3.1 copy-start.5
  531.5 5.3 copy-start.33
  531.6 33.1 %copy-start.22 = (f32[1,2048]{1,0:T(1,128)S(1)}, f32[1,2048]{1,0:T(1,128)}, u32[]{:S(2)}) copy-start(f32[1,2048]{1,0:T(1,128)} %get-tuple-element.502) | copy-start | bytes 24580
  531.6 33.1 %copy-start.26 = (f32[512]{0:T(512)S(1)}, f32[512]{0:T(512)}, u32[]{:S(2)}) copy-start(f32[512]{0:T(512)} %copy-done.25) | copy-start | bytes 6148
  (8 other events, 11.4 us)
Sparse Core Ops, SparseCore 0:
  136.2 107.5 all-reduce.4
  257.7 41.6 reduce-scatter.6
  345.2 184.3 all-reduce.6
  533.2 60.7 reduce-scatter.4
  597.3 71.2 reduce-scatter.10
  672.3 71.2 reduce-scatter.8

commit v2 on v1

--- a/solution.py
+++ b/solution.py
@@ -1,4 +1,5 @@
 import functools
+import math
 
 import jax
 import jax.numpy as jnp
@@ -388,6 +389,372 @@
     )(x, lengths, until, gains, shifts, wqkv, bqv, wout)
 
 
+class Scatter:
+    def __init__(self, terms, near, far, send, recv, split):
+        self.cp, self.tp, self.core, self.chip = place()
+        self.count = lax.axis_size("cp")
+        self.depth = (self.count // 2).bit_length() - 1
+        self.terms, self.near, self.far = terms, near, far
+        self.send, self.recv = send, recv
+        self.chunk = terms.shape[0] // self.count
+        self.width = terms.shape[1]
+        self.parts = [p for p in ((0, 0, split), (1, split, self.width)) if p[2] > p[1]]
+        self.block = max(self.chunk, 128)
+
+    def partners(self):
+        others = [(self.cp + 1 - 2 * self.core, self.tp)]
+        for bit in range(self.depth):
+            others.append((self.cp + 2 * self.step(bit), self.tp))
+        return others
+
+    def step(self, bit):
+        return (1 - 2 * self.bit(bit)) * (1 << bit)
+
+    def bit(self, bit):
+        return lax.rem(lax.div(self.chip, 1 << bit), 2)
+
+    def fill(self, k, pick):
+        if self.block == self.chunk:
+            half = self.count // 2
+            block = 2 * lax.rem(k, half) + jnp.where(k < half, 1 - self.core, self.core)
+        else:
+            block = k
+        rows = rows_of(block, self.block)
+        for tile in range(self.width // 512):
+            lanes = slice(tile * 512, (tile + 1) * 512)
+            left, right = pick(tile, rows)
+            self.terms[rows, lanes] = dot_tn(left, right).astype(BF16)
+
+    def blocks(self):
+        return self.terms.shape[0] // self.block
+
+    def near_copy(self, t):
+        return pltpu.make_async_remote_copy(
+            src_ref=self.terms.at[rows_of(2 * t + 1 - self.core, self.chunk)],
+            dst_ref=self.near.at[rows_of(t, self.chunk)],
+            send_sem=self.send.at[t],
+            recv_sem=self.recv.at[t],
+            device_id=(self.cp + 1 - 2 * self.core, self.tp),
+            device_id_type=MESH,
+        )
+
+    def send_near(self, t):
+        self.near_copy(t).start()
+
+    def add_near(self, t):
+        self.near_copy(t).wait_recv()
+        base = (2 * t + self.core) * self.chunk
+
+        @functools.partial(loop, self.chunk // 64)
+        def _(i):
+            mine = pl.ds(pl.multiple_of(base + i * 64, 64), 64)
+            other = pl.ds(pl.multiple_of(t * self.chunk + i * 64, 64), 64)
+            self.terms[mine] = (self.terms[mine].astype(F32) + self.near[other].astype(F32)).astype(BF16)
+
+    def index(self, part, level, t, keep):
+        bit = level - 1 if part == 0 else self.depth - level
+        own = self.bit(bit)
+        own = own if keep else 1 - own
+        if part == 0:
+            return lax.rem(self.chip, 1 << bit) + own * (1 << bit) + t * (2 << bit), bit
+        return self.chip - lax.rem(self.chip, 2 << bit) + own * (1 << bit) + t, bit
+
+    def pieces(self, level):
+        first = self.count // 2
+        for earlier in range(1, level):
+            first += len(self.parts) * (1 << (self.depth - earlier))
+        for part, low, high in self.parts:
+            for t in range(1 << (self.depth - level)):
+                yield part, slice(low, high), t, first
+                first += 1
+
+    def far_copy(self, level, part, lanes, t, sem):
+        index, bit = self.index(part, level, t, False)
+        return pltpu.make_async_remote_copy(
+            src_ref=self.terms.at[rows_of(2 * index + self.core, self.chunk), lanes],
+            dst_ref=self.far.at[pl.ds(self.place(level) + t * self.chunk, self.chunk), lanes],
+            send_sem=self.send.at[sem],
+            recv_sem=self.recv.at[sem],
+            device_id=(self.cp + 2 * self.step(bit), self.tp),
+            device_id_type=MESH,
+        )
+
+    def send_far(self, level):
+        for piece in self.pieces(level):
+            self.far_copy(level, *piece).start()
+
+    def add_far(self, level):
+        for part, lanes, t, sem in self.pieces(level):
+            self.far_copy(level, part, lanes, t, sem).wait_recv()
+            index, _ = self.index(part, level, t, True)
+            base = (2 * index + self.core) * self.chunk
+            there = self.place(level) + t * self.chunk
+
+            @functools.partial(loop, self.chunk // 64)
+            def _(i, base=base, lanes=lanes, there=there):
+                mine = pl.ds(pl.multiple_of(base + i * 64, 64), 64)
+                other = pl.ds(pl.multiple_of(there + i * 64, 64), 64)
+                self.terms[mine, lanes] = (
+                    self.terms[mine, lanes].astype(F32) + self.far[other, lanes].astype(F32)
+                ).astype(BF16)
+
+    def place(self, level):
+        return sum(self.terms.shape[0] >> (earlier + 1) for earlier in range(1, level))
+
+    def finish(self, write):
+        level = self.depth
+        mine = rows_of(self.cp, self.chunk)
+        for part, lanes, t, sem in self.pieces(level):
+            self.far_copy(level, part, lanes, t, sem).wait_recv()
+            for tile in range(lanes.start // 512, lanes.stop // 512):
+                cut = slice(tile * 512, (tile + 1) * 512)
+                other = pl.ds(self.place(level), self.chunk)
+                write(tile, self.terms[mine, cut].astype(F32) + self.far[other, cut].astype(F32))
+
+    def drain(self):
+        loop(self.count // 2, lambda t: self.near_copy(t).wait_send())
+        for level in range(1, self.depth + 1):
+            for piece in self.pieces(level):
+                self.far_copy(level, *piece).wait_send()
+
+
+def scatter_scratch(depth, width, split):
+    count = lax.axis_size("cp")
+    parts = (split > 0) + (split < width)
+    sems = count // 2 + parts * (count // 2 - 1)
+    return [
+        pltpu.VMEM((depth // 2, width), BF16),
+        pltpu.VMEM((depth // 2 - depth // count, width), BF16),
+        pltpu.SemaphoreType.DMA((sems,)),
+        pltpu.SemaphoreType.DMA((sems,)),
+    ]
+
+
+def fold(v):
+    return jnp.sum(v.reshape(v.shape[0] // 8, 8, v.shape[1]), axis=0)
+
+
+def gelu_parts(u):
+    root = math.sqrt(2.0 / math.pi)
+    square = u * u
+    th = jnp.tanh(root * (u + 0.044715 * u * square))
+    half = 0.5 * (1.0 + th)
+    return u * half, half + 0.5 * u * (1.0 - th * th) * (root * (1.0 + 3 * 0.044715 * square))
+
+
+LAG = 4
+SPLIT_DOWN = 1024
+
+
+def ffn_kernel(
+    sum_hbm, x_hbm, d_hbm, lengths_ref, until_ref, gains, shifts, b_outs, b_up, up_hbm, down_hbm,
+    norm_hbm, g_pre_hbm, ffn_hbm, g_hidden_hbm, g_attn_hbm, sums_out, down_out,
+    up_v, down_v, d_v, xhat, rstd, norm_v, act_v, g_pre_v, g_ffn_v, ffn_v, g_hidden, g_attn, acc,
+    part, slot_a, slot_b, total, ar_send, ar_recv, near, far, rs_send, rs_recv, load_sem, store_sem,
+):
+    cp, tp, core, chip = place()
+    rows, depth = d_v.shape
+    hidden = up_v.shape[1]
+    count = rows // SUB
+    loads = [
+        pltpu.make_async_copy(x_hbm, g_attn, load_sem.at[0]),
+        pltpu.make_async_copy(sum_hbm, ffn_v, load_sem.at[1]),
+        pltpu.make_async_copy(d_hbm, d_v, load_sem.at[2]),
+        pltpu.make_async_copy(up_hbm, up_v, load_sem.at[3]),
+        pltpu.make_async_copy(down_hbm, down_v, load_sem.at[4]),
+    ]
+    for item in loads:
+        item.start()
+    line = LineSum(part, slot_a, slot_b, total, ar_send, ar_recv)
+    scatter = Scatter(up_v, near, far, rs_send, rs_recv, SPLIT_DOWN)
+    greet(cp, tp, scatter.partners())
+    _, live = band_info(lengths_ref, until_ref, cp * rows)
+    acc[...] = jnp.zeros_like(acc)
+    for item in loads[:3]:
+        item.wait()
+
+    for c in range(rows // CHUNK):
+        chunk = slice(c * CHUNK, (c + 1) * CHUNK)
+
+        @functools.partial(loop, CHUNK // 64)
+        def _(i, c=c):
+            at = pl.ds(pl.multiple_of(c * CHUNK + i * 64, 64), 64)
+            row = lax.broadcasted_iota(jnp.int32, (64, 1), 0) + (c * CHUNK + i * 64)
+            on = row < live
+            branch = ffn_v[at].astype(F32) + b_outs[0:1]
+            v = g_attn[at].astype(F32) + jnp.where(on, branch, 0.0)
+            mean = jnp.mean(v, axis=-1, keepdims=True)
+            centred = v - mean
+            scale = lax.rsqrt(jnp.mean(centred * centred, axis=-1, keepdims=True) + EPS)
+            hat = centred * scale
+            xhat[at] = hat
+            rstd[at] = jnp.broadcast_to(scale, (64, 128))
+            norm_v[at] = (hat * gains[1:2] + shifts[1:2]).astype(BF16)
+            g_ffn = jnp.where(on, d_v[at].astype(F32), 0.0)
+            g_ffn_v[at] = g_ffn.astype(BF16)
+            acc[3] += fold(g_ffn)
+
+        if c == 0:
+            loads[3].wait()
+            loads[4].wait()
+
+        @functools.partial(loop, hidden // 512)
+        def _(t, c=c, chunk=chunk):
+            lanes = rows_of(t, 512)
+            pre = dot(norm_v[chunk], up_v[:, lanes]) + b_up[0:1, lanes]
+            g_act = dot_nt(g_ffn_v[chunk], down_v[lanes])
+            act, slope = gelu_parts(pre)
+            act_v[chunk, lanes] = act.astype(BF16)
+            g_pre = (g_act * slope).astype(BF16)
+            g_pre_v[chunk, lanes] = g_pre
+            acc[4, :, lanes] += fold(g_pre.astype(F32))
+            if c > 0:
+                line.relay_in(t)
+
+                @pl.when(t > 0)
+                def _():
+                    line.relay_out(t - 1)
+
+        @functools.partial(loop, depth // 512)
+        def _(t, chunk=chunk):
+            lanes = rows_of(t, 512)
+            part[chunk, lanes] = dot_nt(g_pre_v[chunk], up_v[lanes]).astype(BF16)
+
+        loop(CHUNK // SUB, lambda s, c=c: line.push(s + c * (CHUNK // SUB)))
+
+    stores = [
+        pltpu.make_async_copy(norm_v, norm_hbm, store_sem.at[0]),
+        pltpu.make_async_copy(g_pre_v, g_pre_hbm, store_sem.at[1]),
+        pltpu.make_async_copy(ffn_v, ffn_hbm, store_sem.at[2]),
+        pltpu.make_async_copy(g_hidden, g_hidden_hbm, store_sem.at[3]),
+        pltpu.make_async_copy(g_attn, g_attn_hbm, store_sem.at[4]),
+    ]
+    stores[0].start()
+    stores[1].start()
+
+    def back(s):
+        line.get(s)
+        at = rows_of(s, SUB)
+        e = total[at].astype(F32)
+        hat = xhat[at]
+        t = e * gains[1:2]
+        along = t - jnp.mean(t, axis=-1, keepdims=True) - hat * jnp.mean(t * hat, axis=-1, keepdims=True)
+        value = d_v[at].astype(F32) + along * rstd[at, 0:1]
+        g_hidden[at] = value
+        row = lax.broadcasted_iota(jnp.int32, (SUB, 1), 0) + s * SUB
+        low = jnp.where(row < live, value, 0.0).astype(BF16)
+        g_attn[at] = low
+        acc[0] += fold(e * hat)
+        acc[1] += fold(e)
+        acc[2] += fold(low.astype(F32))
+
+    def ahead(s):
+        @pl.when(s < count)
+        def _():
+            line.relay_in(s)
+
+        line.relay_out(s - 1)
+        back(s - LAG)
+
+    def term(k):
+        scatter.fill(k, lambda tile, rows: (g_ffn_v[:, rows], act_v[:, tile * 512 : (tile + 1) * 512]))
+
+    def project(k):
+        chunk = rows_of(lax.div(k, depth // 512), CHUNK)
+        lanes = rows_of(lax.rem(k, depth // 512), 512)
+        ffn_v[chunk, lanes] = dot(act_v[chunk], down_v[:, lanes]).astype(BF16)
+
+    blocks, half = scatter.blocks(), scatter.count // 2
+
+    @functools.partial(loop, 4)
+    def _(i):
+        loop(blocks // 4, lambda j: term(i * (blocks // 4) + j))
+
+        @pl.when((i == 1) if scatter.block == scatter.chunk else (i == 3))
+        def _():
+            loop(half, scatter.send_near)
+
+        ahead(4 + i)
+
+    @functools.partial(loop, 2)
+    def _(i):
+        loop(half // 2, lambda j: scatter.add_near(i * (half // 2) + j))
+        ahead(8 + i)
+
+    scatter.send_far(1)
+
+    @functools.partial(loop, 4)
+    def _(i):
+        project(2 * i)
+        project(2 * i + 1)
+        ahead(10 + i)
+
+    stores[2].start()
+    loop(count - 13, lambda i: ahead(14 + i))
+    loop(LAG - 1, lambda i: back(count - LAG + 1 + i))
+    stores[3].start()
+    stores[4].start()
+    for level in range(1, scatter.depth):
+        scatter.add_far(level)
+        scatter.send_far(level + 1)
+
+    for k in range(5):
+        sums_out[k : k + 1] = jnp.sum(acc[k], axis=0, keepdims=True)
+
+    sums_out[5:8] = jnp.zeros((3, sums_out.shape[1]), F32)
+
+    def write(tile, value):
+        down_out[tile * 512 : (tile + 1) * 512] = value.T
+
+    scatter.finish(write)
+    scatter.drain()
+    line.drain_all(count)
+    for item in stores:
+        item.wait()
+
+
+def ffn(attn_sum, x, d_out, lengths, until, gains, shifts, b_outs, b_up, w_up, w_down):
+    rows, depth = x.shape
+    hidden = w_up.shape[1]
+    chunk = depth // lax.axis_size("cp")
+    shape = jax.ShapeDtypeStruct
+    return pl.pallas_call(
+        ffn_kernel,
+        out_shape=(
+            shape((rows, depth), BF16),
+            shape((rows, hidden), BF16),
+            shape((rows, depth), BF16),
+            shape((rows, depth), F32),
+            shape((rows, depth), BF16),
+            shape((8, depth), F32),
+            shape((hidden, chunk), F32),
+        ),
+        in_specs=[ANY, ANY, ANY, IN_SMEM, IN_SMEM, IN_VMEM, IN_VMEM, IN_VMEM, IN_VMEM, ANY, ANY],
+        out_specs=(ANY,) * 5 + (IN_VMEM,) * 2,
+        scratch_shapes=[
+            pltpu.VMEM((depth, hidden), BF16),
+            pltpu.VMEM((hidden, depth), BF16),
+            pltpu.VMEM((rows, depth), BF16),
+            pltpu.VMEM((rows, depth), F32),
+            pltpu.VMEM((rows, 128), F32),
+            pltpu.VMEM((rows, depth), BF16),
+            pltpu.VMEM((rows, hidden), BF16),
+            pltpu.VMEM((rows, hidden), BF16),
+            pltpu.VMEM((rows, depth), BF16),
+            pltpu.VMEM((rows, depth), BF16),
+            pltpu.VMEM((rows, depth), F32),
+            pltpu.VMEM((rows, depth), BF16),
+            pltpu.VMEM((5, 8, depth), F32),
+            *line_scratch(rows, depth),
+            *scatter_scratch(depth, hidden, SPLIT_DOWN),
+            pltpu.SemaphoreType.DMA((5,)),
+            pltpu.SemaphoreType.DMA((5,)),
+        ],
+        compiler_params=pltpu.CompilerParams(collective_id=1, has_side_effects=True, vmem_limit_bytes=62 * 2**20),
+        name="ffn",
+    )(attn_sum, x, d_out, lengths, until, gains, shifts, b_outs, b_up, w_up, w_down)
+
+
 def passed_along(value, axis, steps):
     count = lax.axis_size(axis)
     first, last = (max(0, -steps), min(count, count - steps))
@@ -399,10 +766,6 @@
     centred = v - mean
     var = jnp.mean(centred * centred, axis=-1, keepdims=True)
     return centred * lax.rsqrt(var + EPS) * gain + shift
-
-
-def gelu_tanh(v):
-    return jax.nn.gelu(v, approximate=True)
 
 
 def row_info(seq_lengths, active_until, first, count):
@@ -472,43 +835,16 @@
 
     zero_q = jnp.zeros((rows, heads, HD), jnp.float32)
     combined = attended_t.T.reshape(rows, heads, HD)
-    attn = attn_sum.astype(jnp.float32) + b_outs[0]
-    hidden_state = input_full + gate * attn
-    norm2, ln2_pull = jax.vjp(layer_norm, hidden_state, ln_gains[1], ln_shifts[1])
-    norm2_low = norm2.astype(jnp.bfloat16)
-    pre = jnp.dot(norm2_low, w_up, preferred_element_type=jnp.float32) + b_up
-    act, gelu_pull = jax.vjp(gelu_tanh, pre)
-    act_low = act.astype(jnp.bfloat16)
-    ffn = (
-        lax.psum(
-            jnp.dot(act_low, w_down, preferred_element_type=jnp.float32).astype(jnp.bfloat16), "tp"
-        ).astype(jnp.float32)
-        + b_outs[1]
+    (norm2_low, g_pre, ffn_low, g_hidden, g_attn, sums2, down_part) = ffn(
+        attn_sum, layer_input, d_out, seq_lengths, active_until, ln_gains, ln_shifts, b_outs, b_up[None], w_up, w_down
     )
-    out = hidden_state + gate * ffn
-    grad_out = d_out.astype(jnp.float32)
-    g_ffn = (gate * grad_out).astype(jnp.bfloat16)
-    g_act = jnp.einsum("td,fd->tf", g_ffn, w_down, preferred_element_type=jnp.float32)
-    g_pre = gelu_pull(g_act)[0].astype(jnp.bfloat16)
-    down_term = jnp.einsum("tf,td->fd", act_low, g_ffn, preferred_element_type=jnp.float32)
+    hidden_state = input_full + gate * (attn_sum.astype(jnp.float32) + b_outs[0])
+    out = hidden_state + gate * (lax.psum(ffn_low, "tp").astype(jnp.float32) + b_outs[1])
     up_term = jnp.einsum("td,tf->df", norm2_low, g_pre, preferred_element_type=jnp.float32)
-    bup_term = jnp.sum(g_pre.astype(jnp.float32), axis=0)
-    g_norm2 = lax.psum(
-        jnp.einsum("tf,df->td", g_pre, w_up, preferred_element_type=jnp.float32).astype(
-            jnp.bfloat16
-        ),
-        "tp",
-    ).astype(jnp.float32)
-    from_norm2, gain2_term, shift2_term = ln2_pull(g_norm2)
-    g_hidden = grad_out + from_norm2
-    g_attn = (gate * g_hidden).astype(jnp.bfloat16)
     g_attended = jnp.einsum("td,ed->te", g_attn, w_out, preferred_element_type=jnp.float32).astype(
         jnp.bfloat16
     )
     out_term = jnp.einsum("te,td->ed", attended_low, g_attn, preferred_element_type=jnp.float32)
-    bouts_term = jnp.stack(
-        [jnp.sum(g_attn.astype(jnp.float32), axis=0), jnp.sum(g_ffn.astype(jnp.float32), axis=0)]
-    )
     g_att_h = g_attended.reshape(rows, heads, HD)
     delta = jnp.einsum("qhd,qhd->hq", g_att_h.astype(jnp.float32), combined)
     zero_kv = jnp.zeros((rows, 2 * width), jnp.float32)
@@ -574,7 +910,7 @@
     ).astype(jnp.float32)
     from_norm1, gain1_term, shift1_term = ln1_pull(g_norm1)
     g_x = g_hidden + from_norm1
-    g_qkv, g_out, g_up, g_down = (
+    g_qkv, g_out, g_up = (
         lax.psum_scatter(
             query_key_value_term.astype(jnp.bfloat16), "cp", scatter_dimension=0, tiled=True
         ).astype(jnp.float32),
@@ -584,21 +920,16 @@
         lax.psum_scatter(
             up_term.astype(jnp.bfloat16), "cp", scatter_dimension=0, tiled=True
         ).astype(jnp.float32),
-        lax.psum_scatter(
-            down_term.astype(jnp.bfloat16), "cp", scatter_dimension=1, tiled=True
-        ).astype(jnp.float32),
     )
-    g_ln_gains, g_ln_shifts, g_bqv, g_bup, g_bouts = (
-        lax.psum(jnp.stack([gain1_term, gain2_term]).astype(jnp.bfloat16), "cp").astype(
-            jnp.float32
-        ),
-        lax.psum(jnp.stack([shift1_term, shift2_term]).astype(jnp.bfloat16), "cp").astype(
-            jnp.float32
-        ),
-        lax.psum(bqv_term.astype(jnp.bfloat16), "cp").astype(jnp.float32),
-        lax.psum(bup_term.astype(jnp.bfloat16), "cp").astype(jnp.float32),
-        lax.psum(bouts_term.astype(jnp.bfloat16), "cp").astype(jnp.float32),
+    g_down = down_part
+    small = lax.psum(
+        (sums2, gain1_term, shift1_term, bqv_term), "cp",
     )
+    sums2, gain1, shift1, g_bqv = small
+    g_ln_gains = jnp.stack([gain1, sums2[0]])
+    g_ln_shifts = jnp.stack([shift1, sums2[1]])
+    g_bouts = sums2[2:4]
+    g_bup = sums2[4]
     return (out, g_x, g_ln_gains, g_ln_shifts, g_qkv, g_bqv, g_out, g_bouts, g_up, g_bup, g_down)
 
 

time: 765 us -> 636 us (0.83)
  waiting for transfers between devices: 440 us -> 269 us
  Pallas kernels: 92.1 us -> 206 us
  matrix products: 90.3 us -> 41.4 us
  other arithmetic: 63.5 us -> 39.3 us
  loops' own time: 0.46 us -> 8.97 us
    pallas_call x0 -> x1, Pallas kernels: none -> 114 us  [ffn(): pl.pallas_call(ffn_kernel, out_shape=(shape((rows, depth), BF16), shape((...]
    psum x2, waiting for transfers between devices: 256 us -> 159 us  [the longest x1 159 us: shards(): lax.psum(ffn_low, 'tp').astype(jnp.float32) + b_outs[1]]
    reduce_scatter x1 -> x0, waiting for transfers between devices: 72.1 us -> none  [shards(): lax.psum_scatter(down_term.astype(jnp.bfloat16), 'cp', scatter_dimension=...]
    dot_general x5 -> x0, matrix products: 47.9 us -> none  [the longest x1 11.6 us: shards(): jnp.einsum('td,fd->tf', g_ffn, w_down, preferred_element_type=jnp.float32)]
    reduce_sum x4 -> x1, other arithmetic: 11.5 us -> 2.2 us  [layer_norm(): return centred * lax.rsqrt(var + EPS) * gain + shift]
    another operation x4, loops' own time: 0.16 us -> 8.82 us  [grad_terms(): return lax.cond(key_start >= 0, grad_work, no_terms, 0)]
  transfers between devices with their start and end apart: 9 -> 8, of which waited for: 8 -> 6; matrix products, arithmetic and copies ran while one was open for 16% -> 15% of each run, Pallas kernels for 0% -> 0%
where the time goes in v2:
time: 636 us; the launch traced here: 629 us
  waiting for transfers between devices  269 us (42%)
  Pallas kernels  206 us (32%)
  matrix products  41.4 us (7%)
  other arithmetic  39.3 us (6%)
  blocking collectives  24.7 us (4%)
  local copies, waits for them, and re-layouts  21.3 us (3%)
  between operations  14.2 us (2%)
  loops' own time  8.97 us (1%)
    psum x1, waiting for transfers between devices, shards(): lax.psum(ffn_low, 'tp').astype(jnp.float32) + b_outs[1]  159 us
    pallas_call x1, Pallas kernels, ffn(): pl.pallas_call(ffn_kernel, out_shape=(shape((rows, depth), BF16), shape((...  114 us
    pallas_call x1, Pallas kernels, attend(): pl.pallas_call(attend_kernel, out_shape=(shape((rows, depth), BF16), shap...  92.1 us
    reduce_scatter x1, waiting for transfers between devices, shards(): lax.psum_scatter(up_term.astype(jnp.bfloat16), 'cp', scatter_dimension=0,...  72.1 us
    reduce_scatter x1, waiting for transfers between devices, shards(): lax.psum_scatter(query_key_value_term.astype(jnp.bfloat16), 'cp', scatter...  25.7 us
    psum x1, blocking collectives, shards(): small = lax.psum((sums2, gain1_term, shift1_term, bqv_term), 'cp')  24.7 us
    add x6, other arithmetic, return_step(): return (g_q_acc + term_q, kv_acc + term_kv)  14.8 us
  transfers between devices with their start and end apart: 8, of which 6 were waited for; matrix products, arithmetic and copies ran while one was open for 15% of the time, Pallas kernels for 0%

profile of v2, /device:TPU:0, one launch (start us, length us, event | category | flops | bytes accessed | tf_op | source)
XLA Modules:
  0.0 629.4 jit_solution(16297445024753172217)
XLA Ops:
  7.2 92.1 %attend.1 = (bf16[512,2048]{1,0:T(8,128)(2,1)}, bf16[512,2048]{1,0:T(8,128)(2,1)}, bf16[512,512]{1,0:T(8,128)(2,1)}, bf16[2048,1024]{1,0:T(8,128)(2,1)}, bf16[51...) custom-call(bf16[512,2048]{1,0:T(8,128)(2,1)} %x_hbm.3, s32[3]{0:T(128)} %lengths_ref.3, s32[3]{0:T(128)} %until_ref.3, ...), custom_call_target="tpu_custom_call" | custom-call | tf_op jit(solution)/shard_map/attend/pallas_call | solution.py:355
  99.3 114.4 %ffn.1 = (bf16[512,2048]{1,0:T(8,128)(2,1)}, bf16[512,2048]{1,0:T(8,128)(2,1)}, bf16[512,2048]{1,0:T(8,128)(2,1)}, f32[512,2048]{1,0:T(8,128)}, bf16[512,2048]{1...) custom-call(bf16[512,2048]{1,0:T(8,128)(2,1)} %get-tuple-element.307.sum_hbm, bf16[512,2048]{1,0:T(8,128)(2,1)} %x_hbm.3, ...), custom_call_target="tpu_custom_call" | custom-call | tf_op jit(solution)/shard_map/ffn/pallas_call | solution.py:721
  213.8 4.2 convolution_convert_fusion.2
  218.3 1.0 copy.55
  219.3 6.6 %copy.57 = bf16[2048,1024]{0,1:T(8,128)(2,1)} copy(bf16[2048,1024]{1,0:T(8,128)(2,1)} %get-tuple-element.445) | data formatting | bytes 8388608
  226.6 3.1 fusion.37
  229.7 10.8 %conditional.2 = (f32[512,8,64]{0,2,1:T(8,128)}, bf16[512,1024]{0,1:T(8,128)(2,1)}) conditional(s32[]{:T(128)} %convert_element_type.107, () %tuple.38, (s32[]{:T(128)}, bf16[2048,1024]{1,0:T(8,128)(2,1)}, s32[]{:T(128)}, s32[512]{0:T(512)S(1)}, s32[3]{0:T(128)S(1)}, /*index=5*/s32[512]{0:T(512)S(1)}, bf16[512,8,64]{0,2,1:T(8,128)(2,1)}, ...), branch_computations={%region_5.6_spmd, %region_6.0_spmd} | conditional | flops 1371284480 | bytes 56956120 | solution.py:880
  229.8 1.1 broadcast_in_dim.140
  230.9 1.0 broadcast_in_dim.141
  240.5 45.8 %while.17 = (s32[]{:T(128)}, f32[512,8,64]{0,2,1:T(8,128)}, bf16[512,1024]{0,1:T(8,128)(2,1)}, s32[]{:T(128)}, s32[]{:T(128)}, /*index=5*/bf16[2048,1024]{0,1:T(...) while((s32[]{:T(128)}, f32[512,8,64]{0,2,1:T(8,128)}, ...), condition=%wide.region_14.15_spmd.clone.clone, body=%wide.region_9.14_spmd.clone.clone.sunk | while | flops 1371284992 | bytes 71642800 | solution.py:891
  240.6 1.3 collective-permute-start
  242.3 2.4 add.262
  244.7 0.7 collective-permute-done
  245.5 2.5 convert_add_fusion.3
  248.0 1.3 collective-permute-start
  249.7 2.4 add.262
  252.1 10.8 %collective-permute-done = bf16[512,1024]{0,1:T(8,128)(2,1)} collective-permute-done((bf16[512,1024]{0,1:T(8,128)(2,1)}, bf16[512,1024]{0,1:T(8,128)(2,1)}, u32[]{:S(2)}, u32[]{:S(2)}) %collective-permute-start) | collective-permute-done | bytes 1048608 | tf_op jit(solution)/shard_map/while/body/eval_jaxpr/ppermute | solution.py:761
  263.0 2.5 convert_add_fusion.3
  265.5 1.3 collective-permute-start
  266.9 13.8 %conditional.6 = (f32[512,8,64]{0,2,1:T(8,128)S(1)}, f32[512,1024]{0,1:T(8,128)S(1)}) conditional(s32[]{:T(128)} %convert_element_type.192, () %tuple.85, (s32[]{:T(128)}, s32[]{:T(128)}, bf16[2048,1024]{0,1:T(8,128)(2,1)}, s32[]{:T(128)}, s32[]{:T(128)}, /*index=5*/s32[3]{0:T(128)S(1)}, s32[512]{0:T(512)S(1)}, bf16[512,8,64]{0,2,1:T(8,128)(2,1)}, ...), branch_computations={%region_10.10_spmd, %region_11.13_spmd} | conditional | flops 1369449984 | bytes 55911716 | solution.py:880
  266.9 1.5 fusion.43
  268.4 2.3 fusion.47
  271.3 3.4 fusion.14
  274.7 0.8 fusion.22
  275.7 2.3 fusion.19
  278.0 2.4 convolution_multiply_fusion.2
  280.6 2.4 add.262
  283.1 0.7 collective-permute-done
  283.8 2.5 convert_add_fusion.3
  286.4 1.5 copy.58
  287.8 1.4 convert_reduce_fusion.3
  289.5 7.4 %bitcast_convert_fusion = bf16[512,2048]{1,0:T(8,128)(2,1)} fusion(bf16[2048,3,512]{2,0,1:T(8,128)(2,1)} %param.24, bf16[512,1,512]{2,0,1:T(8,128)(2,1)S(1)} %get-tuple-element.503, bf16[512,1,512]{2,0,1:T(8,128)(2,1)S(1)} %get-tuple-element.502, bf16[512,1,512]{2,0,1:T(8,128)(2,1)S(1)} %copy.59), kind=kOutput, calls=%fused_computation.71 | convolution fusion | flops 3223846912 | bytes 9961472 | tf_op jit(solution)/shard_map/wzb,gzb->wg/dot_general | solution.py:903
  297.0 7.0 %convolution_convert_fusion.1 = bf16[2048,3,512]{2,0,1:T(8,128)(2,1)} fusion(bf16[512,2048]{1,0:T(8,128)(2,1)} %get-tuple-element.320, bf16[512,1,512]{2,0,1:T(8,128)(2,1)S(1)} %get-tuple-element.503, bf16[512,1,512]{2,0,1:T(8,128)(2,1)S(1)} %get-tuple-element.502, bf16[512,1,512]{2,0,1:T(8,128)(2,1)S(1)} %copy.59), kind=kOutput, calls=%fused_computation.66 | convolution fusion | flops 3229089792 | bytes 9961472 | tf_op jit(solution)/shard_map/hm,hwz->mwz/dot_general | solution.py:896
  304.3 1.5 copy-done.11
  305.8 8.3 %convolution_convert_fusion = bf16[2048,2048]{1,0:T(8,128)(2,1)} fusion(bf16[512,2048]{1,0:T(8,128)(2,1)S(1)} %copy-done.11, bf16[512,2048]{1,0:T(8,128)(2,1)} %get-tuple-element.323), kind=kOutput, calls=%fused_computation.53 | convolution fusion | flops 4299161600 | bytes 12582912 | tf_op jit(solution)/shard_map/td,tf->df/dot_general | solution.py:843
  316.2 1.5 slice.54
  317.6 1.6 fusion.44
  319.2 1.8 convert_element_type.118
  321.0 158.6 %all-reduce.7.cloned.1.call-done = (bf16[512,2048]{1,0:T(8,128)(2,1)}, bf16[512,2048]{1,0:T(8,128)(2,1)}) async-done(((bf16[512,2048]{1,0:T(8,128)(2,1)}, bf16[512,2048]{1,0:T(8,128)(2,1)}), (bf16[512,2048]{1,0:T(8,128)(2,1)}, bf16[512,2048]{1,0:T(8,128)(2,1)})) %all-reduce.7.cloned.1.call-update) | async-done | bytes 4194320 | tf_op jit(solution)/shard_map/psum | solution.py:842
  479.6 3.3 fusion.31
  482.9 2.2 fusion.34
  485.1 24.7 %all-reduce = (f32[1,2048]{1,0:T(1,128)S(1)}, f32[1,2048]{1,0:T(1,128)S(1)}, f32[2,512]{1,0:T(2,128)}) all-reduce(f32[1,2048]{1,0:T(1,128)S(1)} %bitcast.125, f32[1,2048]{1,0:T(1,128)S(1)} %bitcast.124, f32[2,512]{1,0:T(2,128)S(1)} %pad_maximum_fusion.7), channel_id=1, replica_groups=mesh['cp'=8,'tp'=4] {'cp'}, use_global_device_ids=true, to_apply=%region_21.22 | all-reduce | flops 5120 | bytes 40960 | tf_op jit(solution)/shard_map/psum | solution.py:925
  510.5 7.9 %add_add_fusion.1 = (f32[512,2048]{1,0:T(8,128)}, f32[512,2048]{1,0:T(8,128)}) fusion(f32[512,2048]{1,0:T(8,128)} %get-tuple-element.309, bf16[512,2048]{1,0:T(8,128)(2,1)S(1)} %copy-done, bf16[512,2048]{1,0:T(8,128)(2,1)} %get-tuple-element.491, f32[512]{0:T(512)S(1)} %negate_multiply_fusion, f32[512]{0:T(512)S(1)} %get-tuple-element.509, ...), kind=kLoop, calls=%fused_computation.72 | loop fusion | flops 18874368 | bytes 21006336 | tf_op jit(solution)/shard_map/add | solution.py:912
  518.3 25.7 %reduce-scatter.4.cloned.1.call-done = bf16[256,3,512]{2,0,1:T(8,128)(2,1)} async-done(((bf16[2048,3,512]{2,0,1:T(8,128)(2,1)}), bf16[256,3,512]{2,0,1:T(8,128)(2,1)}) %reduce-scatter.4.cloned.1.call-update) | async-done | bytes 786448 | tf_op jit(solution)/shard_map/reduce_scatter | solution.py:914
  544.0 2.5 convert_element_type.114
  546.5 72.1 %reduce-scatter.8.cloned.1.call-done = bf16[256,2048]{1,0:T(8,128)(2,1)} async-done(((bf16[2048,2048]{1,0:T(8,128)(2,1)}), bf16[256,2048]{1,0:T(8,128)(2,1)}) %reduce-scatter.8.cloned.1.call-update) | async-done | bytes 1048592 | tf_op jit(solution)/shard_map/reduce_scatter | solution.py:920
  618.6 2.8 convert_element_type.120
  621.4 1.3 copy.97
  (90 shorter events, 6.8 us)
Async XLA Ops:
  7.2 309.0 %all-reduce.5.cloned.1.call-start = ((), (), s32[]{:S(2)}) async-start(), calls=%async_computation.3 | async-start | bytes 131072 | tf_op jit(solution)/shard_map/psum | solution.py:925
  7.2 92.1 %copy-start.10 = (s32[3]{0:T(128)S(1)}, s32[3]{0:T(128)}, u32[]{:S(2)}) copy-start(s32[3]{0:T(128)} %lengths_ref.3) | copy-start | bytes 40
  99.3 114.5 %copy-start.12 = (bf16[512,512]{1,0:T(8,128)(2,1)S(1)}, bf16[512,512]{1,0:T(8,128)(2,1)}, u32[]{:S(2)}) copy-start(bf16[512,512]{1,0:T(8,128)(2,1)} %get-tuple-element.321) | copy-start | bytes 1572868
  213.7 4.6 copy-start.4
  213.8 105.4 %reduce-scatter.6.cloned.1.call-start = ((), (), s32[]{:S(2)}) async-start(), calls=%async_computation.5 | async-start | bytes 2359296 | tf_op jit(solution)/shard_map/reduce_scatter | solution.py:917
  218.1 261.5 %all-reduce.7.cloned.1.call-start = ((), (), s32[]{:S(2)}) async-start(), calls=%async_computation.7 | async-start | bytes 8388608 | tf_op jit(solution)/shard_map/psum | solution.py:842
  219.3 6.6 %copy-start.9 = (s32[3]{0:T(128)S(1)}, s32[3]{0:T(128)}, u32[]{:S(2)}) copy-start(s32[3]{0:T(128)} %until_ref.3) | copy-start | bytes 40
  219.3 7.3 %copy-start.2 = (bf16[512,2048]{1,0:T(8,128)(2,1)S(1)}, bf16[512,2048]{1,0:T(8,128)(2,1)}, u32[]{:S(2)}) copy-start(bf16[512,2048]{1,0:T(8,128)(2,1)} %wout_hbm.1) | copy-start | bytes 6291460
  240.5 1.3 copy-start.13
  240.6 4.9 collective-permute-start
  244.7 3.3 copy-start.14
  248.0 1.3 copy-start.13
  248.0 15.0 %collective-permute-start = (bf16[512,1024]{0,1:T(8,128)(2,1)}, bf16[512,1024]{0,1:T(8,128)(2,1)}, u32[]{:S(2)}, u32[]{:S(2)}) collective-permute-start(bf16[512,1024]{0,1:T(8,128)(2,1)} %get-tuple-element.618), channel_id=1, source_target_pairs={{4,0},{8,4},{12,8},{16,12},{20,16},{24,20},{28,24},{5,1},{9,5},{13... | collective-permute-start | bytes 3145736 | tf_op jit(solution)/shard_map/while/body/eval_jaxpr/ppermute | solution.py:761
  252.1 13.4 %copy-start.14 = (bf16[512,8,64]{0,2,1:T(8,128)(2,1)S(1)}, bf16[512,8,64]{0,2,1:T(8,128)(2,1)}, u32[]{:S(2)}) copy-start(bf16[512,8,64]{0,2,1:T(8,128)(2,1)} %copy-done.13) | copy-start | bytes 1572868 | tf_op jit(solution)/shard_map/while
  265.5 1.3 copy-start.13
  265.5 18.3 %collective-permute-start = (bf16[512,1024]{0,1:T(8,128)(2,1)}, bf16[512,1024]{0,1:T(8,128)(2,1)}, u32[]{:S(2)}, u32[]{:S(2)}) collective-permute-start(bf16[512,1024]{0,1:T(8,128)(2,1)} %get-tuple-element.618), channel_id=1, source_target_pairs={{4,0},{8,4},{12,8},{16,12},{20,16},{24,20},{28,24},{5,1},{9,5},{13... | collective-permute-start | bytes 3145736 | tf_op jit(solution)/shard_map/while/body/eval_jaxpr/ppermute | solution.py:761
  266.9 4.4 copy-start.15
  274.7 1.1 copy-start.16
  283.1 3.3 copy-start.14
  297.0 247.0 %reduce-scatter.4.cloned.1.call-start = ((), (), s32[]{:S(2)}) async-start(), calls=%async_computation.4 | async-start | bytes 7077888 | tf_op jit(solution)/shard_map/reduce_scatter | solution.py:914
  304.0 1.7 copy-start.11
  304.1 314.5 %reduce-scatter.8.cloned.1.call-start = ((), (), s32[]{:S(2)}) async-start(), calls=%async_computation.6 | async-start | bytes 9437184 | tf_op jit(solution)/shard_map/reduce_scatter | solution.py:920
  314.1 0.7 copy-start.5
  314.1 1.6 copy-start
  314.1 2.0 copy-start.7
  314.1 2.0 copy-start.8
  314.1 2.0 copy-start.6
  479.6 3.3 copy-start.1
  518.3 103.0 %copy-start.3 = (f32[2048,256]{1,0:T(8,128)S(1)}, f32[2048,256]{1,0:T(8,128)}, u32[]{:S(2)}) copy-start(f32[2048,256]{1,0:T(8,128)} %get-tuple-element.669) | copy-start | bytes 6291460
Sparse Core Ops, SparseCore 0:
  213.9 49.8 all-reduce.4
  268.0 43.2 reduce-scatter.5
  314.3 165.2 all-reduce.6
  483.2 60.7 reduce-scatter.3
  547.3 71.2 reduce-scatter.7

commit v3 on v2

--- a/solution.py
+++ b/solution.py
@@ -755,41 +755,504 @@
     )(attn_sum, x, d_out, lengths, until, gains, shifts, b_outs, b_up, w_up, w_down)
 
 
-def passed_along(value, axis, steps):
-    count = lax.axis_size(axis)
-    first, last = (max(0, -steps), min(count, count - steps))
-    return lax.ppermute(value, axis, [(source, source + steps) for source in range(first, last)])
-
-
-def layer_norm(v, gain, shift):
-    mean = jnp.mean(v, axis=-1, keepdims=True)
-    centred = v - mean
-    var = jnp.mean(centred * centred, axis=-1, keepdims=True)
-    return centred * lax.rsqrt(var + EPS) * gain + shift
-
-
-def row_info(seq_lengths, active_until, first, count):
-    index = jnp.arange(seq_lengths.shape[0])
-    ends = jnp.sum(jnp.where(index[None, :] <= index[:, None], seq_lengths[None, :], 0), axis=1)
-    starts = ends - seq_lengths
-    rows = first + jnp.arange(count)
-    inside = (rows[:, None] >= starts[None, :]) & (rows[:, None] < ends[None, :])
-    numbers = jnp.arange(seq_lengths.shape[0])
-    segment = jnp.sum(jnp.where(inside, numbers[None, :] + 1, 0), axis=1) - 1
-    position = rows - jnp.sum(jnp.where(inside, starts[None, :], 0), axis=1)
-    limit = jnp.sum(jnp.where(inside, active_until[None, :], 0), axis=1)
-    active = (position < limit).astype(jnp.float32)
-    return (rows, segment, active)
-
-
-def block_scores(query_h, key_h, query_rows, query_seg, key_rows, key_seg, scale):
-    scores = jnp.einsum("qhd,khd->hqk", query_h, key_h, preferred_element_type=jnp.float32) * scale
-    allowed = (
-        (key_rows[None, :] <= query_rows[:, None])
-        & (key_seg[None, :] == query_seg[:, None])
-        & (key_seg[None, :] >= 0)
-    )
-    return (jnp.where(allowed[None], scores, NEG), allowed)
+SPLIT_UP = 1024
+SPLIT_LAST = 1024
+
+
+def grad_attend_kernel(
+    g_attn_hbm, wout_hbm, q_hbm, kv_hbm, att_t_hbm, lse, lengths_ref, until_ref, ffn_hbm, norm_hbm, g_pre_hbm,
+    g_qkv_hbm, ffn_sum_hbm, up_out,
+    g_attn_v, wout_v, q_v, kv, k_t, att_t, q_t, g_v, g_t, delta, acc, g_qkv_v,
+    give_near, got_near, give_before, got_after, give_own, got_own, kv_send, kv_recv,
+    norm_v, g_pre_v, terms, near, far, rs_send, rs_recv,
+    part, slot_a, slot_b, total, ar_send, ar_recv, load_sem, store_sem,
+):
+    cp, tp, core, chip = place()
+    bands = lax.axis_size("cp")
+    chips = bands // 2
+    rows, width = q_v.shape
+    heads = width // HD
+    count = rows // SUB
+    sibling = (cp + 1 - 2 * core, tp)
+    after = (lax.rem(cp + 2, bands), tp)
+    before = (lax.rem(cp + bands - 2, bands), tp)
+    loads = [
+        pltpu.make_async_copy(source, target, load_sem.at[i])
+        for i, (source, target) in enumerate(
+            (
+                (norm_hbm, norm_v),
+                (g_pre_hbm, g_pre_v),
+                (ffn_hbm, part),
+                (g_attn_hbm, g_attn_v),
+                (wout_hbm, wout_v),
+                (q_hbm, q_v),
+                (kv_hbm, kv),
+                (att_t_hbm, att_t),
+            )
+        )
+    ]
+    for item in loads:
+        item.start()
+    line = LineSum(part, slot_a, slot_b, total, ar_send, ar_recv)
+    scatter = Scatter(terms, near, far, rs_send, rs_recv, SPLIT_UP)
+    greet(cp, tp, [*scatter.partners(), after, before])
+    begin, _ = band_info(lengths_ref, until_ref, cp * rows)
+    bias = jnp.where(begin < chip * 2 * rows, 0.0, NEG)
+    loads[0].wait()
+    loads[1].wait()
+    loads[2].wait()
+    loop(count, line.push)
+    blocks, half = scatter.blocks(), scatter.count // 2
+
+    def term(k):
+        scatter.fill(k, lambda tile, at: (norm_v[:, at], g_pre_v[:, tile * 512 : (tile + 1) * 512]))
+
+    loop(blocks // 2, term)
+    if scatter.block == scatter.chunk:
+        loop(half, scatter.send_near)
+    loop(blocks - blocks // 2, lambda k: term(blocks // 2 + k))
+    if scatter.block != scatter.chunk:
+        loop(half, scatter.send_near)
+
+    def relay(s):
+        @pl.when(s < count)
+        def _():
+            line.relay_in(s)
+
+        @pl.when(s > 0)
+        def _():
+            line.relay_out(s - 1)
+
+    loop(2, relay)
+    for item in loads[3:]:
+        item.wait()
+    scale = HD ** -0.5
+
+    @functools.partial(loop, rows // CHUNK)
+    def _(i):
+        at = rows_of(i, CHUNK)
+        low = dot_nt(g_attn_v[at], wout_v[...]).astype(BF16)
+        g_v[at] = low
+        turned = low.astype(F32).T
+        turned_q = q_v[at].astype(F32).T * scale
+        upper = lax.broadcasted_iota(jnp.int32, (2 * HD, CHUNK), 0) < HD
+        for h in range(heads):
+            both = slice((h // 2) * 2 * HD, (h // 2 + 1) * 2 * HD)
+            mine = slice(h * HD, (h + 1) * HD)
+            g_t[h, :, at] = jnp.where(upper == (h % 2 == 0), turned[both], 0.0).astype(BF16)
+            q_t[h, :, at] = jnp.where(upper == (h % 2 == 0), turned_q[both], 0.0).astype(BF16)
+            delta[h : h + 1, at] = jnp.sum(turned[mine] * att_t[mine, at], axis=0, keepdims=True)
+
+    @functools.partial(loop, 4)
+    def _(i):
+        at = rows_of(i, rows)
+        k_t[:, at] = kv[at, :width].astype(F32).T.astype(BF16)
+
+    @functools.partial(loop, rows // 64)
+    def _(i):
+        att_t[rows_of(i, 64)] = jnp.zeros((64, rows), F32)
+
+    @functools.partial(loop, 4 * rows // 64)
+    def _(i):
+        acc[rows_of(i, 64)] = jnp.zeros((64, 2 * width), F32)
+
+    g_q_t = att_t
+    relay(2)
+
+    def head(h, bands_of):
+        offset = lax.div(h, 2) * 2 * HD
+        lanes = pl.ds(pl.multiple_of(offset, 2 * HD), 2 * HD)
+        lanes_v = pl.ds(pl.multiple_of(offset + width, 2 * HD), 2 * HD)
+        feature = pl.ds(pl.multiple_of(h * HD, HD), HD)
+        low_lanes = lax.broadcasted_iota(jnp.int32, (CHUNK, 2 * HD), 1) < HD
+        mine = low_lanes == (lax.rem(h, 2) == 0)
+        for c in range(rows // CHUNK):
+            cols = slice(c * CHUNK, (c + 1) * CHUNK)
+            q_n = jnp.where(mine, q_v[cols, lanes].astype(F32), 0.0).astype(BF16)
+            g_n = jnp.where(mine, g_v[cols, lanes].astype(F32), 0.0).astype(BF16)
+            lse_row = lse[pl.ds(h, 1), cols]
+            delta_row = delta[pl.ds(h, 1), cols]
+            for b in bands_of:
+                keys = slice(b * rows, (b + 1) * rows)
+                s = dot(kv[keys, lanes], q_t[h, :, cols])
+                if b < 2:
+                    s = s + (bias - lse_row)
+                else:
+                    key = lax.broadcasted_iota(jnp.int32, (rows, CHUNK), 0) + (b - 2) * rows
+                    row = lax.broadcasted_iota(jnp.int32, (rows, CHUNK), 1) + c * CHUNK
+                    s = jnp.where(key <= row + core * rows, s - lse_row, NEG)
+                p = jnp.exp(s)
+                g_s = (p * (dot(kv[keys, lanes_v], g_t[h, :, cols]) - delta_row)).astype(BF16)
+                acc[keys, lanes] += dot(g_s, q_n)
+                acc[keys, lanes_v] += dot(p.astype(BF16), g_n)
+                g_q_t[feature, cols] += dot(k_t[feature, keys], g_s)
+
+    @functools.partial(loop, heads)
+    def _(h):
+        head(h, (0, 1))
+
+        @pl.when(h == 0)
+        def _():
+            loop(half, scatter.add_near)
+            scatter.send_far(1)
+
+        @pl.when(lax.rem(h, 2) == 1)
+        def _():
+            relay(3 + lax.div(h, 2))
+
+    def kv_copy(kind, source, target, device):
+        return pltpu.make_async_remote_copy(
+            src_ref=source, dst_ref=target, send_sem=kv_send.at[kind], recv_sem=kv_recv.at[kind],
+            device_id=device, device_id_type=MESH,
+        )
+
+    to_near = kv_copy(0, give_near, got_near, sibling)
+    to_before = kv_copy(1, give_before, got_after, before)
+    to_own = kv_copy(2, give_own, got_own, sibling)
+
+    def lower(target, slot):
+        @functools.partial(loop, rows // 64)
+        def _(i):
+            at = pl.ds(pl.multiple_of(slot * rows + i * 64, 64), 64)
+            target[rows_of(i, 64)] = acc[at].astype(BF16)
+
+    def add_to(slot, source):
+        @functools.partial(loop, rows // 64)
+        def _(i):
+            at = pl.ds(pl.multiple_of(slot * rows + i * 64, 64), 64)
+            acc[at] += source[rows_of(i, 64)].astype(F32)
+
+    lower(give_near, 1 - core)
+    to_near.start()
+    to_near.wait_recv()
+    add_to(core, got_near)
+    lower(give_before, core)
+
+    @pl.when(chip > 0)
+    def _():
+        to_before.start()
+
+    @functools.partial(loop, heads)
+    def _(h):
+        head(h, (2, 3))
+
+        @pl.when(lax.rem(h, 2) == 1)
+        def _():
+            relay(7 + lax.div(h, 2))
+
+    own = 2 + core
+    lower(give_own, 3 - core)
+    to_own.start()
+    loop(2, lambda i: relay(11 + i))
+    levels = scatter.depth
+    for level in range(1, levels):
+        scatter.add_far(level)
+        scatter.send_far(level + 1)
+    loop(4, lambda i: relay(13 + i))
+    to_own.wait_recv()
+    add_to(own, got_own)
+
+    @pl.when(chip < chips - 1)
+    def _():
+        to_before.wait_recv()
+        add_to(own, got_after)
+
+    @functools.partial(loop, rows // 64)
+    def _(i):
+        at = pl.ds(pl.multiple_of(own * rows + i * 64, 64), 64)
+        g_qkv_v[rows_of(i, 64), width : 2 * width] = (acc[at, :width] * scale).astype(BF16)
+        g_qkv_v[rows_of(i, 64), 2 * width :] = acc[at, width:].astype(BF16)
+
+    @functools.partial(loop, rows // CHUNK)
+    def _(i):
+        at = rows_of(i, CHUNK)
+        g_qkv_v[at, :width] = (g_q_t[:, at].T * scale).astype(BF16)
+
+    stores = [
+        pltpu.make_async_copy(g_qkv_v, g_qkv_hbm, store_sem.at[0]),
+        pltpu.make_async_copy(total, ffn_sum_hbm, store_sem.at[1]),
+    ]
+    stores[0].start()
+    loop(count, line.get)
+    stores[1].start()
+
+    def write(tile, value):
+        up_out[:, tile * 512 : (tile + 1) * 512] = value
+
+    scatter.finish(write)
+    scatter.drain()
+    line.drain_all(count)
+    to_near.wait_send()
+    to_own.wait_send()
+
+    @pl.when(chip > 0)
+    def _():
+        to_before.wait_send()
+
+    for item in stores:
+        item.wait()
+
+
+def grad_attend(g_attn, wout, q, kv, att_t, lse, lengths, until, ffn_low, norm2, g_pre):
+    rows, depth = g_attn.shape
+    width = q.shape[1]
+    heads = width // HD
+    hidden = g_pre.shape[1]
+    chunk = depth // lax.axis_size("cp")
+    shape = jax.ShapeDtypeStruct
+    return pl.pallas_call(
+        grad_attend_kernel,
+        out_shape=(
+            shape((rows, 3 * width), BF16),
+            shape((rows, depth), BF16),
+            shape((chunk, hidden), F32),
+        ),
+        in_specs=[ANY, ANY, ANY, ANY, ANY, IN_VMEM, IN_SMEM, IN_SMEM, ANY, ANY, ANY],
+        out_specs=(ANY, ANY, IN_VMEM),
+        scratch_shapes=[
+            pltpu.VMEM((rows, depth), BF16),
+            pltpu.VMEM((width, depth), BF16),
+            pltpu.VMEM((rows, width), BF16),
+            pltpu.VMEM((4 * rows, 2 * width), BF16),
+            pltpu.VMEM((width, 4 * rows), BF16),
+            pltpu.VMEM((width, rows), F32),
+            pltpu.VMEM((heads, 2 * HD, rows), BF16),
+            pltpu.VMEM((rows, width), BF16),
+            pltpu.VMEM((heads, 2 * HD, rows), BF16),
+            pltpu.VMEM((heads, rows), F32),
+            pltpu.VMEM((4 * rows, 2 * width), F32),
+            pltpu.VMEM((rows, 3 * width), BF16),
+            *[pltpu.VMEM((rows, 2 * width), BF16)] * 6,
+            pltpu.SemaphoreType.DMA((3,)),
+            pltpu.SemaphoreType.DMA((3,)),
+            pltpu.VMEM((rows, depth), BF16),
+            pltpu.VMEM((rows, hidden), BF16),
+            pltpu.VMEM((depth, hidden), BF16),
+            *scatter_scratch(depth, hidden, SPLIT_UP),
+            *line_scratch(rows, depth),
+            pltpu.SemaphoreType.DMA((8,)),
+            pltpu.SemaphoreType.DMA((2,)),
+        ],
+        compiler_params=pltpu.CompilerParams(collective_id=2, has_side_effects=True, vmem_limit_bytes=63 * 2**20),
+        name="grad_attend",
+    )(g_attn, wout, q, kv, att_t, lse, lengths, until, ffn_low, norm2, g_pre)
+
+
+def last_kernel(
+    g_qkv_hbm, wqkv_hbm, x_hbm, g_hidden_hbm, norm_hbm, g_attn_hbm, att_hbm, attn_sum_hbm, ffn_sum_hbm,
+    lengths_ref, until_ref, gains, b_outs, sums_in,
+    g_x_hbm, out_hbm, qkv_out, w_out_out, gains_out, shifts_out, bqv_out, bouts_out, bup_out,
+    g_qkv_v, w_v, x_v, g_hidden, norm_v, g_attn_v, att_v, attn_sum, ffn_sum, out_v, acc, small, small_got,
+    terms, near, far, rs_send, rs_recv,
+    part, slot_a, slot_b, total, ar_send, ar_recv, small_send, small_recv, load_sem, store_sem,
+):
+    cp, tp, core, chip = place()
+    rows, depth = x_v.shape
+    width = att_v.shape[1]
+    count = rows // SUB
+    loads = [
+        pltpu.make_async_copy(source, target, load_sem.at[i])
+        for i, (source, target) in enumerate(
+            (
+                (g_qkv_hbm, g_qkv_v),
+                (wqkv_hbm, w_v),
+                (norm_hbm, norm_v),
+                (g_attn_hbm, g_attn_v),
+                (att_hbm, att_v),
+                (x_hbm, x_v),
+                (g_hidden_hbm, g_hidden),
+                (attn_sum_hbm, attn_sum),
+                (ffn_sum_hbm, ffn_sum),
+            )
+        )
+    ]
+    for item in loads:
+        item.start()
+    line = LineSum(part, slot_a, slot_b, total, ar_send, ar_recv)
+    scatter = Scatter(terms, near, far, rs_send, rs_recv, SPLIT_LAST)
+    partners = scatter.partners()
+    greet(cp, tp, partners)
+    _, live = band_info(lengths_ref, until_ref, cp * rows)
+    acc[...] = jnp.zeros_like(acc)
+    loads[0].wait()
+    loads[1].wait()
+
+    for c in range(rows // CHUNK):
+        chunk = slice(c * CHUNK, (c + 1) * CHUNK)
+
+        @functools.partial(loop, depth // 512)
+        def _(t, chunk=chunk):
+            lanes = rows_of(t, 512)
+            value = dot_nt(g_qkv_v[chunk, :width], w_v[0, lanes])
+            value = value + dot_nt(g_qkv_v[chunk, width : 2 * width], w_v[1, lanes])
+            value = value + dot_nt(g_qkv_v[chunk, 2 * width :], w_v[2, lanes])
+            part[chunk, lanes] = value.astype(BF16)
+
+        loop(CHUNK // SUB, lambda s, c=c: line.push(s + c * (CHUNK // SUB)))
+
+    for item in loads[2:]:
+        item.wait()
+
+    def back(s):
+        line.get(s)
+        at = rows_of(s, SUB)
+        e = total[at].astype(F32)
+        v = x_v[at].astype(F32)
+        centred = v - jnp.mean(v, axis=-1, keepdims=True)
+        scale = lax.rsqrt(jnp.mean(centred * centred, axis=-1, keepdims=True) + EPS)
+        hat = centred * scale
+        t = e * gains[0:1]
+        along = t - jnp.mean(t, axis=-1, keepdims=True) - hat * jnp.mean(t * hat, axis=-1, keepdims=True)
+        g_hidden[at] = g_hidden[at] + along * scale
+        row = lax.broadcasted_iota(jnp.int32, (SUB, 1), 0) + s * SUB
+        branches = attn_sum[at].astype(F32) + b_outs[0:1] + (ffn_sum[at].astype(F32) + b_outs[1:2])
+        out_v[at] = v + jnp.where(row < live, branches, 0.0)
+        acc[0] += fold(e * hat)
+        acc[1] += fold(e)
+        pltpu.make_async_copy(g_hidden.at[at], g_x_hbm.at[at], store_sem.at[0, s]).start()
+        pltpu.make_async_copy(out_v.at[at], out_hbm.at[at], store_sem.at[1, s]).start()
+
+    behind = 2
+
+    def ahead(s):
+        @pl.when(s < count)
+        def _():
+            line.relay_in(s)
+
+        @pl.when(s > 0)
+        def _():
+            line.relay_out(s - 1)
+
+        @pl.when(s >= behind)
+        def _():
+            back(s - behind)
+
+    def term(k):
+        def pick(tile, at):
+            if tile < 3:
+                return norm_v[:, at], g_qkv_v[:, tile * width : (tile + 1) * width]
+            return g_attn_v[:, at], att_v[...]
+
+        scatter.fill(k, pick)
+
+    blocks, half = scatter.blocks(), scatter.count // 2
+
+    @functools.partial(loop, 4)
+    def _(i):
+        loop(blocks // 4, lambda j: term(i * (blocks // 4) + j))
+
+        @pl.when((i == 1) if scatter.block == scatter.chunk else (i == 3))
+        def _():
+            loop(half, scatter.send_near)
+
+        ahead(i)
+
+    @functools.partial(loop, 2)
+    def _(i):
+        loop(half // 2, lambda j: scatter.add_near(i * (half // 2) + j))
+        ahead(4 + i)
+
+    scatter.send_far(1)
+    for j in range(2):
+        bias = jnp.sum(g_qkv_v[:, 2 * j * width : (2 * j + 1) * width].astype(F32), axis=0, keepdims=True)
+        small[0, 7:8, j * width : (j + 1) * width] = bias
+    small[0, 7:8, 2 * width :] = jnp.zeros((1, depth - 2 * width), F32)
+    loop(8, lambda i: ahead(6 + i))
+    for level in range(1, scatter.depth):
+        scatter.add_far(level)
+        scatter.send_far(level + 1)
+    loop(count - 13, lambda i: ahead(14 + i))
+    loop(behind - 1, lambda i: back(count + 1 - behind + i))
+
+    small[0, 0:5] = sums_in[0:5]
+    for k in range(2):
+        small[0, 5 + k : 6 + k] = jnp.sum(acc[k], axis=0, keepdims=True)
+    rounds = []
+    for level, other in enumerate(partners):
+        item = pltpu.make_async_remote_copy(
+            src_ref=small.at[level], dst_ref=small_got.at[level], send_sem=small_send.at[level],
+            recv_sem=small_recv.at[level], device_id=other, device_id_type=MESH,
+        )
+        item.start()
+        item.wait_recv()
+        rounds.append(item)
+        small[level + 1] = small[level] + small_got[level]
+    final = len(partners)
+    gains_out[0:1] = small[final, 5:6]
+    gains_out[1:2] = small[final, 0:1]
+    shifts_out[0:1] = small[final, 6:7]
+    shifts_out[1:2] = small[final, 1:2]
+    bouts_out[...] = small[final, 2:4]
+    bup_out[...] = small[final, 4:5]
+    for j in range(2):
+        bqv_out[j : j + 1] = small[final, 7:8, j * width : (j + 1) * width]
+
+    def write(tile, value):
+        if tile < 3:
+            qkv_out[tile] = value
+        else:
+            w_out_out[...] = value.T
+
+    scatter.finish(write)
+    scatter.drain()
+    line.drain_all(count)
+    for item in rounds:
+        item.wait_send()
+
+    @functools.partial(loop, count)
+    def _(s):
+        at = rows_of(s, SUB)
+        pltpu.make_async_copy(g_hidden.at[at], g_x_hbm.at[at], store_sem.at[0, s]).wait()
+        pltpu.make_async_copy(out_v.at[at], out_hbm.at[at], store_sem.at[1, s]).wait()
+
+
+def last(g_qkv, wqkv, x, g_hidden, norm1, g_attn, att, attn_sum, ffn_sum, lengths, until, gains, b_outs, sums):
+    rows, depth = x.shape
+    width = att.shape[1]
+    bands = lax.axis_size("cp")
+    chunk = depth // bands
+    rounds = bands.bit_length() - 1
+    shape = jax.ShapeDtypeStruct
+    return pl.pallas_call(
+        last_kernel,
+        out_shape=(
+            shape((rows, depth), F32),
+            shape((rows, depth), F32),
+            shape((3, chunk, width), F32),
+            shape((width, chunk), F32),
+            shape((2, depth), F32),
+            shape((2, depth), F32),
+            shape((2, width), F32),
+            shape((2, depth), F32),
+            shape((1, depth), F32),
+        ),
+        in_specs=[ANY] * 9 + [IN_SMEM] * 2 + [IN_VMEM] * 3,
+        out_specs=(ANY,) * 2 + (IN_VMEM,) * 7,
+        scratch_shapes=[
+            pltpu.VMEM((rows, 3 * width), BF16),
+            pltpu.VMEM((3, depth, width), BF16),
+            pltpu.VMEM((rows, depth), BF16),
+            pltpu.VMEM((rows, depth), F32),
+            pltpu.VMEM((rows, depth), BF16),
+            pltpu.VMEM((rows, depth), BF16),
+            pltpu.VMEM((rows, width), BF16),
+            pltpu.VMEM((rows, depth), BF16),
+            pltpu.VMEM((rows, depth), BF16),
+            pltpu.VMEM((rows, depth), F32),
+            pltpu.VMEM((2, 8, depth), F32),
+            pltpu.VMEM((rounds + 1, 8, depth), F32),
+            pltpu.VMEM((rounds, 8, depth), F32),
+            pltpu.VMEM((depth, depth), BF16),
+            *scatter_scratch(depth, depth, SPLIT_LAST),
+            *line_scratch(rows, depth),
+            pltpu.SemaphoreType.DMA((rounds,)),
+            pltpu.SemaphoreType.DMA((rounds,)),
+            pltpu.SemaphoreType.DMA((9,)),
+            pltpu.SemaphoreType.DMA((2, rows // SUB)),
+        ],
+        compiler_params=pltpu.CompilerParams(collective_id=3, has_side_effects=True, vmem_limit_bytes=62 * 2**20),
+        name="last",
+    )(g_qkv, wqkv, x, g_hidden, norm1, g_attn, att, attn_sum, ffn_sum, lengths, until, gains, b_outs, sums)
 
 
 def shards(
@@ -807,130 +1270,22 @@
     w_down,
     d_out,
 ):
-    rows = layer_input.shape[0]
-    width = query_key_value_weight.shape[2]
-    heads = width // HD
-    scale = HD ** (-0.5)
-    bands = lax.axis_size("cp")
-    total_rows = rows * bands
-    reach = min(LONG, total_rows // 2) // rows - 1
-    first = lax.axis_index("cp") * rows
-    my_rows, my_seg, active = row_info(seq_lengths, active_until, first, rows)
-    gate = active[:, None]
-    input_full = layer_input.astype(jnp.float32)
-    first_norm_output, ln1_pull = jax.vjp(layer_norm, input_full, ln_gains[0], ln_shifts[0])
-    (attn_sum, first_norm_lowered, q_b, kv_all, attended_low, attended_t, lse) = attend(
-        layer_input, seq_lengths, active_until, ln_gains, ln_shifts,
-        jnp.transpose(query_key_value_weight, (1, 0, 2)), b_qv, w_out,
+    wqkv = jnp.transpose(query_key_value_weight, (1, 0, 2))
+    attn_sum, norm1, q, kv, att, att_t, lse = attend(
+        layer_input, seq_lengths, active_until, ln_gains, ln_shifts, wqkv, b_qv, w_out
     )
-    q_h = q_b.reshape(rows, heads, HD)
-    core = lax.rem(lax.axis_index("cp"), 2)
-
-    def block_of(index):
-        block = lax.dynamic_slice_in_dim(kv_all, jnp.maximum(2 + core - index, 0) * rows, rows, 0)
-        return (
-            block[:, :width].reshape(rows, heads, HD),
-            block[:, width:].reshape(rows, heads, HD),
-        )
-
-    zero_q = jnp.zeros((rows, heads, HD), jnp.float32)
-    combined = attended_t.T.reshape(rows, heads, HD)
-    (norm2_low, g_pre, ffn_low, g_hidden, g_attn, sums2, down_part) = ffn(
+    norm2, g_pre, ffn_low, g_hidden, g_attn, sums, g_down = ffn(
         attn_sum, layer_input, d_out, seq_lengths, active_until, ln_gains, ln_shifts, b_outs, b_up[None], w_up, w_down
     )
-    hidden_state = input_full + gate * (attn_sum.astype(jnp.float32) + b_outs[0])
-    out = hidden_state + gate * (lax.psum(ffn_low, "tp").astype(jnp.float32) + b_outs[1])
-    up_term = jnp.einsum("td,tf->df", norm2_low, g_pre, preferred_element_type=jnp.float32)
-    g_attended = jnp.einsum("td,ed->te", g_attn, w_out, preferred_element_type=jnp.float32).astype(
-        jnp.bfloat16
+    g_qkv_rows, ffn_sum, g_up = grad_attend(
+        g_attn, w_out, q, kv, att_t, lse, seq_lengths, active_until, ffn_low, norm2, g_pre
     )
-    out_term = jnp.einsum("te,td->ed", attended_low, g_attn, preferred_element_type=jnp.float32)
-    g_att_h = g_attended.reshape(rows, heads, HD)
-    delta = jnp.einsum("qhd,qhd->hq", g_att_h.astype(jnp.float32), combined)
-    zero_kv = jnp.zeros((rows, 2 * width), jnp.float32)
-
-    def grad_terms(index):
-        key_start = first - index * rows
-
-        def grad_work(unused_arg):
-            keys3, vals3 = block_of(index)
-            key_rows, key_seg, unused = row_info(seq_lengths, active_until, key_start, rows)
-            masked, allowed = block_scores(q_h, keys3, my_rows, my_seg, key_rows, key_seg, scale)
-            probs = jnp.where(allowed[None], jnp.exp(masked - lse[:, :, None]), 0.0)
-            g_probs = jnp.einsum("qhd,khd->hqk", g_att_h, vals3, preferred_element_type=jnp.float32)
-            g_scores = (probs * (g_probs - delta[:, :, None])).astype(jnp.bfloat16)
-            g_q = (
-                jnp.einsum("hqk,khd->qhd", g_scores, keys3, preferred_element_type=jnp.float32)
-                * scale
-            )
-            probs_low = probs.astype(jnp.bfloat16)
-            g_k = (
-                jnp.einsum("hqk,qhd->khd", g_scores, q_h, preferred_element_type=jnp.float32)
-                * scale
-            )
-            g_v = jnp.einsum("hqk,qhd->khd", probs_low, g_att_h, preferred_element_type=jnp.float32)
-            return (
-                g_q,
-                jnp.concatenate([g_k.reshape(rows, width), g_v.reshape(rows, width)], axis=1),
-            )
-
-        def no_terms(unused_arg):
-            return (zero_q, zero_kv)
-
-        return lax.cond(key_start >= 0, grad_work, no_terms, 0)
-
-    last_q, last_kv = grad_terms(reach)
-
-    def return_step(step, state):
-        g_q_acc, kv_acc = state
-        index = reach - 1 - step
-        kv_acc = passed_along(kv_acc.astype(jnp.bfloat16), "cp", -1).astype(kv_acc.dtype)
-        term_q, term_kv = grad_terms(index)
-        return (g_q_acc + term_q, kv_acc + term_kv)
-
-    g_q_sum, kv_sum = lax.fori_loop(0, reach, return_step, (last_q, last_kv))
-    g_q_b = g_q_sum.reshape(rows, width).astype(jnp.bfloat16)
-    g_k_b = kv_sum[:, :width].astype(jnp.bfloat16)
-    g_v_b = kv_sum[:, width:].astype(jnp.bfloat16)
-    projection_gradient = jnp.stack([g_q_b, g_k_b, g_v_b], axis=1)
-    query_key_value_term = jnp.einsum(
-        "hm,hwz->mwz", first_norm_lowered, projection_gradient, preferred_element_type=jnp.float32
+    g_x, out, g_qkv, g_out, g_ln_gains, g_ln_shifts, g_bqv, g_bouts, g_bup = last(
+        g_qkv_rows, wqkv, layer_input, g_hidden, norm1, g_attn, att, attn_sum, ffn_sum,
+        seq_lengths, active_until, ln_gains, b_outs, sums,
     )
-    bqv_term = jnp.stack(
-        [jnp.sum(g_q_b.astype(jnp.float32), axis=0), jnp.sum(g_v_b.astype(jnp.float32), axis=0)]
-    )
-    g_norm1 = lax.psum(
-        jnp.einsum(
-            "wzb,gzb->wg",
-            projection_gradient,
-            query_key_value_weight,
-            preferred_element_type=jnp.float32,
-        ).astype(jnp.bfloat16),
-        "tp",
-    ).astype(jnp.float32)
-    from_norm1, gain1_term, shift1_term = ln1_pull(g_norm1)
-    g_x = g_hidden + from_norm1
-    g_qkv, g_out, g_up = (
-        lax.psum_scatter(
-            query_key_value_term.astype(jnp.bfloat16), "cp", scatter_dimension=0, tiled=True
-        ).astype(jnp.float32),
-        lax.psum_scatter(
-            out_term.astype(jnp.bfloat16), "cp", scatter_dimension=1, tiled=True
-        ).astype(jnp.float32),
-        lax.psum_scatter(
-            up_term.astype(jnp.bfloat16), "cp", scatter_dimension=0, tiled=True
-        ).astype(jnp.float32),
-    )
-    g_down = down_part
-    small = lax.psum(
-        (sums2, gain1_term, shift1_term, bqv_term), "cp",
-    )
-    sums2, gain1, shift1, g_bqv = small
-    g_ln_gains = jnp.stack([gain1, sums2[0]])
-    g_ln_shifts = jnp.stack([shift1, sums2[1]])
-    g_bouts = sums2[2:4]
-    g_bup = sums2[4]
-    return (out, g_x, g_ln_gains, g_ln_shifts, g_qkv, g_bqv, g_out, g_bouts, g_up, g_bup, g_down)
+    g_qkv = jnp.transpose(g_qkv, (1, 0, 2))
+    return (out, g_x, g_ln_gains, g_ln_shifts, g_qkv, g_bqv, g_out, g_bouts, g_up, g_bup[0], g_down)
 
 
 def solution(mesh):

time: 636 us -> 373 us (0.59); the launches traced: 629 us -> 373 us
  waiting for transfers between devices: 269 us -> 0 us
  Pallas kernels: 206 us -> 357 us
  matrix products: 41.4 us -> 0 us
  other arithmetic: 39.3 us -> 0 us
  blocking collectives: 24.7 us -> 0 us
  between operations: 14.2 us -> 0.7 us
  loops' own time: 8.97 us -> 0 us
  local copies, waits for them, and re-layouts: 21.3 us -> 14.9 us
    psum x2 -> x0, waiting for transfers between devices: 159 us -> none  [the longest x1 159 us: shards(): lax.psum(ffn_low, 'tp').astype(jnp.float32) + b_outs[1]]
    pallas_call x0 -> x2, Pallas kernels: none -> 150 us  [the longest x1 75.7 us: last(): pl.pallas_call(last_kernel, out_shape=(shape((rows, depth), F32), shape((...]
    reduce_scatter x3 -> x0, waiting for transfers between devices: 97.7 us -> none  [the longest x1 72.1 us: shards(): lax.psum_scatter(up_term.astype(jnp.bfloat16), 'cp', scatter_dimension=0,...]
    dot_general x10 -> x0, matrix products: 41.4 us -> none  [the longest x1 8.34 us: shards(): jnp.einsum('td,tf->df', norm2_low, g_pre, preferred_element_type=jnp.floa...]
    psum x1 -> x0, blocking collectives: 24.7 us -> none  [shards(): small = lax.psum((sums2, gain1_term, shift1_term, bqv_term), 'cp')]
    add x11 -> x0, other arithmetic: 22.7 us -> none  [the longest x6 14.8 us: return_step(): return (g_q_acc + term_q, kv_acc + term_kv)]
    ppermute x3 -> x0, waiting for transfers between devices: 12.3 us -> none  [passed_along(): lax.ppermute(value, axis, [(source, source + steps) for source in range(f...]
    another operation x5 -> x0, loops' own time: 8.97 us -> none  [the longest x4 8.82 us: grad_terms(): return lax.cond(key_start >= 0, grad_work, no_terms, 0)]
  transfers between devices with their start and end apart: 8 -> 0, of which waited for: 6 -> 0; matrix products, arithmetic and copies ran while one was open for 15% -> 0% of each run, Pallas kernels for 0% -> 0%
where the time goes in v3:
time: 373 us
  Pallas kernels  357 us (96%)
  local copies, waits for them, and re-layouts  14.9 us (4%)
    pallas_call x1, Pallas kernels, ffn(): pl.pallas_call(ffn_kernel, out_shape=(shape((rows, depth), BF16), shape((...  114 us
    pallas_call x1, Pallas kernels, attend(): pl.pallas_call(attend_kernel, out_shape=(shape((rows, depth), BF16), shap...  92.7 us
    pallas_call x1, Pallas kernels, last(): pl.pallas_call(last_kernel, out_shape=(shape((rows, depth), F32), shape((...  75.7 us
    pallas_call x1, Pallas kernels, grad_attend(): pl.pallas_call(grad_attend_kernel, out_shape=(shape((rows, 3 * width), BF...  74.6 us
    unnamed x31, local copies, waits for them, and re-layouts  14.9 us

profile of v3, /device:TPU:0, one launch (start us, length us, event | category | flops | bytes accessed | tf_op | source)
XLA Modules:
  0.0 373.0 jit_solution(15310365217437004383)
XLA Ops:
  0.6 92.7 %attend.1 = (bf16[512,2048]{1,0:T(8,128)(2,1)}, bf16[512,2048]{1,0:T(8,128)(2,1)}, bf16[512,512]{1,0:T(8,128)(2,1)}, bf16[2048,1024]{1,0:T(8,128)(2,1)}, bf16[51...) custom-call(bf16[512,2048]{1,0:T(8,128)(2,1)} %x_hbm.5, s32[3]{0:T(128)} %lengths_ref.7, s32[3]{0:T(128)} %until_ref.7, ...), custom_call_target="tpu_custom_call" | custom-call | tf_op jit(solution)/shard_map/attend/pallas_call | solution.py:355
  93.3 114.4 %ffn.1 = (bf16[512,2048]{1,0:T(8,128)(2,1)}, bf16[512,2048]{1,0:T(8,128)(2,1)}, bf16[512,2048]{1,0:T(8,128)(2,1)}, f32[512,2048]{1,0:T(8,128)}, bf16[512,2048]{1...) custom-call(bf16[512,2048]{1,0:T(8,128)(2,1)} %get-tuple-element.37.sum_hbm.attn_sum_hbm, ...), custom_call_target="tpu_custom_call" | custom-call | tf_op jit(solution)/shard_map/ffn/pallas_call | solution.py:721
  207.7 74.6 %grad_attend.1 = (bf16[512,1536]{1,0:T(8,128)(2,1)}, bf16[512,2048]{1,0:T(8,128)(2,1)}, f32[256,2048]{1,0:T(8,128)}) custom-call(bf16[512,2048]{1,0:T(8,128)(2,1)} %get-tuple-element.38.g_attn_hbm, bf16[512,2048]{1,0:T(8,128)(2,1)} %wout_hbm.3, bf16[512,512]{1,0:T(8,128)(2,1)} %get-tuple-element.39.q_hbm, bf16[2048,1024]{1,0:T(8,128)(2,1)} %get-tuple-element.40.kv_hbm, ...), custom_call_target="tpu_custom_call" | custom-call | tf_op jit(solution)/shard_map/grad_attend/pallas_call | solution.py:1003
  282.3 75.7 %last.1 = (f32[512,2048]{1,0:T(8,128)}, f32[512,2048]{1,0:T(8,128)}, f32[3,256,512]{2,1,0:T(8,128)}, f32[512,256]{1,0:T(8,128)}, f32[2,2048]{1,0:T(2,128)}, /*in...) custom-call(bf16[512,1536]{1,0:T(8,128)(2,1)} %get-tuple-element.46.g_qkv_hbm, ...), custom_call_target="tpu_custom_call" | custom-call | tf_op jit(solution)/shard_map/last/pallas_call | solution.py:1216
  358.0 0.0 copy-start
  358.0 4.8 %copy.35 = f32[512,2048]{1,0:T(8,128)} copy(f32[512,2048]{1,0:T(8,128)} %get-tuple-element.74) | data formatting | bytes 8388608
  362.9 0.0 copy-done
  362.9 0.0 copy-start.7
  362.9 0.0 copy-start.6
  362.9 0.0 copy-start.3
  362.9 2.0 copy.36
  364.9 0.0 copy-done.7
  364.9 0.0 copy-start.9
  364.9 0.0 copy-start.4
  364.9 0.6 copy.37
  365.5 0.0 copy-done.6
  365.5 0.6 copy.38
  366.1 0.0 copy-done.3
  366.1 0.0 copy-start.5
  366.1 0.0 copy-start.2
  366.1 1.1 copy.39
  367.3 0.0 copy-done.9
  367.3 0.6 copy.40
  367.9 0.0 copy-done.4
  367.9 0.8 copy.41
  368.7 0.0 copy-done.5
  368.7 0.6 copy.42
  369.3 0.0 copy-done.2
  369.3 0.0 copy-start.8
  369.3 0.0 copy-start.1
  369.3 1.3 copy.43
  370.6 0.0 copy-done.8
  370.6 0.6 copy.44
  371.2 0.4 copy-done.1
  371.7 1.3 copy.45
Async XLA Ops:
  358.0 4.9 %copy-start = (f32[512,2048]{1,0:T(8,128)S(1)}, f32[512,2048]{1,0:T(8,128)}, u32[]{:S(2)}) copy-start(f32[512,2048]{1,0:T(8,128)} %get-tuple-element.75) | copy-start | bytes 12582916
  362.9 2.0 copy-start.7
  362.9 2.6 copy-start.6
  362.9 3.2 copy-start.3
  364.9 2.4 copy-start.9
  364.9 3.0 copy-start.4
  366.1 2.5 copy-start.5
  366.1 3.1 copy-start.2
  369.3 1.3 copy-start.8
  369.3 2.4 copy-start.1

commit v4 on v3

--- a/solution.py
+++ b/solution.py
@@ -67,6 +67,7 @@
         self.edge = (self.tp == 0) | (self.tp == 3)
         self.refs = (part, slot_a, slot_b, total)
         self.send, self.recv = send, recv
+        self.count = part.shape[0] // SUB
 
     def copy(self, kind, s):
         part, slot_a, slot_b, total = self.refs
@@ -122,20 +123,14 @@
             self.copy(1, s).wait_send()
             self.copy(2, s).wait_send()
 
-    def run(self, first, last):
-        def step(s, carry):
-            @pl.when(s < last)
-            def _():
-                self.relay_in(s)
-
-            @pl.when(s > first)
-            def _():
-                self.relay_out(s - 1)
-                self.get(s - 1)
-
-            return carry
-
-        lax.fori_loop(first, last + 1, step, 0)
+    def tick(self, s):
+        @pl.when(s < self.count)
+        def _():
+            self.relay_in(s)
+
+        @pl.when(s >= 2)
+        def _():
+            self.relay_out(s - 2)
 
     def drain_all(self, count):
         def step(s, carry):
@@ -174,11 +169,170 @@
     lax.fori_loop(0, count, step, 0)
 
 
-def attend_kernel(
-    x_hbm, lengths_ref, until_ref, gains, shifts, wqkv_hbm, bqv, wout_hbm,
-    sum_hbm, norm_hbm, q_hbm, kv_hbm, att_hbm, att_t_hbm, lse_out,
-    x_v, norm_v, w_v, wout_v, q_v, kv, q_t, v_t, s_v, p_v, att_t, att_v,
-    part, slot_a, slot_b, total, ar_send, ar_recv, kv_send, kv_recv, load_sem, store_sem,
+class Scatter:
+    def __init__(self, terms, near, far, send, recv, split):
+        self.cp, self.tp, self.core, self.chip = place()
+        self.count = lax.axis_size("cp")
+        self.depth = (self.count // 2).bit_length() - 1
+        self.terms, self.near, self.far = terms, near, far
+        self.send, self.recv = send, recv
+        self.chunk = terms.shape[0] // self.count
+        self.width = terms.shape[1]
+        self.parts = [p for p in ((0, 0, split), (1, split, self.width)) if p[2] > p[1]]
+        self.block = max(self.chunk, 128)
+
+    def partners(self):
+        others = [(self.cp + 1 - 2 * self.core, self.tp)]
+        for bit in range(self.depth):
+            others.append((self.cp + 2 * self.step(bit), self.tp))
+        return others
+
+    def step(self, bit):
+        return (1 - 2 * self.bit(bit)) * (1 << bit)
+
+    def bit(self, bit):
+        return lax.rem(lax.div(self.chip, 1 << bit), 2)
+
+    def fill(self, k, pick):
+        if self.block == self.chunk:
+            half = self.count // 2
+            block = 2 * lax.rem(k, half) + jnp.where(k < half, 1 - self.core, self.core)
+        else:
+            block = k
+        rows = rows_of(block, self.block)
+        for tile in range(self.width // 512):
+            lanes = slice(tile * 512, (tile + 1) * 512)
+            left, right = pick(tile, rows)
+            self.terms[rows, lanes] = dot_tn(left, right).astype(BF16)
+
+    def blocks(self):
+        return self.terms.shape[0] // self.block
+
+    def near_copy(self, t):
+        return pltpu.make_async_remote_copy(
+            src_ref=self.terms.at[rows_of(2 * t + 1 - self.core, self.chunk)],
+            dst_ref=self.near.at[rows_of(t, self.chunk)],
+            send_sem=self.send.at[t],
+            recv_sem=self.recv.at[t],
+            device_id=(self.cp + 1 - 2 * self.core, self.tp),
+            device_id_type=MESH,
+        )
+
+    def send_near(self, t):
+        self.near_copy(t).start()
+
+    def add_near(self, t):
+        self.near_copy(t).wait_recv()
+        base = (2 * t + self.core) * self.chunk
+
+        @functools.partial(loop, self.chunk // 64)
+        def _(i):
+            mine = pl.ds(pl.multiple_of(base + i * 64, 64), 64)
+            other = pl.ds(pl.multiple_of(t * self.chunk + i * 64, 64), 64)
+            self.terms[mine] = (self.terms[mine].astype(F32) + self.near[other].astype(F32)).astype(BF16)
+
+    def index(self, part, level, t, keep):
+        bit = level - 1 if part == 0 else self.depth - level
+        own = self.bit(bit)
+        own = own if keep else 1 - own
+        if part == 0:
+            return lax.rem(self.chip, 1 << bit) + own * (1 << bit) + t * (2 << bit), bit
+        return self.chip - lax.rem(self.chip, 2 << bit) + own * (1 << bit) + t, bit
+
+    def pieces(self, level):
+        first = self.count // 2
+        for earlier in range(1, level):
+            first += len(self.parts) * (1 << (self.depth - earlier))
+        for part, low, high in self.parts:
+            for t in range(1 << (self.depth - level)):
+                yield part, slice(low, high), t, first
+                first += 1
+
+    def far_copy(self, level, part, lanes, t, sem):
+        index, bit = self.index(part, level, t, False)
+        return pltpu.make_async_remote_copy(
+            src_ref=self.terms.at[rows_of(2 * index + self.core, self.chunk), lanes],
+            dst_ref=self.far.at[pl.ds(self.place(level) + t * self.chunk, self.chunk), lanes],
+            send_sem=self.send.at[sem],
+            recv_sem=self.recv.at[sem],
+            device_id=(self.cp + 2 * self.step(bit), self.tp),
+            device_id_type=MESH,
+        )
+
+    def send_far(self, level):
+        for piece in self.pieces(level):
+            self.far_copy(level, *piece).start()
+
+    def add_far(self, level):
+        for part, lanes, t, sem in self.pieces(level):
+            self.far_copy(level, part, lanes, t, sem).wait_recv()
+            index, _ = self.index(part, level, t, True)
+            base = (2 * index + self.core) * self.chunk
+            there = self.place(level) + t * self.chunk
+
+            @functools.partial(loop, self.chunk // 64)
+            def _(i, base=base, lanes=lanes, there=there):
+                mine = pl.ds(pl.multiple_of(base + i * 64, 64), 64)
+                other = pl.ds(pl.multiple_of(there + i * 64, 64), 64)
+                self.terms[mine, lanes] = (
+                    self.terms[mine, lanes].astype(F32) + self.far[other, lanes].astype(F32)
+                ).astype(BF16)
+
+    def place(self, level):
+        return sum(self.terms.shape[0] >> (earlier + 1) for earlier in range(1, level))
+
+    def finish(self, write):
+        level = self.depth
+        mine = rows_of(self.cp, self.chunk)
+        for part, lanes, t, sem in self.pieces(level):
+            self.far_copy(level, part, lanes, t, sem).wait_recv()
+            for tile in range(lanes.start // 512, lanes.stop // 512):
+                cut = slice(tile * 512, (tile + 1) * 512)
+                other = pl.ds(self.place(level), self.chunk)
+                write(tile, self.terms[mine, cut].astype(F32) + self.far[other, cut].astype(F32))
+
+    def drain(self):
+        loop(self.count // 2, lambda t: self.near_copy(t).wait_send())
+        for level in range(1, self.depth + 1):
+            for piece in self.pieces(level):
+                self.far_copy(level, *piece).wait_send()
+
+
+def scatter_scratch(depth, width, split):
+    count = lax.axis_size("cp")
+    parts = (split > 0) + (split < width)
+    sems = count // 2 + parts * (count // 2 - 1)
+    return [
+        pltpu.VMEM((depth // 2, width), BF16),
+        pltpu.VMEM((depth // 2 - depth // count, width), BF16),
+        pltpu.SemaphoreType.DMA((sems,)),
+        pltpu.SemaphoreType.DMA((sems,)),
+    ]
+
+
+def fold(v):
+    return jnp.sum(v.reshape(v.shape[0] // 8, 8, v.shape[1]), axis=0)
+
+
+def gelu_parts(u):
+    root = math.sqrt(2.0 / math.pi)
+    square = u * u
+    th = jnp.tanh(root * (u + 0.044715 * u * square))
+    half = 0.5 * (1.0 + th)
+    return u * half, half + 0.5 * u * (1.0 - th * th) * (root * (1.0 + 3 * 0.044715 * square))
+
+
+LAG = 4
+SPLIT_DOWN = 1024
+
+
+def front_kernel(
+    x_hbm, d_hbm, lengths_ref, until_ref, gains, shifts, wqkv_hbm, bqv, wout_hbm, b_outs, b_up, up_hbm, down_hbm,
+    attn_sum_hbm, norm1_hbm, q_hbm, kv_hbm, att_hbm, att_t_hbm, norm2_hbm, g_pre_hbm, ffn_hbm, g_hidden_hbm,
+    g_attn_hbm, lse_out, sums_out, down_out,
+    x_v, d_v, norm_v, up_v, down_v, q_v, kv, q_t, v_t, att_t, att_v, xhat, rstd, act_v, g_pre_v, acc,
+    part, slot_a, total, slot_b1, slot_b2, ar_send, ar_recv, near, far, rs_send, rs_recv,
+    kv_send, kv_recv, load_sem, store_sem,
 ):
     cp, tp, core, chip = place()
     bands = lax.axis_size("cp")
@@ -186,34 +340,65 @@
     rows, depth = x_v.shape
     width = q_v.shape[1]
     heads = width // HD
-    near = (cp + 1 - 2 * core, tp)
+    hidden = act_v.shape[1]
+    count = rows // SUB
+    per_chunk = CHUNK // SUB
+    sibling = (cp + 1 - 2 * core, tp)
     after = (lax.rem(cp + 2, bands), tp)
     before = (lax.rem(cp + bands - 2, bands), tp)
+    wout_v, scores, g_hidden, g_attn, part2, ffn_v = act_v, xhat, xhat, x_v, v_t, part
     loads = [
         pltpu.make_async_copy(x_hbm, x_v, load_sem.at[0]),
-        pltpu.make_async_copy(wqkv_hbm.at[1], w_v.at[1], load_sem.at[1]),
-        pltpu.make_async_copy(wqkv_hbm.at[2], w_v.at[2], load_sem.at[2]),
-        pltpu.make_async_copy(wqkv_hbm.at[0], w_v.at[0], load_sem.at[3]),
+        *[
+            pltpu.make_async_copy(
+                wqkv_hbm.at[j], up_v.at[:, j * width : (j + 1) * width], load_sem.at[i]
+            )
+            for i, j in ((1, 1), (2, 2), (3, 0))
+        ],
         pltpu.make_async_copy(wout_hbm, wout_v, load_sem.at[4]),
+        pltpu.make_async_copy(down_hbm, down_v, load_sem.at[5]),
+        pltpu.make_async_copy(d_hbm, d_v, load_sem.at[6]),
+        pltpu.make_async_copy(up_hbm, up_v, load_sem.at[7]),
     ]
-    for item in loads:
+    for item in loads[:-1]:
         item.start()
-    greet(cp, tp, [near, after, before])
-    begin, _ = band_info(lengths_ref, until_ref, cp * rows)
-    has_before = begin < chip * 2 * rows
+    stores = {
+        name: pltpu.make_async_copy(source, target, store_sem.at[i])
+        for i, (name, source, target) in enumerate(
+            (
+                ("norm1", norm_v, norm1_hbm),
+                ("q", q_v, q_hbm),
+                ("kv", kv, kv_hbm),
+                ("att", att_v, att_hbm),
+                ("att_t", att_t, att_t_hbm),
+                ("sum0", total.at[:CHUNK], attn_sum_hbm.at[:CHUNK]),
+                ("sum1", total.at[CHUNK:], attn_sum_hbm.at[CHUNK:]),
+                ("norm2", norm_v, norm2_hbm),
+                ("g_pre", g_pre_v, g_pre_hbm),
+                ("ffn", ffn_v, ffn_hbm),
+                ("g_hidden", g_hidden, g_hidden_hbm),
+                ("g_attn", g_attn, g_attn_hbm),
+            )
+        )
+    }
+    line1 = LineSum(part, slot_a, slot_b1, total, ar_send.at[0], ar_recv.at[0])
+    line2 = LineSum(part2, slot_a, slot_b2, total, ar_send.at[1], ar_recv.at[1])
+    scatter = Scatter(up_v, near, far, rs_send, rs_recv, SPLIT_DOWN)
+    greet(cp, tp, [*scatter.partners(), after, before])
+    begin, live = band_info(lengths_ref, until_ref, cp * rows)
+    bias = jnp.where(begin < chip * 2 * rows, 0.0, NEG)
     loads[0].wait()
 
     @functools.partial(loop, rows // 64)
     def _(i):
-        part_rows = rows_of(i, 64)
-        v = x_v[part_rows].astype(F32)
+        at = rows_of(i, 64)
+        v = x_v[at].astype(F32)
         mean = jnp.mean(v, axis=-1, keepdims=True)
         centred = v - mean
         var = jnp.mean(centred * centred, axis=-1, keepdims=True)
-        norm_v[part_rows] = (centred * lax.rsqrt(var + EPS) * gains[0:1] + shifts[0:1]).astype(BF16)
-
-    stores = [pltpu.make_async_copy(norm_v, norm_hbm, store_sem.at[0])]
-    stores[0].start()
+        norm_v[at] = (centred * lax.rsqrt(var + EPS) * gains[0:1] + shifts[0:1]).astype(BF16)
+
+    stores["norm1"].start()
     own = 2 + core
 
     for load, column in ((1, 0), (2, 1)):
@@ -221,7 +406,7 @@
 
         @functools.partial(loop, rows // CHUNK)
         def _(i):
-            value = dot(norm_v[rows_of(i, CHUNK)], w_v[load])
+            value = dot(norm_v[rows_of(i, CHUNK)], up_v[:, (column + 1) * width : (column + 2) * width])
             if column:
                 value = value + bqv[1:2]
             target = pl.ds(pl.multiple_of(own * rows + i * CHUNK, CHUNK), CHUNK)
@@ -236,8 +421,8 @@
         )
 
     to_next = kv_copy(0, own, after)
-    to_near = kv_copy(1, own, near)
-    forward = kv_copy(2, core, near)
+    to_near = kv_copy(1, own, sibling)
+    forward = kv_copy(2, core, sibling)
 
     @pl.when(chip < chips - 1)
     def _():
@@ -255,17 +440,17 @@
 
     @functools.partial(loop, rows // CHUNK)
     def _(i):
-        part_rows = rows_of(i, CHUNK)
-        value = (dot(norm_v[part_rows], w_v[0]) + bqv[0:1]).astype(BF16)
-        q_v[part_rows] = value
+        at = rows_of(i, CHUNK)
+        value = (dot(norm_v[at], up_v[:, :width]) + bqv[0:1]).astype(BF16)
+        q_v[at] = value
         turned = (value.astype(F32) * (HD ** -0.5)).T
         upper = lax.broadcasted_iota(jnp.int32, (2 * HD, CHUNK), 0) < HD
         for h in range(heads):
             both = turned[(h // 2) * 2 * HD : (h // 2 + 1) * 2 * HD]
-            q_t[h, :, part_rows] = jnp.where(upper == (h % 2 == 0), both, 0.0).astype(BF16)
-
-    stores.append(pltpu.make_async_copy(q_v, q_hbm, store_sem.at[1]))
-    stores[1].start()
+            q_t[h, :, at] = jnp.where(upper == (h % 2 == 0), both, 0.0).astype(BF16)
+
+    loads[7].start()
+    stores["q"].start()
     to_near.wait_recv()
 
     def turn_values(slot):
@@ -280,19 +465,15 @@
         forward.start()
         forward.wait_recv()
 
-    stores.append(pltpu.make_async_copy(kv, kv_hbm, store_sem.at[2]))
-    stores[2].start()
+    stores["kv"].start()
     turn_values(0)
     turn_values(1)
     loads[4].wait()
-    line = LineSum(part, slot_a, slot_b, total, ar_send, ar_recv)
-    bias = jnp.where(has_before, 0.0, NEG)
-    keys = 4 * rows
 
     for c in range(rows // CHUNK):
         columns = slice(c * CHUNK, (c + 1) * CHUNK)
 
-        def head(h, parity, c=c, columns=columns):
+        def head(h, c=c, columns=columns):
             lanes = pl.ds(pl.multiple_of(lax.div(h, 2) * 2 * HD, 2 * HD), 2 * HD)
             query = q_t[h, :, columns]
             top = jnp.full((1, CHUNK), NEG, F32)
@@ -304,336 +485,107 @@
                     key = lax.broadcasted_iota(jnp.int32, (rows, CHUNK), 0) + (b - 2) * rows
                     row = lax.broadcasted_iota(jnp.int32, (rows, CHUNK), 1) + c * CHUNK
                     s = jnp.where(key <= row + core * rows, s, NEG)
-                s_v[b * rows : (b + 1) * rows] = s
+                scores[:, b * CHUNK : (b + 1) * CHUNK] = s
                 top = jnp.maximum(top, jnp.max(s, axis=0, keepdims=True))
             mass = jnp.zeros((1, CHUNK), F32)
+            mixed = jnp.zeros((HD, CHUNK), F32)
+            feature = pl.ds(pl.multiple_of(h * HD, HD), HD)
             for b in range(4):
-                p = jnp.exp(s_v[b * rows : (b + 1) * rows] - top)
+                p = jnp.exp(scores[:, b * CHUNK : (b + 1) * CHUNK] - top)
                 mass = mass + jnp.sum(p, axis=0, keepdims=True)
-                p_v[b * rows : (b + 1) * rows] = p.astype(BF16)
-            feature = pl.ds(pl.multiple_of(h * HD, HD), HD)
-            att_t[feature, columns] = dot(v_t[feature], p_v[...]) / mass
+                mixed = mixed + dot(v_t[feature, b * rows : (b + 1) * rows], p.astype(BF16))
+            att_t[feature, columns] = mixed / mass
             lse_out[pl.ds(h, 1), columns] = top + jnp.log(mass)
-
-        loop(heads, lambda h: head(h, 0))
+            if c > 0:
+                @pl.when((h >= 3) & (lax.rem(h, 2) == 1))
+                def _():
+                    line1.tick(lax.div(h - 3, 2))
+
+        loop(heads, head)
         att_v[columns] = att_t[:, columns].T.astype(BF16)
+
+        @functools.partial(loop, depth // 512)
+        def _(t, columns=columns):
+            lanes = rows_of(t, 512)
+            part[columns, lanes] = dot(att_v[columns], wout_v[:, lanes]).astype(BF16)
+
+        loop(per_chunk, lambda s, c=c: line1.push(s + c * per_chunk))
+
+    stores["att"].start()
+    stores["att_t"].start()
+    acc[...] = jnp.zeros_like(acc)
+    stores["norm1"].wait()
+    loads[6].wait()
+
+    def second_norm(s):
+        line1.get(s)
+        at = rows_of(s, SUB)
+        row = lax.broadcasted_iota(jnp.int32, (SUB, 1), 0) + s * SUB
+        on = row < live
+        v = x_v[at].astype(F32) + jnp.where(on, total[at].astype(F32) + b_outs[0:1], 0.0)
+        mean = jnp.mean(v, axis=-1, keepdims=True)
+        centred = v - mean
+        scale = lax.rsqrt(jnp.mean(centred * centred, axis=-1, keepdims=True) + EPS)
+        hat = centred * scale
+        xhat[at] = hat
+        rstd[at] = jnp.broadcast_to(scale, (SUB, 128))
+        norm_v[at] = (hat * gains[1:2] + shifts[1:2]).astype(BF16)
+        acc[3] += fold(jnp.where(on, d_v[at].astype(F32), 0.0))
+
+    def feed_forward(c, ticks):
+        chunk = slice(c * CHUNK, (c + 1) * CHUNK)
+        on = lax.broadcasted_iota(jnp.int32, (CHUNK, 1), 0) + c * CHUNK < live
+
+        @functools.partial(loop, hidden // 512)
+        def _(t):
+            lanes = rows_of(t, 512)
+            pre = dot(norm_v[chunk], up_v[:, lanes]) + b_up[0:1, lanes]
+            g_act = dot_nt(d_v[chunk], down_v[lanes])
+            act, slope = gelu_parts(pre)
+            act_v[chunk, lanes] = jnp.where(on, act, 0.0).astype(BF16)
+            g_pre = jnp.where(on, g_act * slope, 0.0).astype(BF16)
+            g_pre_v[chunk, lanes] = g_pre
+            acc[4, :, lanes] += fold(g_pre.astype(F32))
+
+            @pl.when(lax.rem(t, 2) == 1)
+            def _():
+                ticks(lax.div(t, 2))
 
         @functools.partial(loop, depth // 512)
         def _(t):
             lanes = rows_of(t, 512)
-            part[columns, lanes] = dot(att_v[columns], wout_v[:, lanes]).astype(BF16)
-
-        loop(CHUNK // SUB, lambda s, c=c: line.push(s + c * (CHUNK // SUB)))
-
-    stores.append(pltpu.make_async_copy(att_v, att_hbm, store_sem.at[3]))
-    stores.append(pltpu.make_async_copy(att_t, att_t_hbm, store_sem.at[4]))
-    stores[3].start()
-    stores[4].start()
-    line.run(0, rows // SUB)
-    stores.append(pltpu.make_async_copy(total, sum_hbm, store_sem.at[5]))
-    stores[5].start()
-    line.drain_all(rows // SUB)
-
-    @pl.when(chip < chips - 1)
-    def _():
-        to_next.wait_send()
-
-    @pl.when(chip > 0)
-    def _():
-        forward.wait_send()
-
-    to_near.wait_send()
-    for item in stores:
-        item.wait()
-
-
-def attend(x, lengths, until, gains, shifts, wqkv, bqv, wout):
-    rows, depth = x.shape
-    width = wqkv.shape[2]
-    heads = width // HD
-    shape = jax.ShapeDtypeStruct
-    return pl.pallas_call(
-        attend_kernel,
-        out_shape=(
-            shape((rows, depth), BF16),
-            shape((rows, depth), BF16),
-            shape((rows, width), BF16),
-            shape((4 * rows, 2 * width), BF16),
-            shape((rows, width), BF16),
-            shape((width, rows), F32),
-            shape((heads, rows), F32),
-        ),
-        in_specs=[ANY, IN_SMEM, IN_SMEM, IN_VMEM, IN_VMEM, ANY, IN_VMEM, ANY],
-        out_specs=(ANY,) * 6 + (IN_VMEM,),
-        scratch_shapes=[
-            pltpu.VMEM((rows, depth), BF16),
-            pltpu.VMEM((rows, depth), BF16),
-            pltpu.VMEM((3, depth, width), BF16),
-            pltpu.VMEM((width, depth), BF16),
-            pltpu.VMEM((rows, width), BF16),
-            pltpu.VMEM((4 * rows, 2 * width), BF16),
-            pltpu.VMEM((heads, 2 * HD, rows), BF16),
-            pltpu.VMEM((width, 4 * rows), BF16),
-            pltpu.VMEM((4 * rows, CHUNK), F32),
-            pltpu.VMEM((4 * rows, CHUNK), BF16),
-            pltpu.VMEM((width, rows), F32),
-            pltpu.VMEM((rows, width), BF16),
-            *line_scratch(rows, depth),
-            pltpu.SemaphoreType.DMA((3,)),
-            pltpu.SemaphoreType.DMA((3,)),
-            pltpu.SemaphoreType.DMA((5,)),
-            pltpu.SemaphoreType.DMA((6,)),
-        ],
-        compiler_params=pltpu.CompilerParams(collective_id=0, has_side_effects=True, vmem_limit_bytes=56 * 2**20),
-        name="attend",
-    )(x, lengths, until, gains, shifts, wqkv, bqv, wout)
-
-
-class Scatter:
-    def __init__(self, terms, near, far, send, recv, split):
-        self.cp, self.tp, self.core, self.chip = place()
-        self.count = lax.axis_size("cp")
-        self.depth = (self.count // 2).bit_length() - 1
-        self.terms, self.near, self.far = terms, near, far
-        self.send, self.recv = send, recv
-        self.chunk = terms.shape[0] // self.count
-        self.width = terms.shape[1]
-        self.parts = [p for p in ((0, 0, split), (1, split, self.width)) if p[2] > p[1]]
-        self.block = max(self.chunk, 128)
-
-    def partners(self):
-        others = [(self.cp + 1 - 2 * self.core, self.tp)]
-        for bit in range(self.depth):
-            others.append((self.cp + 2 * self.step(bit), self.tp))
-        return others
-
-    def step(self, bit):
-        return (1 - 2 * self.bit(bit)) * (1 << bit)
-
-    def bit(self, bit):
-        return lax.rem(lax.div(self.chip, 1 << bit), 2)
-
-    def fill(self, k, pick):
-        if self.block == self.chunk:
-            half = self.count // 2
-            block = 2 * lax.rem(k, half) + jnp.where(k < half, 1 - self.core, self.core)
-        else:
-            block = k
-        rows = rows_of(block, self.block)
-        for tile in range(self.width // 512):
-            lanes = slice(tile * 512, (tile + 1) * 512)
-            left, right = pick(tile, rows)
-            self.terms[rows, lanes] = dot_tn(left, right).astype(BF16)
-
-    def blocks(self):
-        return self.terms.shape[0] // self.block
-
-    def near_copy(self, t):
-        return pltpu.make_async_remote_copy(
-            src_ref=self.terms.at[rows_of(2 * t + 1 - self.core, self.chunk)],
-            dst_ref=self.near.at[rows_of(t, self.chunk)],
-            send_sem=self.send.at[t],
-            recv_sem=self.recv.at[t],
-            device_id=(self.cp + 1 - 2 * self.core, self.tp),
-            device_id_type=MESH,
-        )
-
-    def send_near(self, t):
-        self.near_copy(t).start()
-
-    def add_near(self, t):
-        self.near_copy(t).wait_recv()
-        base = (2 * t + self.core) * self.chunk
-
-        @functools.partial(loop, self.chunk // 64)
-        def _(i):
-            mine = pl.ds(pl.multiple_of(base + i * 64, 64), 64)
-            other = pl.ds(pl.multiple_of(t * self.chunk + i * 64, 64), 64)
-            self.terms[mine] = (self.terms[mine].astype(F32) + self.near[other].astype(F32)).astype(BF16)
-
-    def index(self, part, level, t, keep):
-        bit = level - 1 if part == 0 else self.depth - level
-        own = self.bit(bit)
-        own = own if keep else 1 - own
-        if part == 0:
-            return lax.rem(self.chip, 1 << bit) + own * (1 << bit) + t * (2 << bit), bit
-        return self.chip - lax.rem(self.chip, 2 << bit) + own * (1 << bit) + t, bit
-
-    def pieces(self, level):
-        first = self.count // 2
-        for earlier in range(1, level):
-            first += len(self.parts) * (1 << (self.depth - earlier))
-        for part, low, high in self.parts:
-            for t in range(1 << (self.depth - level)):
-                yield part, slice(low, high), t, first
-                first += 1
-
-    def far_copy(self, level, part, lanes, t, sem):
-        index, bit = self.index(part, level, t, False)
-        return pltpu.make_async_remote_copy(
-            src_ref=self.terms.at[rows_of(2 * index + self.core, self.chunk), lanes],
-            dst_ref=self.far.at[pl.ds(self.place(level) + t * self.chunk, self.chunk), lanes],
-            send_sem=self.send.at[sem],
-            recv_sem=self.recv.at[sem],
-            device_id=(self.cp + 2 * self.step(bit), self.tp),
-            device_id_type=MESH,
-        )
-
-    def send_far(self, level):
-        for piece in self.pieces(level):
-            self.far_copy(level, *piece).start()
-
-    def add_far(self, level):
-        for part, lanes, t, sem in self.pieces(level):
-            self.far_copy(level, part, lanes, t, sem).wait_recv()
-            index, _ = self.index(part, level, t, True)
-            base = (2 * index + self.core) * self.chunk
-            there = self.place(level) + t * self.chunk
-
-            @functools.partial(loop, self.chunk // 64)
-            def _(i, base=base, lanes=lanes, there=there):
-                mine = pl.ds(pl.multiple_of(base + i * 64, 64), 64)
-                other = pl.ds(pl.multiple_of(there + i * 64, 64), 64)
-                self.terms[mine, lanes] = (
-                    self.terms[mine, lanes].astype(F32) + self.far[other, lanes].astype(F32)
-                ).astype(BF16)
-
-    def place(self, level):
-        return sum(self.terms.shape[0] >> (earlier + 1) for earlier in range(1, level))
-
-    def finish(self, write):
-        level = self.depth
-        mine = rows_of(self.cp, self.chunk)
-        for part, lanes, t, sem in self.pieces(level):
-            self.far_copy(level, part, lanes, t, sem).wait_recv()
-            for tile in range(lanes.start // 512, lanes.stop // 512):
-                cut = slice(tile * 512, (tile + 1) * 512)
-                other = pl.ds(self.place(level), self.chunk)
-                write(tile, self.terms[mine, cut].astype(F32) + self.far[other, cut].astype(F32))
-
-    def drain(self):
-        loop(self.count // 2, lambda t: self.near_copy(t).wait_send())
-        for level in range(1, self.depth + 1):
-            for piece in self.pieces(level):
-                self.far_copy(level, *piece).wait_send()
-
-
-def scatter_scratch(depth, width, split):
-    count = lax.axis_size("cp")
-    parts = (split > 0) + (split < width)
-    sems = count // 2 + parts * (count // 2 - 1)
-    return [
-        pltpu.VMEM((depth // 2, width), BF16),
-        pltpu.VMEM((depth // 2 - depth // count, width), BF16),
-        pltpu.SemaphoreType.DMA((sems,)),
-        pltpu.SemaphoreType.DMA((sems,)),
-    ]
-
-
-def fold(v):
-    return jnp.sum(v.reshape(v.shape[0] // 8, 8, v.shape[1]), axis=0)
-
-
-def gelu_parts(u):
-    root = math.sqrt(2.0 / math.pi)
-    square = u * u
-    th = jnp.tanh(root * (u + 0.044715 * u * square))
-    half = 0.5 * (1.0 + th)
-    return u * half, half + 0.5 * u * (1.0 - th * th) * (root * (1.0 + 3 * 0.044715 * square))
-
-
-LAG = 4
-SPLIT_DOWN = 1024
-
-
-def ffn_kernel(
-    sum_hbm, x_hbm, d_hbm, lengths_ref, until_ref, gains, shifts, b_outs, b_up, up_hbm, down_hbm,
-    norm_hbm, g_pre_hbm, ffn_hbm, g_hidden_hbm, g_attn_hbm, sums_out, down_out,
-    up_v, down_v, d_v, xhat, rstd, norm_v, act_v, g_pre_v, g_ffn_v, ffn_v, g_hidden, g_attn, acc,
-    part, slot_a, slot_b, total, ar_send, ar_recv, near, far, rs_send, rs_recv, load_sem, store_sem,
-):
-    cp, tp, core, chip = place()
-    rows, depth = d_v.shape
-    hidden = up_v.shape[1]
-    count = rows // SUB
-    loads = [
-        pltpu.make_async_copy(x_hbm, g_attn, load_sem.at[0]),
-        pltpu.make_async_copy(sum_hbm, ffn_v, load_sem.at[1]),
-        pltpu.make_async_copy(d_hbm, d_v, load_sem.at[2]),
-        pltpu.make_async_copy(up_hbm, up_v, load_sem.at[3]),
-        pltpu.make_async_copy(down_hbm, down_v, load_sem.at[4]),
-    ]
-    for item in loads:
-        item.start()
-    line = LineSum(part, slot_a, slot_b, total, ar_send, ar_recv)
-    scatter = Scatter(up_v, near, far, rs_send, rs_recv, SPLIT_DOWN)
-    greet(cp, tp, scatter.partners())
-    _, live = band_info(lengths_ref, until_ref, cp * rows)
-    acc[...] = jnp.zeros_like(acc)
-    for item in loads[:3]:
-        item.wait()
-
-    for c in range(rows // CHUNK):
-        chunk = slice(c * CHUNK, (c + 1) * CHUNK)
-
-        @functools.partial(loop, CHUNK // 64)
-        def _(i, c=c):
-            at = pl.ds(pl.multiple_of(c * CHUNK + i * 64, 64), 64)
-            row = lax.broadcasted_iota(jnp.int32, (64, 1), 0) + (c * CHUNK + i * 64)
-            on = row < live
-            branch = ffn_v[at].astype(F32) + b_outs[0:1]
-            v = g_attn[at].astype(F32) + jnp.where(on, branch, 0.0)
-            mean = jnp.mean(v, axis=-1, keepdims=True)
-            centred = v - mean
-            scale = lax.rsqrt(jnp.mean(centred * centred, axis=-1, keepdims=True) + EPS)
-            hat = centred * scale
-            xhat[at] = hat
-            rstd[at] = jnp.broadcast_to(scale, (64, 128))
-            norm_v[at] = (hat * gains[1:2] + shifts[1:2]).astype(BF16)
-            g_ffn = jnp.where(on, d_v[at].astype(F32), 0.0)
-            g_ffn_v[at] = g_ffn.astype(BF16)
-            acc[3] += fold(g_ffn)
-
-        if c == 0:
-            loads[3].wait()
-            loads[4].wait()
-
-        @functools.partial(loop, hidden // 512)
-        def _(t, c=c, chunk=chunk):
-            lanes = rows_of(t, 512)
-            pre = dot(norm_v[chunk], up_v[:, lanes]) + b_up[0:1, lanes]
-            g_act = dot_nt(g_ffn_v[chunk], down_v[lanes])
-            act, slope = gelu_parts(pre)
-            act_v[chunk, lanes] = act.astype(BF16)
-            g_pre = (g_act * slope).astype(BF16)
-            g_pre_v[chunk, lanes] = g_pre
-            acc[4, :, lanes] += fold(g_pre.astype(F32))
-            if c > 0:
-                line.relay_in(t)
-
-                @pl.when(t > 0)
-                def _():
-                    line.relay_out(t - 1)
-
-        @functools.partial(loop, depth // 512)
-        def _(t, chunk=chunk):
-            lanes = rows_of(t, 512)
-            part[chunk, lanes] = dot_nt(g_pre_v[chunk], up_v[lanes]).astype(BF16)
-
-        loop(CHUNK // SUB, lambda s, c=c: line.push(s + c * (CHUNK // SUB)))
-
-    stores = [
-        pltpu.make_async_copy(norm_v, norm_hbm, store_sem.at[0]),
-        pltpu.make_async_copy(g_pre_v, g_pre_hbm, store_sem.at[1]),
-        pltpu.make_async_copy(ffn_v, ffn_hbm, store_sem.at[2]),
-        pltpu.make_async_copy(g_hidden, g_hidden_hbm, store_sem.at[3]),
-        pltpu.make_async_copy(g_attn, g_attn_hbm, store_sem.at[4]),
-    ]
-    stores[0].start()
-    stores[1].start()
+            part2[chunk, lanes] = dot_nt(g_pre_v[chunk], up_v[lanes]).astype(BF16)
+
+            @pl.when(lax.rem(t, 2) == 1)
+            def _():
+                ticks(2 + lax.div(t, 2))
+
+    @functools.partial(loop, per_chunk)
+    def _(i):
+        line1.tick(3 + i)
+        second_norm(i)
+
+    stores["sum0"].start()
+    loads[5].wait()
+    loads[7].wait()
+    feed_forward(0, lambda i: line1.tick(3 + per_chunk + i))
+    stores["sum0"].wait()
+    loop(per_chunk, line2.push)
+    loop(4, lambda i: second_norm(per_chunk + i))
+    for i in range(3):
+        line1.tick(count - 1 + i)
+        second_norm(per_chunk + 4 + i)
+    second_norm(count - 1)
+    stores["sum1"].start()
+    stores["norm2"].start()
+    line1.drain_all(count)
+    feed_forward(1, line2.tick)
+    stores["g_pre"].start()
+    stores["sum1"].wait()
+    loop(per_chunk, lambda s: line2.push(per_chunk + s))
 
     def back(s):
-        line.get(s)
+        line2.get(s)
         at = rows_of(s, SUB)
         e = total[at].astype(F32)
         hat = xhat[at]
@@ -649,15 +601,11 @@
         acc[2] += fold(low.astype(F32))
 
     def ahead(s):
-        @pl.when(s < count)
-        def _():
-            line.relay_in(s)
-
-        line.relay_out(s - 1)
+        line2.tick(s)
         back(s - LAG)
 
     def term(k):
-        scatter.fill(k, lambda tile, rows: (g_ffn_v[:, rows], act_v[:, tile * 512 : (tile + 1) * 512]))
+        scatter.fill(k, lambda tile, at: (d_v[:, at], act_v[:, tile * 512 : (tile + 1) * 512]))
 
     def project(k):
         chunk = rows_of(lax.div(k, depth // 512), CHUNK)
@@ -689,15 +637,14 @@
         project(2 * i + 1)
         ahead(10 + i)
 
-    stores[2].start()
-    loop(count - 13, lambda i: ahead(14 + i))
-    loop(LAG - 1, lambda i: back(count - LAG + 1 + i))
-    stores[3].start()
-    stores[4].start()
+    stores["ffn"].start()
+    loop(count + 2 - 14, lambda i: ahead(14 + i))
     for level in range(1, scatter.depth):
         scatter.add_far(level)
         scatter.send_far(level + 1)
-
+    loop(LAG - 2, lambda i: back(count - LAG + 2 + i))
+    stores["g_hidden"].start()
+    stores["g_attn"].start()
     for k in range(5):
         sums_out[k : k + 1] = jnp.sum(acc[k], axis=0, keepdims=True)
 
@@ -708,51 +655,78 @@
 
     scatter.finish(write)
     scatter.drain()
-    line.drain_all(count)
-    for item in stores:
-        item.wait()
-
-
-def ffn(attn_sum, x, d_out, lengths, until, gains, shifts, b_outs, b_up, w_up, w_down):
+    line2.drain_all(count)
+
+    @pl.when(chip < chips - 1)
+    def _():
+        to_next.wait_send()
+
+    @pl.when(chip > 0)
+    def _():
+        forward.wait_send()
+
+    to_near.wait_send()
+    for name in ("q", "kv", "att", "att_t", "norm2", "g_pre", "ffn", "g_hidden", "g_attn"):
+        stores[name].wait()
+
+
+def front(x, d_out, lengths, until, gains, shifts, wqkv, bqv, wout, b_outs, b_up, w_up, w_down):
     rows, depth = x.shape
+    width = wqkv.shape[2]
+    heads = width // HD
     hidden = w_up.shape[1]
     chunk = depth // lax.axis_size("cp")
+    count = rows // SUB
     shape = jax.ShapeDtypeStruct
     return pl.pallas_call(
-        ffn_kernel,
+        front_kernel,
         out_shape=(
+            shape((rows, depth), BF16),
+            shape((rows, depth), BF16),
+            shape((rows, width), BF16),
+            shape((4 * rows, 2 * width), BF16),
+            shape((rows, width), BF16),
+            shape((width, rows), F32),
             shape((rows, depth), BF16),
             shape((rows, hidden), BF16),
             shape((rows, depth), BF16),
             shape((rows, depth), F32),
             shape((rows, depth), BF16),
+            shape((heads, rows), F32),
             shape((8, depth), F32),
             shape((hidden, chunk), F32),
         ),
-        in_specs=[ANY, ANY, ANY, IN_SMEM, IN_SMEM, IN_VMEM, IN_VMEM, IN_VMEM, IN_VMEM, ANY, ANY],
-        out_specs=(ANY,) * 5 + (IN_VMEM,) * 2,
+        in_specs=[ANY, ANY, IN_SMEM, IN_SMEM, IN_VMEM, IN_VMEM, ANY, IN_VMEM, ANY, IN_VMEM, IN_VMEM, ANY, ANY],
+        out_specs=(ANY,) * 11 + (IN_VMEM,) * 3,
         scratch_shapes=[
+            pltpu.VMEM((rows, depth), BF16),
+            pltpu.VMEM((rows, depth), BF16),
+            pltpu.VMEM((rows, depth), BF16),
             pltpu.VMEM((depth, hidden), BF16),
             pltpu.VMEM((hidden, depth), BF16),
-            pltpu.VMEM((rows, depth), BF16),
+            pltpu.VMEM((rows, width), BF16),
+            pltpu.VMEM((4 * rows, 2 * width), BF16),
+            pltpu.VMEM((heads, 2 * HD, rows), BF16),
+            pltpu.VMEM((width, 4 * rows), BF16),
+            pltpu.VMEM((width, rows), F32),
+            pltpu.VMEM((rows, width), BF16),
             pltpu.VMEM((rows, depth), F32),
             pltpu.VMEM((rows, 128), F32),
-            pltpu.VMEM((rows, depth), BF16),
             pltpu.VMEM((rows, hidden), BF16),
             pltpu.VMEM((rows, hidden), BF16),
-            pltpu.VMEM((rows, depth), BF16),
-            pltpu.VMEM((rows, depth), BF16),
-            pltpu.VMEM((rows, depth), F32),
-            pltpu.VMEM((rows, depth), BF16),
             pltpu.VMEM((5, 8, depth), F32),
-            *line_scratch(rows, depth),
+            *[pltpu.VMEM((rows, depth), BF16)] * 5,
+            pltpu.SemaphoreType.DMA((2, 3, count)),
+            pltpu.SemaphoreType.DMA((2, 3, count)),
             *scatter_scratch(depth, hidden, SPLIT_DOWN),
-            pltpu.SemaphoreType.DMA((5,)),
-            pltpu.SemaphoreType.DMA((5,)),
+            pltpu.SemaphoreType.DMA((3,)),
+            pltpu.SemaphoreType.DMA((3,)),
+            pltpu.SemaphoreType.DMA((8,)),
+            pltpu.SemaphoreType.DMA((12,)),
         ],
-        compiler_params=pltpu.CompilerParams(collective_id=1, has_side_effects=True, vmem_limit_bytes=62 * 2**20),
-        name="ffn",
-    )(attn_sum, x, d_out, lengths, until, gains, shifts, b_outs, b_up, w_up, w_down)
+        compiler_params=pltpu.CompilerParams(collective_id=1, has_side_effects=True, vmem_limit_bytes=63 * 2**20),
+        name="front",
+    )(x, d_out, lengths, until, gains, shifts, wqkv, bqv, wout, b_outs, b_up, w_up, w_down)
 
 
 SPLIT_UP = 1024
@@ -1271,11 +1245,9 @@
     d_out,
 ):
     wqkv = jnp.transpose(query_key_value_weight, (1, 0, 2))
-    attn_sum, norm1, q, kv, att, att_t, lse = attend(
-        layer_input, seq_lengths, active_until, ln_gains, ln_shifts, wqkv, b_qv, w_out
-    )
-    norm2, g_pre, ffn_low, g_hidden, g_attn, sums, g_down = ffn(
-        attn_sum, layer_input, d_out, seq_lengths, active_until, ln_gains, ln_shifts, b_outs, b_up[None], w_up, w_down
+    (attn_sum, norm1, q, kv, att, att_t, norm2, g_pre, ffn_low, g_hidden, g_attn, lse, sums, g_down) = front(
+        layer_input, d_out, seq_lengths, active_until, ln_gains, ln_shifts, wqkv, b_qv, w_out, b_outs, b_up[None],
+        w_up, w_down,
     )
     g_qkv_rows, ffn_sum, g_up = grad_attend(
         g_attn, w_out, q, kv, att_t, lse, seq_lengths, active_until, ffn_low, norm2, g_pre

time: 373 us -> 342 us (0.917)
  Pallas kernels: 357 us -> 326 us
    pallas_call x2 -> x1, Pallas kernels: 207 us -> 170 us  [front(): pl.pallas_call(front_kernel, out_shape=(shape((rows, depth), BF16), shape...]
    pallas_call x1, Pallas kernels: 74.6 us -> 80 us  [grad_attend(): pl.pallas_call(grad_attend_kernel, out_shape=(shape((rows, 3 * width), BF...]
where the time goes in v4:
time: 342 us; the launch traced here: 341 us
  Pallas kernels  326 us (95%)
  local copies, waits for them, and re-layouts  14.9 us (4%)
    pallas_call x1, Pallas kernels, front(): pl.pallas_call(front_kernel, out_shape=(shape((rows, depth), BF16), shape...  170 us
    pallas_call x1, Pallas kernels, grad_attend(): pl.pallas_call(grad_attend_kernel, out_shape=(shape((rows, 3 * width), BF...  80 us
    pallas_call x1, Pallas kernels, last(): pl.pallas_call(last_kernel, out_shape=(shape((rows, depth), F32), shape((...  76 us
    unnamed x31, local copies, waits for them, and re-layouts  14.9 us

profile of v4, /device:TPU:0, one launch (start us, length us, event | category | flops | bytes accessed | tf_op | source)
XLA Modules:
  0.0 341.3 jit_solution(3712407386375619674)
XLA Ops:
  0.6 169.7 %front.1 = (bf16[512,2048]{1,0:T(8,128)(2,1)}, bf16[512,2048]{1,0:T(8,128)(2,1)}, bf16[512,512]{1,0:T(8,128)(2,1)}, bf16[2048,1024]{1,0:T(8,128)(2,1)}, bf16[512...) custom-call(bf16[512,2048]{1,0:T(8,128)(2,1)} %x_hbm.3, ...), custom_call_target="tpu_custom_call" | custom-call | tf_op jit(solution)/shard_map/front/pallas_call | solution.py:681
  170.4 80.0 %grad_attend.1 = (bf16[512,1536]{1,0:T(8,128)(2,1)}, bf16[512,2048]{1,0:T(8,128)(2,1)}, f32[256,2048]{1,0:T(8,128)}) custom-call(bf16[512,2048]{1,0:T(8,128)(2,1)} %get-tuple-element.37.g_attn_hbm, bf16[512,2048]{1,0:T(8,128)(2,1)} %wout_hbm.3, bf16[512,512]{1,0:T(8,128)(2,1)} %get-tuple-element.38.q_hbm, bf16[2048,1024]{1,0:T(8,128)(2,1)} %get-tuple-element.39.kv_hbm, ...), custom_call_target="tpu_custom_call" | custom-call | tf_op jit(solution)/shard_map/grad_attend/pallas_call | solution.py:977
  250.4 76.0 %last.1 = (f32[512,2048]{1,0:T(8,128)}, f32[512,2048]{1,0:T(8,128)}, f32[3,256,512]{2,1,0:T(8,128)}, f32[512,256]{1,0:T(8,128)}, f32[2,2048]{1,0:T(2,128)}, /*in...) custom-call(bf16[512,1536]{1,0:T(8,128)(2,1)} %get-tuple-element.45.g_qkv_hbm, ...), custom_call_target="tpu_custom_call" | custom-call | tf_op jit(solution)/shard_map/last/pallas_call | solution.py:1190
  326.4 0.0 copy-start
  326.4 4.8 %copy.35 = f32[512,2048]{1,0:T(8,128)} copy(f32[512,2048]{1,0:T(8,128)} %get-tuple-element.74) | data formatting | bytes 8388608
  331.2 0.0 copy-done
  331.2 0.0 copy-start.7
  331.2 0.0 copy-start.6
  331.2 0.0 copy-start.3
  331.2 2.0 copy.36
  333.3 0.0 copy-done.7
  333.3 0.0 copy-start.9
  333.3 0.0 copy-start.4
  333.3 0.6 copy.37
  333.9 0.0 copy-done.6
  333.9 0.6 copy.38
  334.5 0.0 copy-done.3
  334.5 0.0 copy-start.5
  334.5 0.0 copy-start.2
  334.5 1.1 copy.39
  335.6 0.0 copy-done.9
  335.6 0.6 copy.40
  336.2 0.0 copy-done.4
  336.2 0.8 copy.41
  337.0 0.0 copy-done.5
  337.0 0.6 copy.42
  337.6 0.0 copy-done.2
  337.6 0.0 copy-start.8
  337.6 0.0 copy-start.1
  337.6 1.3 copy.43
  338.9 0.0 copy-done.8
  339.0 0.6 copy.44
  339.6 0.4 copy-done.1
  340.0 1.3 copy.45
Async XLA Ops:
  326.4 4.9 %copy-start = (f32[512,2048]{1,0:T(8,128)S(1)}, f32[512,2048]{1,0:T(8,128)}, u32[]{:S(2)}) copy-start(f32[512,2048]{1,0:T(8,128)} %get-tuple-element.75) | copy-start | bytes 12582916
  331.2 2.0 copy-start.7
  331.2 2.6 copy-start.6
  331.2 3.2 copy-start.3
  333.3 2.4 copy-start.9
  333.3 3.0 copy-start.4
  334.5 2.5 copy-start.5
  334.5 3.1 copy-start.2
  337.6 1.3 copy-start.8
  337.6 2.4 copy-start.1

commit v5 on v4

--- a/solution.py
+++ b/solution.py
@@ -322,17 +322,17 @@
     return u * half, half + 0.5 * u * (1.0 - th * th) * (root * (1.0 + 3 * 0.044715 * square))
 
 
-LAG = 4
+LAG = 5
 SPLIT_DOWN = 1024
 
 
 def front_kernel(
     x_hbm, d_hbm, lengths_ref, until_ref, gains, shifts, wqkv_hbm, bqv, wout_hbm, b_outs, b_up, up_hbm, down_hbm,
-    attn_sum_hbm, norm1_hbm, q_hbm, kv_hbm, att_hbm, att_t_hbm, norm2_hbm, g_pre_hbm, ffn_hbm, g_hidden_hbm,
+    attn_sum_hbm, norm1_hbm, q_hbm, q_next_hbm, kv_hbm, att_hbm, att_t_hbm, norm2_hbm, g_pre_hbm, ffn_hbm, g_hidden_hbm,
     g_attn_hbm, lse_out, sums_out, down_out,
-    x_v, d_v, norm_v, up_v, down_v, q_v, kv, q_t, v_t, att_t, att_v, xhat, rstd, act_v, g_pre_v, acc,
+    x_v, d_v, norm_v, up_v, down_v, q_v, q_next, kv, q_t, q_t_next, v_t, att_t, att_v, cross, cross_in, lse_cross, lse_in, xhat, rstd, act_v, g_pre_v, acc,
     part, slot_a, total, slot_b1, slot_b2, ar_send, ar_recv, near, far, rs_send, rs_recv,
-    kv_send, kv_recv, load_sem, store_sem,
+    x_send, x_recv, load_sem, store_sem,
 ):
     cp, tp, core, chip = place()
     bands = lax.axis_size("cp")
@@ -353,14 +353,14 @@
             pltpu.make_async_copy(
                 wqkv_hbm.at[j], up_v.at[:, j * width : (j + 1) * width], load_sem.at[i]
             )
-            for i, j in ((1, 1), (2, 2), (3, 0))
+            for i, j in ((1, 0), (2, 1), (3, 2))
         ],
         pltpu.make_async_copy(wout_hbm, wout_v, load_sem.at[4]),
         pltpu.make_async_copy(down_hbm, down_v, load_sem.at[5]),
         pltpu.make_async_copy(d_hbm, d_v, load_sem.at[6]),
         pltpu.make_async_copy(up_hbm, up_v, load_sem.at[7]),
     ]
-    for item in loads[:-1]:
+    for item in loads[:4]:
         item.start()
     stores = {
         name: pltpu.make_async_copy(source, target, store_sem.at[i])
@@ -369,6 +369,7 @@
                 ("norm1", norm_v, norm1_hbm),
                 ("q", q_v, q_hbm),
                 ("kv", kv, kv_hbm),
+                ("q_next", q_next, q_next_hbm),
                 ("att", att_v, att_hbm),
                 ("att_t", att_t, att_t_hbm),
                 ("sum0", total.at[:CHUNK], attn_sum_hbm.at[:CHUNK]),
@@ -385,8 +386,9 @@
     line2 = LineSum(part2, slot_a, slot_b2, total, ar_send.at[1], ar_recv.at[1])
     scatter = Scatter(up_v, near, far, rs_send, rs_recv, SPLIT_DOWN)
     greet(cp, tp, [*scatter.partners(), after, before])
-    begin, live = band_info(lengths_ref, until_ref, cp * rows)
-    bias = jnp.where(begin < chip * 2 * rows, 0.0, NEG)
+    _, live = band_info(lengths_ref, until_ref, cp * rows)
+    begin, _ = band_info(lengths_ref, until_ref, (chip + 1) * 2 * rows)
+    bias = jnp.where(begin < (chip + 1) * 2 * rows, 0.0, NEG)
     loads[0].wait()
 
     @functools.partial(loop, rows // 64)
@@ -399,9 +401,48 @@
         norm_v[at] = (centred * lax.rsqrt(var + EPS) * gains[0:1] + shifts[0:1]).astype(BF16)
 
     stores["norm1"].start()
-    own = 2 + core
-
-    for load, column in ((1, 0), (2, 1)):
+    pairs = heads // 2
+
+    def exchange(kind, p):
+        lanes = slice(p * 2 * HD, (p + 1) * 2 * HD)
+        source, target, device = (
+            (q_v.at[:, lanes], q_next.at[:, lanes], before),
+            (cross.at[lanes], cross_in.at[lanes], after),
+            (lse_cross, lse_in, after),
+            (kv.at[rows_of(core, rows)], kv.at[rows_of(core, rows)], sibling),
+        )[kind]
+        sem = (p, pairs + p, 2 * pairs, 2 * pairs + 1)[kind]
+        return pltpu.make_async_remote_copy(
+            src_ref=source, dst_ref=target, send_sem=x_send.at[sem], recv_sem=x_recv.at[sem],
+            device_id=device, device_id_type=MESH,
+        )
+
+    queries = [exchange(0, p) for p in range(pairs)]
+    gathered = [exchange(1, p) for p in range(pairs)] + [exchange(2, 0)]
+    to_near = exchange(3, 0)
+    has_before, has_after = chip > 0, chip < chips - 1
+    loads[1].wait()
+
+    @functools.partial(loop, rows // CHUNK)
+    def _(i):
+        at = rows_of(i, CHUNK)
+        q_v[at] = (dot(norm_v[at], up_v[:, :width]) + bqv[0:1]).astype(BF16)
+
+    @pl.when(has_before)
+    def _():
+        for item in queries:
+            item.start()
+
+    @pl.when(jnp.logical_not(has_after))
+    def _():
+        q_next[...] = jnp.zeros_like(q_next)
+
+    @pl.when(jnp.logical_not(has_before))
+    def _():
+        cross_in[...] = jnp.zeros_like(cross_in)
+        lse_in[...] = jnp.full_like(lse_in, NEG)
+
+    for load, column in ((2, 0), (3, 1)):
         loads[load].wait()
 
         @functools.partial(loop, rows // CHUNK)
@@ -409,99 +450,113 @@
             value = dot(norm_v[rows_of(i, CHUNK)], up_v[:, (column + 1) * width : (column + 2) * width])
             if column:
                 value = value + bqv[1:2]
-            target = pl.ds(pl.multiple_of(own * rows + i * CHUNK, CHUNK), CHUNK)
+            target = pl.ds(pl.multiple_of(core * rows + i * CHUNK, CHUNK), CHUNK)
             kv[target, column * width : (column + 1) * width] = value.astype(BF16)
 
-    def kv_copy(kind, slot, device):
-        block = kv.at[rows_of(slot, rows)]
-        to = kv.at[rows_of(core, rows)] if kind == 0 else block
-        return pltpu.make_async_remote_copy(
-            src_ref=block, dst_ref=to, send_sem=kv_send.at[kind], recv_sem=kv_recv.at[kind],
-            device_id=device, device_id_type=MESH,
-        )
-
-    to_next = kv_copy(0, own, after)
-    to_near = kv_copy(1, own, sibling)
-    forward = kv_copy(2, core, sibling)
-
-    @pl.when(chip < chips - 1)
-    def _():
-        to_next.start()
-
     to_near.start()
-
-    @pl.when(chip == 0)
-    def _():
-        @functools.partial(loop, 2 * rows // 64)
-        def _(i):
-            kv[rows_of(i, 64)] = jnp.zeros((64, 2 * width), BF16)
-
-    loads[3].wait()
+    for item in loads[4:]:
+        item.start()
+    stores["q"].start()
+
+    def turned(value, h):
+        upper = lax.broadcasted_iota(jnp.int32, value.shape, 0) < HD
+        return jnp.where(upper == (h % 2 == 0), value, 0.0).astype(BF16)
 
     @functools.partial(loop, rows // CHUNK)
     def _(i):
         at = rows_of(i, CHUNK)
-        value = (dot(norm_v[at], up_v[:, :width]) + bqv[0:1]).astype(BF16)
-        q_v[at] = value
-        turned = (value.astype(F32) * (HD ** -0.5)).T
-        upper = lax.broadcasted_iota(jnp.int32, (2 * HD, CHUNK), 0) < HD
+        value = q_v[at].astype(F32).T * (HD ** -0.5)
         for h in range(heads):
-            both = turned[(h // 2) * 2 * HD : (h // 2 + 1) * 2 * HD]
-            q_t[h, :, at] = jnp.where(upper == (h % 2 == 0), both, 0.0).astype(BF16)
-
-    loads[7].start()
-    stores["q"].start()
-    to_near.wait_recv()
+            q_t[h, :, at] = turned(value[(h // 2) * 2 * HD : (h // 2 + 1) * 2 * HD], h)
 
     def turn_values(slot):
         v_t[:, rows_of(slot, rows)] = kv[rows_of(slot, rows), width:].astype(F32).T.astype(BF16)
 
-    turn_values(2)
-    turn_values(3)
-
-    @pl.when(chip > 0)
+    turn_values(core)
+    to_near.wait_recv()
+    stores["kv"].start()
+    turn_values(1 - core)
+
+    def attend(query, lanes, feature, mask):
+        top = jnp.full((1, CHUNK), NEG, F32)
+        for b in range(2):
+            s = mask(b, dot(kv[b * rows : (b + 1) * rows, lanes], query))
+            scores[:, b * CHUNK : (b + 1) * CHUNK] = s
+            top = jnp.maximum(top, jnp.max(s, axis=0, keepdims=True))
+        mass = jnp.zeros((1, CHUNK), F32)
+        mixed = jnp.zeros((HD, CHUNK), F32)
+        for b in range(2):
+            p = jnp.exp(scores[:, b * CHUNK : (b + 1) * CHUNK] - top)
+            mass = mass + jnp.sum(p, axis=0, keepdims=True)
+            mixed = mixed + dot(v_t[feature, b * rows : (b + 1) * rows], p.astype(BF16))
+        return mixed / mass, top + jnp.log(mass)
+
+    def cross_pair(p):
+        start = p * 2 * HD
+        lanes = pl.ds(start, 2 * HD)
+        queries[p].wait_recv()
+        value = q_next[:, lanes].astype(F32).T * (HD ** -0.5)
+        for parity in range(2):
+            q_t_next[parity] = turned(value, parity)
+
+        @functools.partial(loop, 2)
+        def _(parity):
+            h = 2 * p + parity
+            feature = pl.ds(pl.multiple_of(h * HD, HD), HD)
+            for c in range(rows // CHUNK):
+                columns = slice(c * CHUNK, (c + 1) * CHUNK)
+                mixed, lse_row = attend(q_t_next[parity, :, columns], lanes, feature, lambda b, s: s + bias)
+                cross[feature, columns] = mixed.astype(BF16)
+                lse_cross[pl.ds(h, 1), columns] = lse_row
+
+        gathered[p].start()
+
+    @pl.when(has_after)
     def _():
-        to_next.wait_recv()
-        forward.start()
-        forward.wait_recv()
-
-    stores["kv"].start()
-    turn_values(0)
-    turn_values(1)
+        for p in range(pairs):
+            cross_pair(p)
+        gathered[pairs].start()
+
+    stores["q_next"].start()
     loads[4].wait()
 
     for c in range(rows // CHUNK):
         columns = slice(c * CHUNK, (c + 1) * CHUNK)
 
-        def head(h, c=c, columns=columns):
+        def causal(b, s, c=c):
+            key = lax.broadcasted_iota(jnp.int32, (rows, CHUNK), 0) + b * rows
+            row = lax.broadcasted_iota(jnp.int32, (rows, CHUNK), 1) + c * CHUNK
+            return jnp.where(key <= row + core * rows, s, NEG)
+
+        def head(h, c=c, columns=columns, causal=causal):
             lanes = pl.ds(pl.multiple_of(lax.div(h, 2) * 2 * HD, 2 * HD), 2 * HD)
-            query = q_t[h, :, columns]
-            top = jnp.full((1, CHUNK), NEG, F32)
-            for b in range(4):
-                s = dot(kv[b * rows : (b + 1) * rows, lanes], query)
-                if b < 2:
-                    s = s + bias
-                else:
-                    key = lax.broadcasted_iota(jnp.int32, (rows, CHUNK), 0) + (b - 2) * rows
-                    row = lax.broadcasted_iota(jnp.int32, (rows, CHUNK), 1) + c * CHUNK
-                    s = jnp.where(key <= row + core * rows, s, NEG)
-                scores[:, b * CHUNK : (b + 1) * CHUNK] = s
-                top = jnp.maximum(top, jnp.max(s, axis=0, keepdims=True))
-            mass = jnp.zeros((1, CHUNK), F32)
-            mixed = jnp.zeros((HD, CHUNK), F32)
             feature = pl.ds(pl.multiple_of(h * HD, HD), HD)
-            for b in range(4):
-                p = jnp.exp(scores[:, b * CHUNK : (b + 1) * CHUNK] - top)
-                mass = mass + jnp.sum(p, axis=0, keepdims=True)
-                mixed = mixed + dot(v_t[feature, b * rows : (b + 1) * rows], p.astype(BF16))
-            att_t[feature, columns] = mixed / mass
-            lse_out[pl.ds(h, 1), columns] = top + jnp.log(mass)
+            mixed, lse_row = attend(q_t[h, :, columns], lanes, feature, causal)
+            att_t[feature, columns] = mixed
+            lse_out[pl.ds(h, 1), columns] = lse_row
             if c > 0:
-                @pl.when((h >= 3) & (lax.rem(h, 2) == 1))
+                @pl.when(lax.rem(h, 2) == 1)
                 def _():
-                    line1.tick(lax.div(h - 3, 2))
+                    line1.tick(lax.div(h, 2))
 
         loop(heads, head)
+        if c == 0:
+            @pl.when(has_before)
+            def _():
+                for item in gathered:
+                    item.wait_recv()
+
+        mine, other = lse_out[:, columns], lse_in[:, columns]
+        top = jnp.maximum(mine, other)
+        both = top + jnp.log(jnp.exp(mine - top) + jnp.exp(other - top))
+        share, share_in = jnp.exp(mine - both), jnp.exp(other - both)
+        lse_out[:, columns] = both
+        for h in range(heads):
+            feature = slice(h * HD, (h + 1) * HD)
+            att_t[feature, columns] = (
+                att_t[feature, columns] * share[h : h + 1]
+                + cross_in[feature, columns].astype(F32) * share_in[h : h + 1]
+            )
         att_v[columns] = att_t[:, columns].T.astype(BF16)
 
         @functools.partial(loop, depth // 512)
@@ -562,24 +617,25 @@
 
     @functools.partial(loop, per_chunk)
     def _(i):
-        line1.tick(3 + i)
+        line1.tick(4 + i)
         second_norm(i)
 
     stores["sum0"].start()
     loads[5].wait()
     loads[7].wait()
-    feed_forward(0, lambda i: line1.tick(3 + per_chunk + i))
+    feed_forward(0, lambda i: line1.tick(4 + per_chunk + i))
     stores["sum0"].wait()
     loop(per_chunk, line2.push)
     loop(4, lambda i: second_norm(per_chunk + i))
-    for i in range(3):
-        line1.tick(count - 1 + i)
-        second_norm(per_chunk + 4 + i)
-    second_norm(count - 1)
+    for i in range(2):
+        line1.tick(count + i)
+        line2.relay_in(i)
+        second_norm(per_chunk + 4 + 2 * i)
+        second_norm(per_chunk + 5 + 2 * i)
     stores["sum1"].start()
     stores["norm2"].start()
     line1.drain_all(count)
-    feed_forward(1, line2.tick)
+    feed_forward(1, lambda i: line2.tick(2 + i))
     stores["g_pre"].start()
     stores["sum1"].wait()
     loop(per_chunk, lambda s: line2.push(per_chunk + s))
@@ -614,31 +670,29 @@
 
     blocks, half = scatter.blocks(), scatter.count // 2
 
-    @functools.partial(loop, 4)
+    @functools.partial(loop, 2)
     def _(i):
-        loop(blocks // 4, lambda j: term(i * (blocks // 4) + j))
-
-        @pl.when((i == 1) if scatter.block == scatter.chunk else (i == 3))
+        loop(blocks // 2, lambda j: term(i * (blocks // 2) + j))
+
+        @pl.when((i == 0) if scatter.block == scatter.chunk else (i == 1))
         def _():
             loop(half, scatter.send_near)
 
-        ahead(4 + i)
-
-    @functools.partial(loop, 2)
-    def _(i):
-        loop(half // 2, lambda j: scatter.add_near(i * (half // 2) + j))
-        ahead(8 + i)
-
+        line2.tick(6 + i)
+
+    line2.tick(8)
+    loop(half, scatter.add_near)
     scatter.send_far(1)
+    loop(4, lambda i: back(i))
 
     @functools.partial(loop, 4)
     def _(i):
         project(2 * i)
         project(2 * i + 1)
-        ahead(10 + i)
+        ahead(9 + i)
 
     stores["ffn"].start()
-    loop(count + 2 - 14, lambda i: ahead(14 + i))
+    loop(count + 2 - 13, lambda i: ahead(13 + i))
     for level in range(1, scatter.depth):
         scatter.add_far(level)
         scatter.send_far(level + 1)
@@ -657,16 +711,19 @@
     scatter.drain()
     line2.drain_all(count)
 
-    @pl.when(chip < chips - 1)
+    to_near.wait_send()
+
+    @pl.when(has_before)
     def _():
-        to_next.wait_send()
-
-    @pl.when(chip > 0)
+        for item in queries:
+            item.wait_send()
+
+    @pl.when(has_after)
     def _():
-        forward.wait_send()
-
-    to_near.wait_send()
-    for name in ("q", "kv", "att", "att_t", "norm2", "g_pre", "ffn", "g_hidden", "g_attn"):
+        for item in gathered:
+            item.wait_send()
+
+    for name in ("q", "q_next", "kv", "att", "att_t", "norm2", "g_pre", "ffn", "g_hidden", "g_attn"):
         stores[name].wait()
 
 
@@ -684,7 +741,8 @@
             shape((rows, depth), BF16),
             shape((rows, depth), BF16),
             shape((rows, width), BF16),
-            shape((4 * rows, 2 * width), BF16),
+            shape((rows, width), BF16),
+            shape((2 * rows, 2 * width), BF16),
             shape((rows, width), BF16),
             shape((width, rows), F32),
             shape((rows, depth), BF16),
@@ -697,7 +755,7 @@
             shape((hidden, chunk), F32),
         ),
         in_specs=[ANY, ANY, IN_SMEM, IN_SMEM, IN_VMEM, IN_VMEM, ANY, IN_VMEM, ANY, IN_VMEM, IN_VMEM, ANY, ANY],
-        out_specs=(ANY,) * 11 + (IN_VMEM,) * 3,
+        out_specs=(ANY,) * 12 + (IN_VMEM,) * 3,
         scratch_shapes=[
             pltpu.VMEM((rows, depth), BF16),
             pltpu.VMEM((rows, depth), BF16),
@@ -705,11 +763,17 @@
             pltpu.VMEM((depth, hidden), BF16),
             pltpu.VMEM((hidden, depth), BF16),
             pltpu.VMEM((rows, width), BF16),
-            pltpu.VMEM((4 * rows, 2 * width), BF16),
+            pltpu.VMEM((rows, width), BF16),
+            pltpu.VMEM((2 * rows, 2 * width), BF16),
             pltpu.VMEM((heads, 2 * HD, rows), BF16),
-            pltpu.VMEM((width, 4 * rows), BF16),
+            pltpu.VMEM((2, 2 * HD, rows), BF16),
+            pltpu.VMEM((width, depth), BF16),
             pltpu.VMEM((width, rows), F32),
             pltpu.VMEM((rows, width), BF16),
+            pltpu.VMEM((width, rows), BF16),
+            pltpu.VMEM((width, rows), BF16),
+            pltpu.VMEM((heads, rows), F32),
+            pltpu.VMEM((heads, rows), F32),
             pltpu.VMEM((rows, depth), F32),
             pltpu.VMEM((rows, 128), F32),
             pltpu.VMEM((rows, hidden), BF16),
@@ -719,10 +783,10 @@
             pltpu.SemaphoreType.DMA((2, 3, count)),
             pltpu.SemaphoreType.DMA((2, 3, count)),
             *scatter_scratch(depth, hidden, SPLIT_DOWN),
-            pltpu.SemaphoreType.DMA((3,)),
-            pltpu.SemaphoreType.DMA((3,)),
+            pltpu.SemaphoreType.DMA((heads + 2,)),
+            pltpu.SemaphoreType.DMA((heads + 2,)),
             pltpu.SemaphoreType.DMA((8,)),
-            pltpu.SemaphoreType.DMA((12,)),
+            pltpu.SemaphoreType.DMA((13,)),
         ],
         compiler_params=pltpu.CompilerParams(collective_id=1, has_side_effects=True, vmem_limit_bytes=63 * 2**20),
         name="front",
@@ -734,10 +798,10 @@
 
 
 def grad_attend_kernel(
-    g_attn_hbm, wout_hbm, q_hbm, kv_hbm, att_t_hbm, lse, lengths_ref, until_ref, ffn_hbm, norm_hbm, g_pre_hbm,
+    g_attn_hbm, wout_hbm, q_hbm, q_next_hbm, kv_hbm, att_t_hbm, lse, lengths_ref, until_ref, ffn_hbm, norm_hbm, g_pre_hbm,
     g_qkv_hbm, ffn_sum_hbm, up_out,
-    g_attn_v, wout_v, q_v, kv, k_t, att_t, q_t, g_v, g_t, delta, acc, g_qkv_v,
-    give_near, got_near, give_before, got_after, give_own, got_own, kv_send, kv_recv,
+    g_attn_v, wout_v, q_v, q_next, kv, k_t, att_t, q_t, g_v, g_next, g_t, stats, stats_next, acc, g_qkv_v,
+    g_q_next, give_q, got_q, give_near, got_near, x_send, x_recv,
     norm_v, g_pre_v, terms, near, far, rs_send, rs_recv,
     part, slot_a, slot_b, total, ar_send, ar_recv, load_sem, store_sem,
 ):
@@ -760,18 +824,20 @@
                 (g_attn_hbm, g_attn_v),
                 (wout_hbm, wout_v),
                 (q_hbm, q_v),
+                (q_next_hbm, q_next),
                 (kv_hbm, kv),
                 (att_t_hbm, att_t),
             )
         )
     ]
-    for item in loads:
+    for item in loads[:5]:
         item.start()
     line = LineSum(part, slot_a, slot_b, total, ar_send, ar_recv)
     scatter = Scatter(terms, near, far, rs_send, rs_recv, SPLIT_UP)
     greet(cp, tp, [*scatter.partners(), after, before])
-    begin, _ = band_info(lengths_ref, until_ref, cp * rows)
-    bias = jnp.where(begin < chip * 2 * rows, 0.0, NEG)
+    begin, _ = band_info(lengths_ref, until_ref, (chip + 1) * 2 * rows)
+    has_before, has_after = chip > 0, chip < chips - 1
+    bias = jnp.where((begin < (chip + 1) * 2 * rows) & has_after, 0.0, NEG)
     loads[0].wait()
     loads[1].wait()
     loads[2].wait()
@@ -781,43 +847,81 @@
     def term(k):
         scatter.fill(k, lambda tile, at: (norm_v[:, at], g_pre_v[:, tile * 512 : (tile + 1) * 512]))
 
+    for item in loads[5:]:
+        item.start()
     loop(blocks // 2, term)
     if scatter.block == scatter.chunk:
         loop(half, scatter.send_near)
-    loop(blocks - blocks // 2, lambda k: term(blocks // 2 + k))
-    if scatter.block != scatter.chunk:
-        loop(half, scatter.send_near)
-
-    def relay(s):
-        @pl.when(s < count)
-        def _():
-            line.relay_in(s)
-
-        @pl.when(s > 0)
-        def _():
-            line.relay_out(s - 1)
-
-    loop(2, relay)
+    relay = line.tick
+    relay(0)
     for item in loads[3:]:
         item.wait()
     scale = HD ** -0.5
+
+    pairs = heads // 2
+
+    def exchange(kind, p=0):
+        lanes = slice(p * 2 * HD, (p + 1) * 2 * HD)
+        source, target, device = (
+            (g_v, g_next, before),
+            (stats, stats_next, before),
+            (give_near, got_near, sibling),
+            (give_q.at[lanes], got_q.at[lanes], after),
+        )[kind]
+        return pltpu.make_async_remote_copy(
+            src_ref=source, dst_ref=target, send_sem=x_send.at[kind + p], recv_sem=x_recv.at[kind + p],
+            device_id=device, device_id_type=MESH,
+        )
+
+    to_before = [exchange(0), exchange(1)]
+    to_near = exchange(2)
+    to_after = [exchange(3, p) for p in range(pairs)]
+
+    def turn(source, target, factor):
+        @functools.partial(loop, rows // CHUNK)
+        def _(i):
+            at = rows_of(i, CHUNK)
+            value = source[at].astype(F32).T * factor
+            upper = lax.broadcasted_iota(jnp.int32, (2 * HD, CHUNK), 0) < HD
+            for h in range(heads):
+                both = slice((h // 2) * 2 * HD, (h // 2 + 1) * 2 * HD)
+                target[h, :, at] = jnp.where(upper == (h % 2 == 0), value[both], 0.0).astype(BF16)
+
+    stats[:heads] = lse[...]
 
     @functools.partial(loop, rows // CHUNK)
     def _(i):
         at = rows_of(i, CHUNK)
         low = dot_nt(g_attn_v[at], wout_v[...]).astype(BF16)
         g_v[at] = low
-        turned = low.astype(F32).T
-        turned_q = q_v[at].astype(F32).T * scale
-        upper = lax.broadcasted_iota(jnp.int32, (2 * HD, CHUNK), 0) < HD
+        value = low.astype(F32).T
         for h in range(heads):
-            both = slice((h // 2) * 2 * HD, (h // 2 + 1) * 2 * HD)
             mine = slice(h * HD, (h + 1) * HD)
-            g_t[h, :, at] = jnp.where(upper == (h % 2 == 0), turned[both], 0.0).astype(BF16)
-            q_t[h, :, at] = jnp.where(upper == (h % 2 == 0), turned_q[both], 0.0).astype(BF16)
-            delta[h : h + 1, at] = jnp.sum(turned[mine] * att_t[mine, at], axis=0, keepdims=True)
-
-    @functools.partial(loop, 4)
+            stats[heads + h : heads + h + 1, at] = jnp.sum(value[mine] * att_t[mine, at], axis=0, keepdims=True)
+
+    @pl.when(has_before)
+    def _():
+        for item in to_before:
+            item.start()
+
+    relay(1)
+    loop(blocks - blocks // 2, lambda k: term(blocks // 2 + k))
+    if scatter.block != scatter.chunk:
+        loop(half, scatter.send_near)
+
+    @pl.when(jnp.logical_not(has_after))
+    def _():
+        g_next[...] = jnp.zeros_like(g_next)
+        stats_next[...] = jnp.zeros_like(stats_next)
+
+    @pl.when(jnp.logical_not(has_before))
+    def _():
+        got_q[...] = jnp.zeros_like(got_q)
+
+    turn(g_v, g_t, 1.0)
+    turn(q_v, q_t, scale)
+
+    @functools.partial(loop, 2)
     def _(i):
         at = rows_of(i, rows)
         k_t[:, at] = kv[at, :width].astype(F32).T.astype(BF16)
@@ -825,15 +929,17 @@
     @functools.partial(loop, rows // 64)
     def _(i):
         att_t[rows_of(i, 64)] = jnp.zeros((64, rows), F32)
-
-    @functools.partial(loop, 4 * rows // 64)
+        g_q_next[rows_of(i, 64)] = jnp.zeros((64, rows), F32)
+
+    @functools.partial(loop, 2 * rows // 64)
     def _(i):
         acc[rows_of(i, 64)] = jnp.zeros((64, 2 * width), F32)
 
-    g_q_t = att_t
     relay(2)
-
-    def head(h, bands_of):
+    loop(half, scatter.add_near)
+    scatter.send_far(1)
+
+    def head(h, q_rows, g_rows, numbers, g_q_t, mask):
         offset = lax.div(h, 2) * 2 * HD
         lanes = pl.ds(pl.multiple_of(offset, 2 * HD), 2 * HD)
         lanes_v = pl.ds(pl.multiple_of(offset + width, 2 * HD), 2 * HD)
@@ -842,105 +948,85 @@
         mine = low_lanes == (lax.rem(h, 2) == 0)
         for c in range(rows // CHUNK):
             cols = slice(c * CHUNK, (c + 1) * CHUNK)
-            q_n = jnp.where(mine, q_v[cols, lanes].astype(F32), 0.0).astype(BF16)
-            g_n = jnp.where(mine, g_v[cols, lanes].astype(F32), 0.0).astype(BF16)
-            lse_row = lse[pl.ds(h, 1), cols]
-            delta_row = delta[pl.ds(h, 1), cols]
-            for b in bands_of:
+            q_n = jnp.where(mine, q_rows[cols, lanes].astype(F32), 0.0).astype(BF16)
+            g_n = jnp.where(mine, g_rows[cols, lanes].astype(F32), 0.0).astype(BF16)
+            lse_row = numbers[pl.ds(h, 1), cols]
+            delta_row = numbers[pl.ds(heads + h, 1), cols]
+            for b in range(2):
                 keys = slice(b * rows, (b + 1) * rows)
                 s = dot(kv[keys, lanes], q_t[h, :, cols])
-                if b < 2:
-                    s = s + (bias - lse_row)
-                else:
-                    key = lax.broadcasted_iota(jnp.int32, (rows, CHUNK), 0) + (b - 2) * rows
-                    row = lax.broadcasted_iota(jnp.int32, (rows, CHUNK), 1) + c * CHUNK
-                    s = jnp.where(key <= row + core * rows, s - lse_row, NEG)
-                p = jnp.exp(s)
+                p = jnp.exp(mask(b, c, s, lse_row))
                 g_s = (p * (dot(kv[keys, lanes_v], g_t[h, :, cols]) - delta_row)).astype(BF16)
                 acc[keys, lanes] += dot(g_s, q_n)
                 acc[keys, lanes_v] += dot(p.astype(BF16), g_n)
                 g_q_t[feature, cols] += dot(k_t[feature, keys], g_s)
 
+    def causal(b, c, s, lse_row):
+        key = lax.broadcasted_iota(jnp.int32, (rows, CHUNK), 0) + b * rows
+        row = lax.broadcasted_iota(jnp.int32, (rows, CHUNK), 1) + c * CHUNK
+        return jnp.where(key <= row + core * rows, s - lse_row, NEG)
+
     @functools.partial(loop, heads)
     def _(h):
-        head(h, (0, 1))
-
-        @pl.when(h == 0)
+        head(h, q_v, g_v, stats, att_t, causal)
+
+        @pl.when(h < heads - 2)
         def _():
-            loop(half, scatter.add_near)
-            scatter.send_far(1)
-
-        @pl.when(lax.rem(h, 2) == 1)
+            relay(3 + h)
+
+    @pl.when(has_after)
+    def _():
+        for item in to_before:
+            item.wait_recv()
+
+    turn(g_next, g_t, 1.0)
+    turn(q_next, q_t, scale)
+    relay(9)
+    for p in range(pairs):
+
+        @functools.partial(loop, 2)
+        def _(parity, p=p):
+            head(2 * p + parity, q_next, g_next, stats_next, g_q_next, lambda b, c, s, row: s + (bias - row))
+            relay(10 + 2 * p + parity)
+
+        pair = slice(p * 2 * HD, (p + 1) * 2 * HD)
+        give_q[pair] = g_q_next[pair].astype(BF16)
+
+        @pl.when(has_after)
         def _():
-            relay(3 + lax.div(h, 2))
-
-    def kv_copy(kind, source, target, device):
-        return pltpu.make_async_remote_copy(
-            src_ref=source, dst_ref=target, send_sem=kv_send.at[kind], recv_sem=kv_recv.at[kind],
-            device_id=device, device_id_type=MESH,
-        )
-
-    to_near = kv_copy(0, give_near, got_near, sibling)
-    to_before = kv_copy(1, give_before, got_after, before)
-    to_own = kv_copy(2, give_own, got_own, sibling)
-
-    def lower(target, slot):
-        @functools.partial(loop, rows // 64)
-        def _(i):
-            at = pl.ds(pl.multiple_of(slot * rows + i * 64, 64), 64)
-            target[rows_of(i, 64)] = acc[at].astype(BF16)
-
-    def add_to(slot, source):
-        @functools.partial(loop, rows // 64)
-        def _(i):
-            at = pl.ds(pl.multiple_of(slot * rows + i * 64, 64), 64)
-            acc[at] += source[rows_of(i, 64)].astype(F32)
-
-    lower(give_near, 1 - core)
-    to_near.start()
-    to_near.wait_recv()
-    add_to(core, got_near)
-    lower(give_before, core)
-
-    @pl.when(chip > 0)
-    def _():
-        to_before.start()
-
-    @functools.partial(loop, heads)
-    def _(h):
-        head(h, (2, 3))
-
-        @pl.when(lax.rem(h, 2) == 1)
-        def _():
-            relay(7 + lax.div(h, 2))
-
-    own = 2 + core
-    lower(give_own, 3 - core)
-    to_own.start()
-    loop(2, lambda i: relay(11 + i))
+            to_after[p].start()
+
     levels = scatter.depth
     for level in range(1, levels):
         scatter.add_far(level)
         scatter.send_far(level + 1)
-    loop(4, lambda i: relay(13 + i))
-    to_own.wait_recv()
-    add_to(own, got_own)
-
-    @pl.when(chip < chips - 1)
-    def _():
-        to_before.wait_recv()
-        add_to(own, got_after)
 
     @functools.partial(loop, rows // 64)
     def _(i):
-        at = pl.ds(pl.multiple_of(own * rows + i * 64, 64), 64)
-        g_qkv_v[rows_of(i, 64), width : 2 * width] = (acc[at, :width] * scale).astype(BF16)
-        g_qkv_v[rows_of(i, 64), 2 * width :] = acc[at, width:].astype(BF16)
+        at = pl.ds(pl.multiple_of((1 - core) * rows + i * 64, 64), 64)
+        give_near[rows_of(i, 64)] = acc[at].astype(BF16)
+
+    to_near.start()
+    to_near.wait_recv()
+
+    @functools.partial(loop, rows // 64)
+    def _(i):
+        at = pl.ds(pl.multiple_of(core * rows + i * 64, 64), 64)
+        near_at = rows_of(i, 64)
+        total_at = acc[at] + got_near[near_at].astype(F32)
+        g_qkv_v[near_at, width : 2 * width] = (total_at[:, :width] * scale).astype(BF16)
+        g_qkv_v[near_at, 2 * width :] = total_at[:, width:].astype(BF16)
+
+    @pl.when(has_before)
+    def _():
+        for item in to_after:
+            item.wait_recv()
 
     @functools.partial(loop, rows // CHUNK)
     def _(i):
         at = rows_of(i, CHUNK)
-        g_qkv_v[at, :width] = (g_q_t[:, at].T * scale).astype(BF16)
+        both = att_t[:, at] + got_q[:, at].astype(F32)
+        g_qkv_v[at, :width] = (both.T * scale).astype(BF16)
 
     stores = [
         pltpu.make_async_copy(g_qkv_v, g_qkv_hbm, store_sem.at[0]),
@@ -957,17 +1043,22 @@
     scatter.drain()
     line.drain_all(count)
     to_near.wait_send()
-    to_own.wait_send()
-
-    @pl.when(chip > 0)
+
+    @pl.when(has_before)
     def _():
-        to_before.wait_send()
+        for item in to_before:
+            item.wait_send()
+
+    @pl.when(has_after)
+    def _():
+        for item in to_after:
+            item.wait_send()
 
     for item in stores:
         item.wait()
 
 
-def grad_attend(g_attn, wout, q, kv, att_t, lse, lengths, until, ffn_low, norm2, g_pre):
+def grad_attend(g_attn, wout, q, q_next, kv, att_t, lse, lengths, until, ffn_low, norm2, g_pre):
     rows, depth = g_attn.shape
     width = q.shape[1]
     heads = width // HD
@@ -981,42 +1072,49 @@
             shape((rows, depth), BF16),
             shape((chunk, hidden), F32),
         ),
-        in_specs=[ANY, ANY, ANY, ANY, ANY, IN_VMEM, IN_SMEM, IN_SMEM, ANY, ANY, ANY],
+        in_specs=[ANY] * 6 + [IN_VMEM, IN_SMEM, IN_SMEM, ANY, ANY, ANY],
         out_specs=(ANY, ANY, IN_VMEM),
         scratch_shapes=[
             pltpu.VMEM((rows, depth), BF16),
             pltpu.VMEM((width, depth), BF16),
             pltpu.VMEM((rows, width), BF16),
-            pltpu.VMEM((4 * rows, 2 * width), BF16),
-            pltpu.VMEM((width, 4 * rows), BF16),
+            pltpu.VMEM((rows, width), BF16),
+            pltpu.VMEM((2 * rows, 2 * width), BF16),
+            pltpu.VMEM((width, 2 * rows), BF16),
             pltpu.VMEM((width, rows), F32),
             pltpu.VMEM((heads, 2 * HD, rows), BF16),
             pltpu.VMEM((rows, width), BF16),
+            pltpu.VMEM((rows, width), BF16),
             pltpu.VMEM((heads, 2 * HD, rows), BF16),
-            pltpu.VMEM((heads, rows), F32),
-            pltpu.VMEM((4 * rows, 2 * width), F32),
+            pltpu.VMEM((2 * heads, rows), F32),
+            pltpu.VMEM((2 * heads, rows), F32),
+            pltpu.VMEM((2 * rows, 2 * width), F32),
             pltpu.VMEM((rows, 3 * width), BF16),
-            *[pltpu.VMEM((rows, 2 * width), BF16)] * 6,
-            pltpu.SemaphoreType.DMA((3,)),
-            pltpu.SemaphoreType.DMA((3,)),
+            pltpu.VMEM((width, rows), F32),
+            pltpu.VMEM((width, rows), BF16),
+            pltpu.VMEM((width, rows), BF16),
+            pltpu.VMEM((rows, 2 * width), BF16),
+            pltpu.VMEM((rows, 2 * width), BF16),
+            pltpu.SemaphoreType.DMA((3 + heads // 2,)),
+            pltpu.SemaphoreType.DMA((3 + heads // 2,)),
             pltpu.VMEM((rows, depth), BF16),
             pltpu.VMEM((rows, hidden), BF16),
             pltpu.VMEM((depth, hidden), BF16),
             *scatter_scratch(depth, hidden, SPLIT_UP),
             *line_scratch(rows, depth),
-            pltpu.SemaphoreType.DMA((8,)),
+            pltpu.SemaphoreType.DMA((9,)),
             pltpu.SemaphoreType.DMA((2,)),
         ],
         compiler_params=pltpu.CompilerParams(collective_id=2, has_side_effects=True, vmem_limit_bytes=63 * 2**20),
         name="grad_attend",
-    )(g_attn, wout, q, kv, att_t, lse, lengths, until, ffn_low, norm2, g_pre)
+    )(g_attn, wout, q, q_next, kv, att_t, lse, lengths, until, ffn_low, norm2, g_pre)
 
 
 def last_kernel(
     g_qkv_hbm, wqkv_hbm, x_hbm, g_hidden_hbm, norm_hbm, g_attn_hbm, att_hbm, attn_sum_hbm, ffn_sum_hbm,
     lengths_ref, until_ref, gains, b_outs, sums_in,
     g_x_hbm, out_hbm, qkv_out, w_out_out, gains_out, shifts_out, bqv_out, bouts_out, bup_out,
-    g_qkv_v, w_v, x_v, g_hidden, norm_v, g_attn_v, att_v, attn_sum, ffn_sum, out_v, acc, small, small_got,
+    g_qkv_v, w_v, x_v, g_hidden, norm_v, g_attn_v, att_v, attn_sum, ffn_sum, out_v, acc, small, small_got, late, late_got,
     terms, near, far, rs_send, rs_recv,
     part, slot_a, slot_b, total, ar_send, ar_recv, small_send, small_recv, load_sem, store_sem,
 ):
@@ -1040,12 +1138,12 @@
             )
         )
     ]
-    for item in loads:
+    for item in loads[:2]:
         item.start()
     line = LineSum(part, slot_a, slot_b, total, ar_send, ar_recv)
     scatter = Scatter(terms, near, far, rs_send, rs_recv, SPLIT_LAST)
-    partners = scatter.partners()
-    greet(cp, tp, partners)
+    bands = lax.axis_size("cp")
+    greet(cp, tp, [(lax.rem(cp + k, bands), tp) for k in range(1, bands)])
     _, live = band_info(lengths_ref, until_ref, cp * rows)
     acc[...] = jnp.zeros_like(acc)
     loads[0].wait()
@@ -1063,7 +1161,41 @@
             part[chunk, lanes] = value.astype(BF16)
 
         loop(CHUNK // SUB, lambda s, c=c: line.push(s + c * (CHUNK // SUB)))
-
+        if c == 0:
+            for item in loads[2:]:
+                item.start()
+
+    def small_copy(which, sender, receiver):
+        source, target = ((small, small_got), (late, late_got))[which]
+        return pltpu.make_async_remote_copy(
+            src_ref=source, dst_ref=target.at[sender], send_sem=small_send.at[which, receiver],
+            recv_sem=small_recv.at[which, sender], device_id=(receiver, tp), device_id_type=MESH,
+        )
+
+    def give_small(which):
+        loop(bands - 1, lambda k: small_copy(which, cp, lax.rem(cp + 1 + k, bands)).start())
+
+    def take_small(which):
+        source, target = ((small, small_got), (late, late_got))[which]
+        target[cp] = source[...]
+
+        @functools.partial(loop, bands - 1)
+        def _(k):
+            sender = lax.rem(cp + 1 + k, bands)
+            small_copy(which, sender, sender).wait_recv()
+
+        value = target[0]
+        for k in range(1, bands):
+            value = value + target[k]
+        return value
+
+    small[0:5] = sums_in[0:5]
+    small[6:8] = jnp.zeros((2, depth), F32)
+    small[5:6, 2 * width :] = jnp.zeros((1, depth - 2 * width), F32)
+    for j in range(2):
+        bias = jnp.sum(g_qkv_v[:, 2 * j * width : (2 * j + 1) * width].astype(F32), axis=0, keepdims=True)
+        small[5:6, j * width : (j + 1) * width] = bias
+    give_small(0)
     for item in loads[2:]:
         item.wait()
 
@@ -1086,16 +1218,10 @@
         pltpu.make_async_copy(g_hidden.at[at], g_x_hbm.at[at], store_sem.at[0, s]).start()
         pltpu.make_async_copy(out_v.at[at], out_hbm.at[at], store_sem.at[1, s]).start()
 
-    behind = 2
+    behind = 4
 
     def ahead(s):
-        @pl.when(s < count)
-        def _():
-            line.relay_in(s)
-
-        @pl.when(s > 0)
-        def _():
-            line.relay_out(s - 1)
+        line.tick(s)
 
         @pl.when(s >= behind)
         def _():
@@ -1127,39 +1253,21 @@
         ahead(4 + i)
 
     scatter.send_far(1)
-    for j in range(2):
-        bias = jnp.sum(g_qkv_v[:, 2 * j * width : (2 * j + 1) * width].astype(F32), axis=0, keepdims=True)
-        small[0, 7:8, j * width : (j + 1) * width] = bias
-    small[0, 7:8, 2 * width :] = jnp.zeros((1, depth - 2 * width), F32)
     loop(8, lambda i: ahead(6 + i))
     for level in range(1, scatter.depth):
         scatter.add_far(level)
         scatter.send_far(level + 1)
-    loop(count - 13, lambda i: ahead(14 + i))
-    loop(behind - 1, lambda i: back(count + 1 - behind + i))
-
-    small[0, 0:5] = sums_in[0:5]
+    loop(count + 2 - 14, lambda i: ahead(14 + i))
+    loop(behind - 2, lambda i: back(count + 2 - behind + i))
+
     for k in range(2):
-        small[0, 5 + k : 6 + k] = jnp.sum(acc[k], axis=0, keepdims=True)
-    rounds = []
-    for level, other in enumerate(partners):
-        item = pltpu.make_async_remote_copy(
-            src_ref=small.at[level], dst_ref=small_got.at[level], send_sem=small_send.at[level],
-            recv_sem=small_recv.at[level], device_id=other, device_id_type=MESH,
-        )
-        item.start()
-        item.wait_recv()
-        rounds.append(item)
-        small[level + 1] = small[level] + small_got[level]
-    final = len(partners)
-    gains_out[0:1] = small[final, 5:6]
-    gains_out[1:2] = small[final, 0:1]
-    shifts_out[0:1] = small[final, 6:7]
-    shifts_out[1:2] = small[final, 1:2]
-    bouts_out[...] = small[final, 2:4]
-    bup_out[...] = small[final, 4:5]
+        late[k : k + 1] = jnp.sum(acc[k], axis=0, keepdims=True)
+    give_small(1)
+    early = take_small(0)
+    bouts_out[...] = early[2:4]
+    bup_out[...] = early[4:5]
     for j in range(2):
-        bqv_out[j : j + 1] = small[final, 7:8, j * width : (j + 1) * width]
+        bqv_out[j : j + 1] = early[5:6, j * width : (j + 1) * width]
 
     def write(tile, value):
         if tile < 3:
@@ -1168,10 +1276,19 @@
             w_out_out[...] = value.T
 
     scatter.finish(write)
+    final = take_small(1)
+    gains_out[0:1] = final[0:1]
+    gains_out[1:2] = early[0:1]
+    shifts_out[0:1] = final[1:2]
+    shifts_out[1:2] = early[1:2]
     scatter.drain()
     line.drain_all(count)
-    for item in rounds:
-        item.wait_send()
+
+    @functools.partial(loop, bands - 1)
+    def _(k):
+        other = lax.rem(cp + 1 + k, bands)
+        small_copy(0, cp, other).wait_send()
+        small_copy(1, cp, other).wait_send()
 
     @functools.partial(loop, count)
     def _(s):
@@ -1185,7 +1302,6 @@
     width = att.shape[1]
     bands = lax.axis_size("cp")
     chunk = depth // bands
-    rounds = bands.bit_length() - 1
     shape = jax.ShapeDtypeStruct
     return pl.pallas_call(
         last_kernel,
@@ -1214,13 +1330,15 @@
             pltpu.VMEM((rows, depth), BF16),
             pltpu.VMEM((rows, depth), F32),
             pltpu.VMEM((2, 8, depth), F32),
-            pltpu.VMEM((rounds + 1, 8, depth), F32),
-            pltpu.VMEM((rounds, 8, depth), F32),
+            pltpu.VMEM((8, depth), F32),
+            pltpu.VMEM((bands, 8, depth), F32),
+            pltpu.VMEM((2, depth), F32),
+            pltpu.VMEM((bands, 2, depth), F32),
             pltpu.VMEM((depth, depth), BF16),
             *scatter_scratch(depth, depth, SPLIT_LAST),
             *line_scratch(rows, depth),
-            pltpu.SemaphoreType.DMA((rounds,)),
-            pltpu.SemaphoreType.DMA((rounds,)),
+            pltpu.SemaphoreType.DMA((2, bands)),
+            pltpu.SemaphoreType.DMA((2, bands)),
             pltpu.SemaphoreType.DMA((9,)),
             pltpu.SemaphoreType.DMA((2, rows // SUB)),
         ],
@@ -1245,12 +1363,12 @@
     d_out,
 ):
     wqkv = jnp.transpose(query_key_value_weight, (1, 0, 2))
-    (attn_sum, norm1, q, kv, att, att_t, norm2, g_pre, ffn_low, g_hidden, g_attn, lse, sums, g_down) = front(
+    (attn_sum, norm1, q, q_next, kv, att, att_t, norm2, g_pre, ffn_low, g_hidden, g_attn, lse, sums, g_down) = front(
         layer_input, d_out, seq_lengths, active_until, ln_gains, ln_shifts, wqkv, b_qv, w_out, b_outs, b_up[None],
         w_up, w_down,
     )
     g_qkv_rows, ffn_sum, g_up = grad_attend(
-        g_attn, w_out, q, kv, att_t, lse, seq_lengths, active_until, ffn_low, norm2, g_pre
+        g_attn, w_out, q, q_next, kv, att_t, lse, seq_lengths, active_until, ffn_low, norm2, g_pre
     )
     g_x, out, g_qkv, g_out, g_ln_gains, g_ln_shifts, g_bqv, g_bouts, g_bup = last(
         g_qkv_rows, wqkv, layer_input, g_hidden, norm1, g_attn, att, attn_sum, ffn_sum,

time: 342 us -> 315 us (0.921)
  Pallas kernels: 326 us -> 299 us
    pallas_call x1, Pallas kernels: 170 us -> 152 us  [front(): pl.pallas_call(front_kernel, out_shape=(shape((rows, depth), BF16), shape...]
    pallas_call x1, Pallas kernels: 80 us -> 70.2 us  [grad_attend(): pl.pallas_call(grad_attend_kernel, out_shape=(shape((rows, 3 * width), BF...]
where the time goes in v5:
time: 315 us; the launch traced here: 314 us
  Pallas kernels  299 us (95%)
  local copies, waits for them, and re-layouts  14.9 us (5%)
    pallas_call x1, Pallas kernels, front(): pl.pallas_call(front_kernel, out_shape=(shape((rows, depth), BF16), shape...  152 us
    pallas_call x1, Pallas kernels, last(): pl.pallas_call(last_kernel, out_shape=(shape((rows, depth), F32), shape((...  76.5 us
    pallas_call x1, Pallas kernels, grad_attend(): pl.pallas_call(grad_attend_kernel, out_shape=(shape((rows, 3 * width), BF...  70.2 us
    unnamed x31, local copies, waits for them, and re-layouts  14.9 us

profile of v5, /device:TPU:0, one launch (start us, length us, event | category | flops | bytes accessed | tf_op | source)
XLA Modules:
  0.0 314.3 jit_solution(12158452402922328038)
XLA Ops:
  0.6 152.0 %front.1 = (bf16[512,2048]{1,0:T(8,128)(2,1)}, bf16[512,2048]{1,0:T(8,128)(2,1)}, bf16[512,512]{1,0:T(8,128)(2,1)}, bf16[512,512]{1,0:T(8,128)(2,1)}, bf16[1024,...) custom-call(bf16[512,2048]{1,0:T(8,128)(2,1)} %x_hbm.3, ...), custom_call_target="tpu_custom_call" | custom-call | tf_op jit(solution)/shard_map/front/pallas_call | solution.py:738
  152.6 70.2 %grad_attend.1 = (bf16[512,1536]{1,0:T(8,128)(2,1)}, bf16[512,2048]{1,0:T(8,128)(2,1)}, f32[256,2048]{1,0:T(8,128)}) custom-call(bf16[512,2048]{1,0:T(8,128)(2,1)} %get-tuple-element.38.g_attn_hbm, bf16[512,2048]{1,0:T(8,128)(2,1)} %wout_hbm.3, bf16[512,512]{1,0:T(8,128)(2,1)} %get-tuple-element.39.q_hbm, bf16[512,512]{1,0:T(8,128)(2,1)} %get-tuple-element.40.q_next_hbm, ...), custom_call_target="tpu_custom_call" | custom-call | tf_op jit(solution)/shard_map/grad_attend/pallas_call | solution.py:1068
  222.9 76.5 %last.1 = (f32[512,2048]{1,0:T(8,128)}, f32[512,2048]{1,0:T(8,128)}, f32[3,256,512]{2,1,0:T(8,128)}, f32[512,256]{1,0:T(8,128)}, f32[2,2048]{1,0:T(2,128)}, /*in...) custom-call(bf16[512,1536]{1,0:T(8,128)(2,1)} %get-tuple-element.47.g_qkv_hbm, ...), custom_call_target="tpu_custom_call" | custom-call | tf_op jit(solution)/shard_map/last/pallas_call | solution.py:1306
  299.4 0.0 copy-start
  299.4 4.8 %copy.35 = f32[512,2048]{1,0:T(8,128)} copy(f32[512,2048]{1,0:T(8,128)} %get-tuple-element.76) | data formatting | bytes 8388608
  304.2 0.0 copy-done
  304.3 0.0 copy-start.7
  304.3 0.0 copy-start.6
  304.3 0.0 copy-start.3
  304.3 2.0 copy.36
  306.3 0.0 copy-done.7
  306.3 0.0 copy-start.9
  306.3 0.0 copy-start.4
  306.3 0.6 copy.37
  306.9 0.0 copy-done.6
  306.9 0.6 copy.38
  307.5 0.0 copy-done.3
  307.5 0.0 copy-start.5
  307.5 0.0 copy-start.2
  307.5 1.1 copy.39
  308.6 0.0 copy-done.9
  308.7 0.6 copy.40
  309.2 0.0 copy-done.4
  309.2 0.8 copy.41
  310.0 0.0 copy-done.5
  310.0 0.6 copy.42
  310.6 0.0 copy-done.2
  310.7 0.0 copy-start.8
  310.7 0.0 copy-start.1
  310.7 1.3 copy.43
  312.0 0.0 copy-done.8
  312.0 0.6 copy.44
  312.6 0.4 copy-done.1
  313.0 1.3 copy.45
Async XLA Ops:
  299.4 4.9 %copy-start = (f32[512,2048]{1,0:T(8,128)S(1)}, f32[512,2048]{1,0:T(8,128)}, u32[]{:S(2)}) copy-start(f32[512,2048]{1,0:T(8,128)} %get-tuple-element.77) | copy-start | bytes 12582916
  304.3 2.0 copy-start.7
  304.3 2.6 copy-start.6
  304.3 3.2 %copy-start.3 = (f32[3,256,512]{2,1,0:T(8,128)S(1)}, f32[3,256,512]{2,1,0:T(8,128)}, u32[]{:S(2)}) copy-start(f32[3,256,512]{2,1,0:T(8,128)} %get-tuple-element.58) | copy-start | bytes 4718596
  306.3 2.4 copy-start.9
  306.3 3.0 copy-start.4
  307.5 2.5 copy-start.5
  307.5 3.1 %copy-start.2 = (f32[256,2048]{1,0:T(8,128)S(1)}, f32[256,2048]{1,0:T(8,128)}, u32[]{:S(2)}) copy-start(f32[256,2048]{1,0:T(8,128)} %get-tuple-element.84) | copy-start | bytes 6291460
  310.7 1.3 copy-start.8
  310.7 2.4 copy-start.1

commit v6 on v5

--- a/solution.py
+++ b/solution.py
@@ -19,6 +19,7 @@
 IN_VMEM = pl.BlockSpec(memory_space=pltpu.VMEM)
 IN_SMEM = pl.BlockSpec(memory_space=pltpu.SMEM)
 SUB = 32
+PIECE = 16
 CHUNK = 256
 
 
@@ -69,59 +70,56 @@
         self.send, self.recv = send, recv
         self.count = part.shape[0] // SUB
 
-    def copy(self, kind, s):
+    def copy(self, kind, piece):
         part, slot_a, slot_b, total = self.refs
         src, dst = ((part, slot_a), (part, slot_b), (total, total))[kind]
         other = (self.cp, 3 - self.tp if kind == 1 else line_near(self.tp))
-        rows = rows_of(s, SUB)
+        rows = rows_of(piece, PIECE)
         return pltpu.make_async_remote_copy(
             src_ref=src.at[rows],
             dst_ref=dst.at[rows],
-            send_sem=self.send.at[kind, s],
-            recv_sem=self.recv.at[kind, s],
+            send_sem=self.send.at[kind, piece],
+            recv_sem=self.recv.at[kind, piece],
             device_id=other,
             device_id_type=MESH,
         )
 
+    def pieces(self, s):
+        return [s * (SUB // PIECE) + j for j in range(SUB // PIECE)]
+
     def push(self, s):
         @pl.when(self.edge)
         def _():
-            self.copy(0, s).start()
+            for piece in self.pieces(s):
+                self.copy(0, piece).start()
 
     def relay_in(self, s):
         part, slot_a, _, _ = self.refs
 
         @pl.when(jnp.logical_not(self.edge))
         def _():
-            rows = rows_of(s, SUB)
-            self.copy(0, s).wait_recv()
-            part[rows] = (part[rows].astype(F32) + slot_a[rows].astype(F32)).astype(BF16)
-            self.copy(1, s).start()
+            for piece in self.pieces(s):
+                rows = rows_of(piece, PIECE)
+                self.copy(0, piece).wait_recv()
+                part[rows] = (part[rows].astype(F32) + slot_a[rows].astype(F32)).astype(BF16)
+                self.copy(1, piece).start()
 
     def relay_out(self, s):
         part, _, slot_b, total = self.refs
 
         @pl.when(jnp.logical_not(self.edge))
         def _():
-            rows = rows_of(s, SUB)
-            self.copy(1, s).wait_recv()
-            total[rows] = (part[rows].astype(F32) + slot_b[rows].astype(F32)).astype(BF16)
-            self.copy(2, s).start()
+            for piece in self.pieces(s):
+                rows = rows_of(piece, PIECE)
+                self.copy(1, piece).wait_recv()
+                total[rows] = (part[rows].astype(F32) + slot_b[rows].astype(F32)).astype(BF16)
+                self.copy(2, piece).start()
 
     def get(self, s):
         @pl.when(self.edge)
         def _():
-            self.copy(2, s).wait_recv()
-
-    def drain(self, s):
-        @pl.when(self.edge)
-        def _():
-            self.copy(0, s).wait_send()
-
-        @pl.when(jnp.logical_not(self.edge))
-        def _():
-            self.copy(1, s).wait_send()
-            self.copy(2, s).wait_send()
+            for piece in self.pieces(s):
+                self.copy(2, piece).wait_recv()
 
     def tick(self, s):
         @pl.when(s < self.count)
@@ -132,20 +130,21 @@
         def _():
             self.relay_out(s - 2)
 
-    def drain_all(self, count):
-        def step(s, carry):
-            self.drain(s)
-            return carry
-
-        lax.fori_loop(0, count, step, 0)
-
-
-def line_scratch(rows, width, with_part=True):
-    count = rows // SUB
-    return [pltpu.VMEM((rows, width), BF16)] * 4 + [
-        pltpu.SemaphoreType.DMA((3, count)),
-        pltpu.SemaphoreType.DMA((3, count)),
-    ]
+    def drain_all(self):
+        @pl.when(self.edge)
+        def _():
+            loop(self.refs[0].shape[0] // PIECE, lambda piece: self.copy(0, piece).wait_send())
+
+        @pl.when(jnp.logical_not(self.edge))
+        def _():
+            @functools.partial(loop, self.refs[0].shape[0] // PIECE)
+            def _(piece):
+                self.copy(1, piece).wait_send()
+                self.copy(2, piece).wait_send()
+
+
+def line_scratch(rows, width):
+    return [pltpu.VMEM((rows, width), BF16)] * 4 + [pltpu.SemaphoreType.DMA((3, rows // PIECE))] * 2
 
 
 def band_info(lengths_ref, until_ref, first):
@@ -173,129 +172,165 @@
     def __init__(self, terms, near, far, send, recv, split):
         self.cp, self.tp, self.core, self.chip = place()
         self.count = lax.axis_size("cp")
-        self.depth = (self.count // 2).bit_length() - 1
+        self.half = self.count // 2
+        self.depth = self.half.bit_length() - 1
         self.terms, self.near, self.far = terms, near, far
         self.send, self.recv = send, recv
         self.chunk = terms.shape[0] // self.count
         self.width = terms.shape[1]
-        self.parts = [p for p in ((0, 0, split), (1, split, self.width)) if p[2] > p[1]]
-        self.block = max(self.chunk, 128)
+        self.lanes = {p: c for p, c in ((0, slice(0, split)), (1, slice(split, self.width))) if c.stop > c.start}
+        self.order = list(range(self.half))[::-1]
+        self.whole_blocks = self.chunk >= 128
 
     def partners(self):
         others = [(self.cp + 1 - 2 * self.core, self.tp)]
         for bit in range(self.depth):
-            others.append((self.cp + 2 * self.step(bit), self.tp))
+            others.append((self.cp + 2 * self.flip(1 << bit), self.tp))
         return others
 
-    def step(self, bit):
-        return (1 - 2 * self.bit(bit)) * (1 << bit)
-
-    def bit(self, bit):
-        return lax.rem(lax.div(self.chip, 1 << bit), 2)
-
-    def fill(self, k, pick):
-        if self.block == self.chunk:
-            half = self.count // 2
-            block = 2 * lax.rem(k, half) + jnp.where(k < half, 1 - self.core, self.core)
+    def flip(self, e):
+        change = 0
+        for bit in range(self.depth):
+            if e >> bit & 1:
+                change = change + (1 - 2 * lax.rem(lax.div(self.chip, 1 << bit), 2)) * (1 << bit)
+        return change
+
+    def row(self, e, core):
+        if isinstance(e, int):
+            other = self.chip + self.flip(e)
         else:
-            block = k
-        rows = rows_of(block, self.block)
+            other = 0
+            for bit in range(self.depth):
+                mine = lax.rem(lax.div(self.chip, 1 << bit), 2)
+                change = lax.rem(lax.div(e, 1 << bit), 2)
+                other = other + (mine + change - 2 * mine * change) * (1 << bit)
+        return (2 * other + core) * self.chunk
+
+    def fill_block(self, first, size, pick):
+        rows = pl.ds(pl.multiple_of(first, size), size)
+
         for tile in range(self.width // 512):
-            lanes = slice(tile * 512, (tile + 1) * 512)
             left, right = pick(tile, rows)
-            self.terms[rows, lanes] = dot_tn(left, right).astype(BF16)
-
-    def blocks(self):
-        return self.terms.shape[0] // self.block
-
-    def near_copy(self, t):
+            self.terms[rows, tile * 512 : (tile + 1) * 512] = dot_tn(left, right).astype(BF16)
+
+    def fill_near(self, pick):
+        if not self.whole_blocks:
+            loop(self.terms.shape[0] // 128, lambda k: self.fill_block(k * 128, 128, pick))
+
+        @functools.partial(loop, self.half)
+        def _(k):
+            e = self.half - 1 - k
+            if self.whole_blocks:
+                self.fill_block(self.row(e, 1 - self.core), self.chunk, pick)
+            self.near_copy(e).start()
+
+    def fill_own(self, pick):
+        if self.whole_blocks:
+            loop(self.half, lambda k: self.fill_block(self.row(self.half - 1 - k, self.core), self.chunk, pick))
+
+    def near_copy(self, e):
         return pltpu.make_async_remote_copy(
-            src_ref=self.terms.at[rows_of(2 * t + 1 - self.core, self.chunk)],
-            dst_ref=self.near.at[rows_of(t, self.chunk)],
-            send_sem=self.send.at[t],
-            recv_sem=self.recv.at[t],
+            src_ref=self.terms.at[pl.ds(pl.multiple_of(self.row(e, 1 - self.core), self.chunk), self.chunk)],
+            dst_ref=self.near.at[rows_of(e, self.chunk)],
+            send_sem=self.send.at[e],
+            recv_sem=self.recv.at[e],
             device_id=(self.cp + 1 - 2 * self.core, self.tp),
             device_id_type=MESH,
         )
 
-    def send_near(self, t):
-        self.near_copy(t).start()
-
-    def add_near(self, t):
-        self.near_copy(t).wait_recv()
-        base = (2 * t + self.core) * self.chunk
-
-        @functools.partial(loop, self.chunk // 64)
+    def add(self, e, source, first, lanes):
+        base = self.row(e, self.core)
+
+        @functools.partial(loop, self.chunk // 32)
         def _(i):
-            mine = pl.ds(pl.multiple_of(base + i * 64, 64), 64)
-            other = pl.ds(pl.multiple_of(t * self.chunk + i * 64, 64), 64)
-            self.terms[mine] = (self.terms[mine].astype(F32) + self.near[other].astype(F32)).astype(BF16)
-
-    def index(self, part, level, t, keep):
-        bit = level - 1 if part == 0 else self.depth - level
-        own = self.bit(bit)
-        own = own if keep else 1 - own
-        if part == 0:
-            return lax.rem(self.chip, 1 << bit) + own * (1 << bit) + t * (2 << bit), bit
-        return self.chip - lax.rem(self.chip, 2 << bit) + own * (1 << bit) + t, bit
-
-    def pieces(self, level):
-        first = self.count // 2
-        for earlier in range(1, level):
-            first += len(self.parts) * (1 << (self.depth - earlier))
-        for part, low, high in self.parts:
-            for t in range(1 << (self.depth - level)):
-                yield part, slice(low, high), t, first
-                first += 1
-
-    def far_copy(self, level, part, lanes, t, sem):
-        index, bit = self.index(part, level, t, False)
+            mine = pl.ds(pl.multiple_of(base + i * 32, 32), 32)
+            other = pl.ds(pl.multiple_of(first + i * 32, 32), 32)
+            self.terms[mine, lanes] = (
+                self.terms[mine, lanes].astype(F32) + source[other, lanes].astype(F32)
+            ).astype(BF16)
+
+    def add_near(self):
+        for e in self.order:
+            self.near_copy(e).wait_recv()
+            self.add(e, self.near, e * self.chunk, slice(0, self.width))
+            for part in self.lanes:
+                if self.sent(1, part, e):
+                    self.far_copy(1, part, e).start()
+
+    def bit(self, level, part):
+        return level - 1 if part == 0 else self.depth - level
+
+    def sent(self, level, part, e):
+        bit = self.bit(level, part)
+        return e >> bit & 1 and (e & ((1 << bit) - 1) if part == 0 else e >> (bit + 1)) == 0
+
+    def slot(self, level, part, e):
+        bit = self.bit(level, part)
+        return e >> (bit + 1) if part == 0 else e & ((1 << bit) - 1)
+
+    def place(self, level):
+        return sum(self.terms.shape[0] >> (earlier + 1) for earlier in range(1, level))
+
+    def far_copy(self, level, part, e):
+        bit = self.bit(level, part)
+        sem = self.half + sum(len(self.lanes) * (self.half >> earlier) for earlier in range(1, level))
+        sem += list(self.lanes).index(part) * (self.half >> level) + self.slot(level, part, e)
+        first = self.place(level) + self.slot(level, part, e) * self.chunk
         return pltpu.make_async_remote_copy(
-            src_ref=self.terms.at[rows_of(2 * index + self.core, self.chunk), lanes],
-            dst_ref=self.far.at[pl.ds(self.place(level) + t * self.chunk, self.chunk), lanes],
+            src_ref=self.terms.at[
+                pl.ds(pl.multiple_of(self.row(e, self.core), self.chunk), self.chunk), self.lanes[part]
+            ],
+            dst_ref=self.far.at[first : first + self.chunk, self.lanes[part]],
             send_sem=self.send.at[sem],
             recv_sem=self.recv.at[sem],
-            device_id=(self.cp + 2 * self.step(bit), self.tp),
+            device_id=(self.cp + 2 * self.flip(1 << bit), self.tp),
             device_id_type=MESH,
         )
 
-    def send_far(self, level):
-        for piece in self.pieces(level):
-            self.far_copy(level, *piece).start()
-
-    def add_far(self, level):
-        for part, lanes, t, sem in self.pieces(level):
-            self.far_copy(level, part, lanes, t, sem).wait_recv()
-            index, _ = self.index(part, level, t, True)
-            base = (2 * index + self.core) * self.chunk
-            there = self.place(level) + t * self.chunk
-
-            @functools.partial(loop, self.chunk // 64)
-            def _(i, base=base, lanes=lanes, there=there):
-                mine = pl.ds(pl.multiple_of(base + i * 64, 64), 64)
-                other = pl.ds(pl.multiple_of(there + i * 64, 64), 64)
-                self.terms[mine, lanes] = (
-                    self.terms[mine, lanes].astype(F32) + self.far[other, lanes].astype(F32)
-                ).astype(BF16)
-
-    def place(self, level):
-        return sum(self.terms.shape[0] >> (earlier + 1) for earlier in range(1, level))
+    def coming(self, level, passed_on):
+        for e in self.order:
+            for part in self.lanes:
+                if self.sent(level, part, e):
+                    kept = e ^ (1 << self.bit(level, part))
+                    if (level < self.depth and bool(self.sent(level + 1, part, kept))) == passed_on:
+                        yield part, e, kept
+
+    def arrive(self, level, part, e, kept):
+        self.far_copy(level, part, e).wait_recv()
+        self.add(kept, self.far, self.place(level) + self.slot(level, part, e) * self.chunk, self.lanes[part])
+
+    def pass_on(self, level):
+        for part, e, kept in self.coming(level, True):
+            self.arrive(level, part, e, kept)
+            self.far_copy(level + 1, part, kept).start()
+
+    def keep(self, level):
+        for part, e, kept in self.coming(level, False):
+            self.arrive(level, part, e, kept)
+
+    def between(self):
+        for level in range(2, self.depth):
+            self.pass_on(level)
+            self.keep(level)
 
     def finish(self, write):
         level = self.depth
-        mine = rows_of(self.cp, self.chunk)
-        for part, lanes, t, sem in self.pieces(level):
-            self.far_copy(level, part, lanes, t, sem).wait_recv()
+        mine = pl.ds(pl.multiple_of(self.row(0, self.core), self.chunk), self.chunk)
+        for part, e, _ in self.coming(level, False):
+            self.far_copy(level, part, e).wait_recv()
+            lanes = self.lanes[part]
             for tile in range(lanes.start // 512, lanes.stop // 512):
                 cut = slice(tile * 512, (tile + 1) * 512)
                 other = pl.ds(self.place(level), self.chunk)
                 write(tile, self.terms[mine, cut].astype(F32) + self.far[other, cut].astype(F32))
 
     def drain(self):
-        loop(self.count // 2, lambda t: self.near_copy(t).wait_send())
-        for level in range(1, self.depth + 1):
-            for piece in self.pieces(level):
-                self.far_copy(level, *piece).wait_send()
+        for e in self.order:
+            self.near_copy(e).wait_send()
+            for part in self.lanes:
+                for level in range(1, self.depth + 1):
+                    if self.sent(level, part, e):
+                        self.far_copy(level, part, e).wait_send()
 
 
 def scatter_scratch(depth, width, split):
@@ -401,37 +436,35 @@
         norm_v[at] = (centred * lax.rsqrt(var + EPS) * gains[0:1] + shifts[0:1]).astype(BF16)
 
     stores["norm1"].start()
-    pairs = heads // 2
-
-    def exchange(kind, p):
-        lanes = slice(p * 2 * HD, (p + 1) * 2 * HD)
+    chunks = rows // CHUNK
+
+    def exchange(kind, c=0):
+        cut = slice(c * CHUNK, (c + 1) * CHUNK)
         source, target, device = (
-            (q_v.at[:, lanes], q_next.at[:, lanes], before),
-            (cross.at[lanes], cross_in.at[lanes], after),
-            (lse_cross, lse_in, after),
+            (q_v.at[cut], q_next.at[cut], before),
+            (cross.at[c], cross_in.at[c], after),
+            (lse_cross.at[c], lse_in.at[c], after),
             (kv.at[rows_of(core, rows)], kv.at[rows_of(core, rows)], sibling),
         )[kind]
-        sem = (p, pairs + p, 2 * pairs, 2 * pairs + 1)[kind]
+        sem = kind * chunks + c
         return pltpu.make_async_remote_copy(
             src_ref=source, dst_ref=target, send_sem=x_send.at[sem], recv_sem=x_recv.at[sem],
             device_id=device, device_id_type=MESH,
         )
 
-    queries = [exchange(0, p) for p in range(pairs)]
-    gathered = [exchange(1, p) for p in range(pairs)] + [exchange(2, 0)]
-    to_near = exchange(3, 0)
+    queries = [exchange(0, c) for c in range(chunks)]
+    gathered = [[exchange(1, c), exchange(2, c)] for c in range(chunks)]
+    to_near = exchange(3)
     has_before, has_after = chip > 0, chip < chips - 1
     loads[1].wait()
 
-    @functools.partial(loop, rows // CHUNK)
-    def _(i):
-        at = rows_of(i, CHUNK)
+    for c in range(chunks):
+        at = slice(c * CHUNK, (c + 1) * CHUNK)
         q_v[at] = (dot(norm_v[at], up_v[:, :width]) + bqv[0:1]).astype(BF16)
 
-    @pl.when(has_before)
-    def _():
-        for item in queries:
-            item.start()
+        @pl.when(has_before)
+        def _(c=c):
+            queries[c].start()
 
     @pl.when(jnp.logical_not(has_after))
     def _():
@@ -491,37 +524,41 @@
             mixed = mixed + dot(v_t[feature, b * rows : (b + 1) * rows], p.astype(BF16))
         return mixed / mass, top + jnp.log(mass)
 
-    def cross_pair(p):
-        start = p * 2 * HD
-        lanes = pl.ds(start, 2 * HD)
-        queries[p].wait_recv()
-        value = q_next[:, lanes].astype(F32).T * (HD ** -0.5)
-        for parity in range(2):
-            q_t_next[parity] = turned(value, parity)
-
-        @functools.partial(loop, 2)
-        def _(parity):
-            h = 2 * p + parity
+    def cross_chunk(c):
+        columns = slice(c * CHUNK, (c + 1) * CHUNK)
+        queries[c].wait_recv()
+        value = q_next[columns].astype(F32).T * (HD ** -0.5)
+        for h in range(heads):
+            q_t_next[h] = turned(value[(h // 2) * 2 * HD : (h // 2 + 1) * 2 * HD], h)
+
+        @functools.partial(loop, heads)
+        def _(h):
+            lanes = pl.ds(pl.multiple_of(lax.div(h, 2) * 2 * HD, 2 * HD), 2 * HD)
             feature = pl.ds(pl.multiple_of(h * HD, HD), HD)
-            for c in range(rows // CHUNK):
-                columns = slice(c * CHUNK, (c + 1) * CHUNK)
-                mixed, lse_row = attend(q_t_next[parity, :, columns], lanes, feature, lambda b, s: s + bias)
-                cross[feature, columns] = mixed.astype(BF16)
-                lse_cross[pl.ds(h, 1), columns] = lse_row
-
-        gathered[p].start()
-
-    @pl.when(has_after)
-    def _():
-        for p in range(pairs):
-            cross_pair(p)
-        gathered[pairs].start()
-
-    stores["q_next"].start()
+            mixed, lse_row = attend(q_t_next[h], lanes, feature, lambda b, s: s + bias)
+            cross[c, feature] = mixed.astype(BF16)
+            lse_cross[c, pl.ds(h, 1)] = lse_row
+            if c > 0:
+                @pl.when(lax.rem(h, 4) == 3)
+                def _():
+                    line1.tick(lax.div(h, 4))
+
+        for item in gathered[c]:
+            item.start()
+
     loads[4].wait()
 
     for c in range(rows // CHUNK):
         columns = slice(c * CHUNK, (c + 1) * CHUNK)
+
+        @pl.when(has_after)
+        def _(c=c):
+            cross_chunk(c)
+
+        if c > 0:
+            @pl.when(jnp.logical_not(has_after))
+            def _():
+                loop(2, line1.tick)
 
         def causal(b, s, c=c):
             key = lax.broadcasted_iota(jnp.int32, (rows, CHUNK), 0) + b * rows
@@ -535,18 +572,18 @@
             att_t[feature, columns] = mixed
             lse_out[pl.ds(h, 1), columns] = lse_row
             if c > 0:
-                @pl.when(lax.rem(h, 2) == 1)
+                @pl.when(lax.rem(h, 4) == 3)
                 def _():
-                    line1.tick(lax.div(h, 2))
+                    line1.tick(2 + lax.div(h, 4))
 
         loop(heads, head)
-        if c == 0:
-            @pl.when(has_before)
-            def _():
-                for item in gathered:
-                    item.wait_recv()
-
-        mine, other = lse_out[:, columns], lse_in[:, columns]
+
+        @pl.when(has_before)
+        def _(c=c):
+            for item in gathered[c]:
+                item.wait_recv()
+
+        mine, other = lse_out[:, columns], lse_in[c]
         top = jnp.maximum(mine, other)
         both = top + jnp.log(jnp.exp(mine - top) + jnp.exp(other - top))
         share, share_in = jnp.exp(mine - both), jnp.exp(other - both)
@@ -555,7 +592,7 @@
             feature = slice(h * HD, (h + 1) * HD)
             att_t[feature, columns] = (
                 att_t[feature, columns] * share[h : h + 1]
-                + cross_in[feature, columns].astype(F32) * share_in[h : h + 1]
+                + cross_in[c, feature].astype(F32) * share_in[h : h + 1]
             )
         att_v[columns] = att_t[:, columns].T.astype(BF16)
 
@@ -566,6 +603,7 @@
 
         loop(per_chunk, lambda s, c=c: line1.push(s + c * per_chunk))
 
+    stores["q_next"].start()
     stores["att"].start()
     stores["att_t"].start()
     acc[...] = jnp.zeros_like(acc)
@@ -634,7 +672,7 @@
         second_norm(per_chunk + 5 + 2 * i)
     stores["sum1"].start()
     stores["norm2"].start()
-    line1.drain_all(count)
+    line1.drain_all()
     feed_forward(1, lambda i: line2.tick(2 + i))
     stores["g_pre"].start()
     stores["sum1"].wait()
@@ -660,30 +698,21 @@
         line2.tick(s)
         back(s - LAG)
 
-    def term(k):
-        scatter.fill(k, lambda tile, at: (d_v[:, at], act_v[:, tile * 512 : (tile + 1) * 512]))
+    def pick(tile, at):
+        return d_v[:, at], act_v[:, tile * 512 : (tile + 1) * 512]
 
     def project(k):
         chunk = rows_of(lax.div(k, depth // 512), CHUNK)
         lanes = rows_of(lax.rem(k, depth // 512), 512)
         ffn_v[chunk, lanes] = dot(act_v[chunk], down_v[:, lanes]).astype(BF16)
 
-    blocks, half = scatter.blocks(), scatter.count // 2
-
-    @functools.partial(loop, 2)
-    def _(i):
-        loop(blocks // 2, lambda j: term(i * (blocks // 2) + j))
-
-        @pl.when((i == 0) if scatter.block == scatter.chunk else (i == 1))
-        def _():
-            loop(half, scatter.send_near)
-
-        line2.tick(6 + i)
-
+    scatter.fill_near(pick)
+    line2.tick(6)
+    scatter.fill_own(pick)
+    line2.tick(7)
+    scatter.add_near()
     line2.tick(8)
-    loop(half, scatter.add_near)
-    scatter.send_far(1)
-    loop(4, lambda i: back(i))
+    loop(4, back)
 
     @functools.partial(loop, 4)
     def _(i):
@@ -691,11 +720,12 @@
         project(2 * i + 1)
         ahead(9 + i)
 
+    scatter.pass_on(1)
     stores["ffn"].start()
-    loop(count + 2 - 13, lambda i: ahead(13 + i))
-    for level in range(1, scatter.depth):
-        scatter.add_far(level)
-        scatter.send_far(level + 1)
+    loop(3, lambda i: ahead(13 + i))
+    scatter.keep(1)
+    scatter.between()
+    loop(count + 2 - 16, lambda i: ahead(16 + i))
     loop(LAG - 2, lambda i: back(count - LAG + 2 + i))
     stores["g_hidden"].start()
     stores["g_attn"].start()
@@ -709,7 +739,7 @@
 
     scatter.finish(write)
     scatter.drain()
-    line2.drain_all(count)
+    line2.drain_all()
 
     to_near.wait_send()
 
@@ -720,8 +750,9 @@
 
     @pl.when(has_after)
     def _():
-        for item in gathered:
-            item.wait_send()
+        for items in gathered:
+            for item in items:
+                item.wait_send()
 
     for name in ("q", "q_next", "kv", "att", "att_t", "norm2", "g_pre", "ffn", "g_hidden", "g_attn"):
         stores[name].wait()
@@ -733,7 +764,6 @@
     heads = width // HD
     hidden = w_up.shape[1]
     chunk = depth // lax.axis_size("cp")
-    count = rows // SUB
     shape = jax.ShapeDtypeStruct
     return pl.pallas_call(
         front_kernel,
@@ -766,25 +796,24 @@
             pltpu.VMEM((rows, width), BF16),
             pltpu.VMEM((2 * rows, 2 * width), BF16),
             pltpu.VMEM((heads, 2 * HD, rows), BF16),
-            pltpu.VMEM((2, 2 * HD, rows), BF16),
+            pltpu.VMEM((heads, 2 * HD, CHUNK), BF16),
             pltpu.VMEM((width, depth), BF16),
             pltpu.VMEM((width, rows), F32),
             pltpu.VMEM((rows, width), BF16),
-            pltpu.VMEM((width, rows), BF16),
-            pltpu.VMEM((width, rows), BF16),
-            pltpu.VMEM((heads, rows), F32),
-            pltpu.VMEM((heads, rows), F32),
+            pltpu.VMEM((rows // CHUNK, width, CHUNK), BF16),
+            pltpu.VMEM((rows // CHUNK, width, CHUNK), BF16),
+            pltpu.VMEM((rows // CHUNK, heads, CHUNK), F32),
+            pltpu.VMEM((rows // CHUNK, heads, CHUNK), F32),
             pltpu.VMEM((rows, depth), F32),
             pltpu.VMEM((rows, 128), F32),
             pltpu.VMEM((rows, hidden), BF16),
             pltpu.VMEM((rows, hidden), BF16),
             pltpu.VMEM((5, 8, depth), F32),
             *[pltpu.VMEM((rows, depth), BF16)] * 5,
-            pltpu.SemaphoreType.DMA((2, 3, count)),
-            pltpu.SemaphoreType.DMA((2, 3, count)),
+            *[pltpu.SemaphoreType.DMA((2, 3, rows // PIECE))] * 2,
             *scatter_scratch(depth, hidden, SPLIT_DOWN),
-            pltpu.SemaphoreType.DMA((heads + 2,)),
-            pltpu.SemaphoreType.DMA((heads + 2,)),
+            pltpu.SemaphoreType.DMA((3 * (rows // CHUNK) + 1,)),
+            pltpu.SemaphoreType.DMA((3 * (rows // CHUNK) + 1,)),
             pltpu.SemaphoreType.DMA((8,)),
             pltpu.SemaphoreType.DMA((13,)),
         ],
@@ -842,16 +871,13 @@
     loads[1].wait()
     loads[2].wait()
     loop(count, line.push)
-    blocks, half = scatter.blocks(), scatter.count // 2
-
-    def term(k):
-        scatter.fill(k, lambda tile, at: (norm_v[:, at], g_pre_v[:, tile * 512 : (tile + 1) * 512]))
+
+    def pick(tile, at):
+        return norm_v[:, at], g_pre_v[:, tile * 512 : (tile + 1) * 512]
 
     for item in loads[5:]:
         item.start()
-    loop(blocks // 2, term)
-    if scatter.block == scatter.chunk:
-        loop(half, scatter.send_near)
+    scatter.fill_near(pick)
     relay = line.tick
     relay(0)
     for item in loads[3:]:
@@ -905,9 +931,8 @@
             item.start()
 
     relay(1)
-    loop(blocks - blocks // 2, lambda k: term(blocks // 2 + k))
-    if scatter.block != scatter.chunk:
-        loop(half, scatter.send_near)
+    scatter.fill_own(pick)
+    scatter.add_near()
 
     @pl.when(jnp.logical_not(has_after))
     def _():
@@ -918,9 +943,6 @@
     def _():
         got_q[...] = jnp.zeros_like(got_q)
 
-    turn(g_v, g_t, 1.0)
-    turn(q_v, q_t, scale)
-
     @functools.partial(loop, 2)
     def _(i):
         at = rows_of(i, rows)
@@ -936,8 +958,6 @@
         acc[rows_of(i, 64)] = jnp.zeros((64, 2 * width), F32)
 
     relay(2)
-    loop(half, scatter.add_near)
-    scatter.send_far(1)
 
     def head(h, q_rows, g_rows, numbers, g_q_t, mask):
         offset = lax.div(h, 2) * 2 * HD
@@ -966,14 +986,6 @@
         row = lax.broadcasted_iota(jnp.int32, (rows, CHUNK), 1) + c * CHUNK
         return jnp.where(key <= row + core * rows, s - lse_row, NEG)
 
-    @functools.partial(loop, heads)
-    def _(h):
-        head(h, q_v, g_v, stats, att_t, causal)
-
-        @pl.when(h < heads - 2)
-        def _():
-            relay(3 + h)
-
     @pl.when(has_after)
     def _():
         for item in to_before:
@@ -981,25 +993,37 @@
 
     turn(g_next, g_t, 1.0)
     turn(q_next, q_t, scale)
-    relay(9)
+    relay(3)
     for p in range(pairs):
 
         @functools.partial(loop, 2)
         def _(parity, p=p):
             head(2 * p + parity, q_next, g_next, stats_next, g_q_next, lambda b, c, s, row: s + (bias - row))
-            relay(10 + 2 * p + parity)
 
         pair = slice(p * 2 * HD, (p + 1) * 2 * HD)
         give_q[pair] = g_q_next[pair].astype(BF16)
 
         @pl.when(has_after)
+        def _(p=p):
+            to_after[p].start()
+
+        relay(4 + p)
+
+    turn(g_v, g_t, 1.0)
+    turn(q_v, q_t, scale)
+    relay(8)
+
+    @functools.partial(loop, heads)
+    def _(h):
+        head(h, q_v, g_v, stats, att_t, causal)
+
+        @pl.when(lax.rem(h, 2) == 1)
         def _():
-            to_after[p].start()
-
-    levels = scatter.depth
-    for level in range(1, levels):
-        scatter.add_far(level)
-        scatter.send_far(level + 1)
+            relay(9 + lax.div(h, 2))
+
+        @pl.when(h == 4)
+        def _():
+            scatter.pass_on(1)
 
     @functools.partial(loop, rows // 64)
     def _(i):
@@ -1007,6 +1031,9 @@
         give_near[rows_of(i, 64)] = acc[at].astype(BF16)
 
     to_near.start()
+    scatter.keep(1)
+    scatter.between()
+    relay(13)
     to_near.wait_recv()
 
     @functools.partial(loop, rows // 64)
@@ -1028,6 +1055,7 @@
         both = att_t[:, at] + got_q[:, at].astype(F32)
         g_qkv_v[at, :width] = (both.T * scale).astype(BF16)
 
+    loop(count + 2 - 14, lambda i: relay(14 + i))
     stores = [
         pltpu.make_async_copy(g_qkv_v, g_qkv_hbm, store_sem.at[0]),
         pltpu.make_async_copy(total, ffn_sum_hbm, store_sem.at[1]),
@@ -1041,7 +1069,7 @@
 
     scatter.finish(write)
     scatter.drain()
-    line.drain_all(count)
+    line.drain_all()
     to_near.wait_send()
 
     @pl.when(has_before)
@@ -1113,10 +1141,10 @@
 def last_kernel(
     g_qkv_hbm, wqkv_hbm, x_hbm, g_hidden_hbm, norm_hbm, g_attn_hbm, att_hbm, attn_sum_hbm, ffn_sum_hbm,
     lengths_ref, until_ref, gains, b_outs, sums_in,
-    g_x_hbm, out_hbm, qkv_out, w_out_out, gains_out, shifts_out, bqv_out, bouts_out, bup_out,
-    g_qkv_v, w_v, x_v, g_hidden, norm_v, g_attn_v, att_v, attn_sum, ffn_sum, out_v, acc, small, small_got, late, late_got,
+    g_x, out, qkv_out, w_out_out, gains_out, shifts_out, bqv_out, bouts_out, bup_out,
+    g_qkv_v, w_v, x_v, norm_v, g_attn_v, att_v, attn_sum, ffn_sum, acc, small, small_got, late, late_got,
     terms, near, far, rs_send, rs_recv,
-    part, slot_a, slot_b, total, ar_send, ar_recv, small_send, small_recv, load_sem, store_sem,
+    part, slot_a, slot_b, total, ar_send, ar_recv, small_send, small_recv, load_sem,
 ):
     cp, tp, core, chip = place()
     rows, depth = x_v.shape
@@ -1132,7 +1160,7 @@
                 (g_attn_hbm, g_attn_v),
                 (att_hbm, att_v),
                 (x_hbm, x_v),
-                (g_hidden_hbm, g_hidden),
+                (g_hidden_hbm, g_x),
                 (attn_sum_hbm, attn_sum),
                 (ffn_sum_hbm, ffn_sum),
             )
@@ -1209,14 +1237,12 @@
         hat = centred * scale
         t = e * gains[0:1]
         along = t - jnp.mean(t, axis=-1, keepdims=True) - hat * jnp.mean(t * hat, axis=-1, keepdims=True)
-        g_hidden[at] = g_hidden[at] + along * scale
+        g_x[at] = g_x[at] + along * scale
         row = lax.broadcasted_iota(jnp.int32, (SUB, 1), 0) + s * SUB
         branches = attn_sum[at].astype(F32) + b_outs[0:1] + (ffn_sum[at].astype(F32) + b_outs[1:2])
-        out_v[at] = v + jnp.where(row < live, branches, 0.0)
+        out[at] = v + jnp.where(row < live, branches, 0.0)
         acc[0] += fold(e * hat)
         acc[1] += fold(e)
-        pltpu.make_async_copy(g_hidden.at[at], g_x_hbm.at[at], store_sem.at[0, s]).start()
-        pltpu.make_async_copy(out_v.at[at], out_hbm.at[at], store_sem.at[1, s]).start()
 
     behind = 4
 
@@ -1227,37 +1253,23 @@
         def _():
             back(s - behind)
 
-    def term(k):
-        def pick(tile, at):
-            if tile < 3:
-                return norm_v[:, at], g_qkv_v[:, tile * width : (tile + 1) * width]
-            return g_attn_v[:, at], att_v[...]
-
-        scatter.fill(k, pick)
-
-    blocks, half = scatter.blocks(), scatter.count // 2
-
-    @functools.partial(loop, 4)
-    def _(i):
-        loop(blocks // 4, lambda j: term(i * (blocks // 4) + j))
-
-        @pl.when((i == 1) if scatter.block == scatter.chunk else (i == 3))
-        def _():
-            loop(half, scatter.send_near)
-
-        ahead(i)
-
-    @functools.partial(loop, 2)
-    def _(i):
-        loop(half // 2, lambda j: scatter.add_near(i * (half // 2) + j))
-        ahead(4 + i)
-
-    scatter.send_far(1)
-    loop(8, lambda i: ahead(6 + i))
-    for level in range(1, scatter.depth):
-        scatter.add_far(level)
-        scatter.send_far(level + 1)
-    loop(count + 2 - 14, lambda i: ahead(14 + i))
+    def pick(tile, at):
+        if tile < 3:
+            return norm_v[:, at], g_qkv_v[:, tile * width : (tile + 1) * width]
+        return g_attn_v[:, at], att_v[...]
+
+    scatter.fill_near(pick)
+    ahead(0)
+    ahead(1)
+    scatter.fill_own(pick)
+    ahead(2)
+    scatter.add_near()
+    loop(9 - 3, lambda i: ahead(3 + i))
+    scatter.pass_on(1)
+    loop(13 - 9, lambda i: ahead(9 + i))
+    scatter.keep(1)
+    scatter.between()
+    loop(count + 2 - 13, lambda i: ahead(13 + i))
     loop(behind - 2, lambda i: back(count + 2 - behind + i))
 
     for k in range(2):
@@ -1282,7 +1294,7 @@
     shifts_out[0:1] = final[1:2]
     shifts_out[1:2] = early[1:2]
     scatter.drain()
-    line.drain_all(count)
+    line.drain_all()
 
     @functools.partial(loop, bands - 1)
     def _(k):
@@ -1290,45 +1302,38 @@
         small_copy(0, cp, other).wait_send()
         small_copy(1, cp, other).wait_send()
 
-    @functools.partial(loop, count)
-    def _(s):
-        at = rows_of(s, SUB)
-        pltpu.make_async_copy(g_hidden.at[at], g_x_hbm.at[at], store_sem.at[0, s]).wait()
-        pltpu.make_async_copy(out_v.at[at], out_hbm.at[at], store_sem.at[1, s]).wait()
-
 
 def last(g_qkv, wqkv, x, g_hidden, norm1, g_attn, att, attn_sum, ffn_sum, lengths, until, gains, b_outs, sums):
     rows, depth = x.shape
     width = att.shape[1]
     bands = lax.axis_size("cp")
     chunk = depth // bands
-    shape = jax.ShapeDtypeStruct
+    pinned = bands <= 8
+    result = pltpu.VMEM if pinned else jax.ShapeDtypeStruct
     return pl.pallas_call(
         last_kernel,
         out_shape=(
-            shape((rows, depth), F32),
-            shape((rows, depth), F32),
-            shape((3, chunk, width), F32),
-            shape((width, chunk), F32),
-            shape((2, depth), F32),
-            shape((2, depth), F32),
-            shape((2, width), F32),
-            shape((2, depth), F32),
-            shape((1, depth), F32),
+            result((rows, depth), F32),
+            result((rows, depth), F32),
+            result((3, chunk, width), F32),
+            result((width, chunk), F32),
+            result((2, depth), F32),
+            result((2, depth), F32),
+            result((2, width), F32),
+            result((2, depth), F32),
+            result((1, depth), F32),
         ),
         in_specs=[ANY] * 9 + [IN_SMEM] * 2 + [IN_VMEM] * 3,
-        out_specs=(ANY,) * 2 + (IN_VMEM,) * 7,
+        out_specs=(IN_VMEM,) * 9,
         scratch_shapes=[
             pltpu.VMEM((rows, 3 * width), BF16),
             pltpu.VMEM((3, depth, width), BF16),
             pltpu.VMEM((rows, depth), BF16),
-            pltpu.VMEM((rows, depth), F32),
             pltpu.VMEM((rows, depth), BF16),
             pltpu.VMEM((rows, depth), BF16),
             pltpu.VMEM((rows, width), BF16),
             pltpu.VMEM((rows, depth), BF16),
             pltpu.VMEM((rows, depth), BF16),
-            pltpu.VMEM((rows, depth), F32),
             pltpu.VMEM((2, 8, depth), F32),
             pltpu.VMEM((8, depth), F32),
             pltpu.VMEM((bands, 8, depth), F32),
@@ -1340,9 +1345,8 @@
             pltpu.SemaphoreType.DMA((2, bands)),
             pltpu.SemaphoreType.DMA((2, bands)),
             pltpu.SemaphoreType.DMA((9,)),
-            pltpu.SemaphoreType.DMA((2, rows // SUB)),
         ],
-        compiler_params=pltpu.CompilerParams(collective_id=3, has_side_effects=True, vmem_limit_bytes=62 * 2**20),
+        compiler_params=pltpu.CompilerParams(collective_id=3, has_side_effects=True, vmem_limit_bytes=(48 if pinned else 62) * 2**20),
         name="last",
     )(g_qkv, wqkv, x, g_hidden, norm1, g_attn, att, attn_sum, ffn_sum, lengths, until, gains, b_outs, sums)
 

time: 315 us -> 304 us (0.965)
  Pallas kernels: 299 us -> 289 us
    pallas_call x1, Pallas kernels: 152 us -> 142 us  [front(): pl.pallas_call(front_kernel, out_shape=(shape((rows, depth), BF16), shape...]
    pallas_call x1, Pallas kernels: 70.2 us -> 76.1 us  [grad_attend(): pl.pallas_call(grad_attend_kernel, out_shape=(shape((rows, 3 * width), BF...]
    pallas_call x1, Pallas kernels: 76.5 us -> 71.3 us  [last(): pl.pallas_call(last_kernel, out_shape=(result((rows, depth), F32), result...]
    unnamed x31 -> x15, local copies, waits for them, and re-layouts: 14.9 us -> 13.7 us
where the time goes in v6:
time: 304 us
  Pallas kernels  289 us (95%)
  local copies, waits for them, and re-layouts  13.7 us (5%)
    pallas_call x1, Pallas kernels, front(): pl.pallas_call(front_kernel, out_shape=(shape((rows, depth), BF16), shape...  142 us
    pallas_call x1, Pallas kernels, grad_attend(): pl.pallas_call(grad_attend_kernel, out_shape=(shape((rows, 3 * width), BF...  76.1 us
    pallas_call x1, Pallas kernels, last(): pl.pallas_call(last_kernel, out_shape=(result((rows, depth), F32), result...  71.3 us
    unnamed x15, local copies, waits for them, and re-layouts  13.7 us

profile of v6, /device:TPU:0, one launch (start us, length us, event | category | flops | bytes accessed | tf_op | source)
XLA Modules:
  0.0 303.7 jit_solution(13591611095466309194)
XLA Ops:
  0.6 141.9 %front.1 = (bf16[512,2048]{1,0:T(8,128)(2,1)}, bf16[512,2048]{1,0:T(8,128)(2,1)}, bf16[512,512]{1,0:T(8,128)(2,1)}, bf16[512,512]{1,0:T(8,128)(2,1)}, bf16[1024,...) custom-call(bf16[512,2048]{1,0:T(8,128)(2,1)} %x_hbm.3, ...), custom_call_target="tpu_custom_call" | custom-call | tf_op jit(solution)/shard_map/front/pallas_call | solution.py:768
  142.5 76.1 %grad_attend.1 = (bf16[512,1536]{1,0:T(8,128)(2,1)}, bf16[512,2048]{1,0:T(8,128)(2,1)}, f32[256,2048]{1,0:T(8,128)}) custom-call(bf16[512,2048]{1,0:T(8,128)(2,1)} %get-tuple-element.38.g_attn_hbm, bf16[512,2048]{1,0:T(8,128)(2,1)} %wout_hbm.3, bf16[512,512]{1,0:T(8,128)(2,1)} %get-tuple-element.39.q_hbm, bf16[512,512]{1,0:T(8,128)(2,1)} %get-tuple-element.40.q_next_hbm, ...), custom_call_target="tpu_custom_call" | custom-call | tf_op jit(solution)/shard_map/grad_attend/pallas_call | solution.py:1096
  218.6 71.3 %last.1 = (f32[512,2048]{1,0:T(8,128)S(1)}, f32[512,2048]{1,0:T(8,128)S(1)}, f32[3,256,512]{2,1,0:T(8,128)S(1)}, f32[512,256]{1,0:T(8,128)S(1)}, f32[2,2048]{1,0...) custom-call(bf16[512,1536]{1,0:T(8,128)(2,1)} %get-tuple-element.47., ...), custom_call_target="tpu_custom_call" | custom-call | tf_op jit(solution)/shard_map/last/pallas_call | solution.py:1313
  289.9 2.0 copy.35
  292.0 0.6 copy.40
  292.5 0.6 copy.43
  293.1 0.6 copy.37
  293.7 0.6 copy.38
  294.4 0.6 copy.42
  295.0 0.8 copy.41
  295.8 1.1 copy.39
  296.9 0.0 copy-start.1
  296.9 2.1 copy.36
  299.0 1.0 copy-done.1
  300.0 0.0 copy-start
  300.0 1.3 copy.44
  301.3 1.0 copy-done
  302.3 1.3 copy.45
Async XLA Ops:
  296.9 3.1 %copy-start.1 = (f32[256,2048]{1,0:T(8,128)S(1)}, f32[256,2048]{1,0:T(8,128)}, u32[]{:S(2)}) copy-start(f32[256,2048]{1,0:T(8,128)} %get-tuple-element.95) | copy-start | bytes 6291460
  300.0 2.3 copy-start

commit v7 on v6

--- a/solution.py
+++ b/solution.py
@@ -1140,8 +1140,8 @@
 
 def last_kernel(
     g_qkv_hbm, wqkv_hbm, x_hbm, g_hidden_hbm, norm_hbm, g_attn_hbm, att_hbm, attn_sum_hbm, ffn_sum_hbm,
-    lengths_ref, until_ref, gains, b_outs, sums_in,
-    g_x, out, qkv_out, w_out_out, gains_out, shifts_out, bqv_out, bouts_out, bup_out,
+    up_hbm, down_hbm, lengths_ref, until_ref, gains, b_outs, sums_in,
+    g_x, out, up_out, down_out, qkv_out, w_out_out, gains_out, shifts_out, bqv_out, bouts_out, bup_out,
     g_qkv_v, w_v, x_v, norm_v, g_attn_v, att_v, attn_sum, ffn_sum, acc, small, small_got, late, late_got,
     terms, near, far, rs_send, rs_recv,
     part, slot_a, slot_b, total, ar_send, ar_recv, small_send, small_recv, load_sem,
@@ -1163,6 +1163,8 @@
                 (g_hidden_hbm, g_x),
                 (attn_sum_hbm, attn_sum),
                 (ffn_sum_hbm, ffn_sum),
+                (up_hbm, up_out),
+                (down_hbm, down_out),
             )
         )
     ]
@@ -1303,7 +1305,7 @@
         small_copy(1, cp, other).wait_send()
 
 
-def last(g_qkv, wqkv, x, g_hidden, norm1, g_attn, att, attn_sum, ffn_sum, lengths, until, gains, b_outs, sums):
+def last(g_qkv, wqkv, x, g_hidden, norm1, g_attn, att, attn_sum, ffn_sum, g_up, g_down, lengths, until, gains, b_outs, sums):
     rows, depth = x.shape
     width = att.shape[1]
     bands = lax.axis_size("cp")
@@ -1315,6 +1317,8 @@
         out_shape=(
             result((rows, depth), F32),
             result((rows, depth), F32),
+            result(g_up.shape, F32),
+            result(g_down.shape, F32),
             result((3, chunk, width), F32),
             result((width, chunk), F32),
             result((2, depth), F32),
@@ -1323,8 +1327,8 @@
             result((2, depth), F32),
             result((1, depth), F32),
         ),
-        in_specs=[ANY] * 9 + [IN_SMEM] * 2 + [IN_VMEM] * 3,
-        out_specs=(IN_VMEM,) * 9,
+        in_specs=[ANY] * 11 + [IN_SMEM] * 2 + [IN_VMEM] * 3,
+        out_specs=(IN_VMEM,) * 11,
         scratch_shapes=[
             pltpu.VMEM((rows, 3 * width), BF16),
             pltpu.VMEM((3, depth, width), BF16),
@@ -1344,11 +1348,11 @@
             *line_scratch(rows, depth),
             pltpu.SemaphoreType.DMA((2, bands)),
             pltpu.SemaphoreType.DMA((2, bands)),
-            pltpu.SemaphoreType.DMA((9,)),
+            pltpu.SemaphoreType.DMA((11,)),
         ],
-        compiler_params=pltpu.CompilerParams(collective_id=3, has_side_effects=True, vmem_limit_bytes=(48 if pinned else 62) * 2**20),
+        compiler_params=pltpu.CompilerParams(collective_id=3, has_side_effects=True, vmem_limit_bytes=(45 if pinned else 62) * 2**20),
         name="last",
-    )(g_qkv, wqkv, x, g_hidden, norm1, g_attn, att, attn_sum, ffn_sum, lengths, until, gains, b_outs, sums)
+    )(g_qkv, wqkv, x, g_hidden, norm1, g_attn, att, attn_sum, ffn_sum, g_up, g_down, lengths, until, gains, b_outs, sums)
 
 
 def shards(
@@ -1374,8 +1378,8 @@
     g_qkv_rows, ffn_sum, g_up = grad_attend(
         g_attn, w_out, q, q_next, kv, att_t, lse, seq_lengths, active_until, ffn_low, norm2, g_pre
     )
-    g_x, out, g_qkv, g_out, g_ln_gains, g_ln_shifts, g_bqv, g_bouts, g_bup = last(
-        g_qkv_rows, wqkv, layer_input, g_hidden, norm1, g_attn, att, attn_sum, ffn_sum,
+    g_x, out, g_up, g_down, g_qkv, g_out, g_ln_gains, g_ln_shifts, g_bqv, g_bouts, g_bup = last(
+        g_qkv_rows, wqkv, layer_input, g_hidden, norm1, g_attn, att, attn_sum, ffn_sum, g_up, g_down,
         seq_lengths, active_until, ln_gains, b_outs, sums,
     )
     g_qkv = jnp.transpose(g_qkv, (1, 0, 2))

time: 304 us -> 302 us (level)
    unnamed x15 -> x11, local copies, waits for them, and re-layouts: 13.7 us -> 11.6 us
where the time goes in v7:
time: 302 us
  Pallas kernels  290 us (96%)
  local copies, waits for them, and re-layouts  11.6 us (4%)
    pallas_call x1, Pallas kernels, front(): pl.pallas_call(front_kernel, out_shape=(shape((rows, depth), BF16), shape...  142 us
    pallas_call x1, Pallas kernels, grad_attend(): pl.pallas_call(grad_attend_kernel, out_shape=(shape((rows, 3 * width), BF...  76 us
    pallas_call x1, Pallas kernels, last(): pl.pallas_call(last_kernel, out_shape=(result((rows, depth), F32), result...  71.7 us
    unnamed x11, local copies, waits for them, and re-layouts  11.6 us

profile of v7, /device:TPU:0, one launch (start us, length us, event | category | flops | bytes accessed | tf_op | source)
XLA Modules:
  0.0 301.9 jit_solution(15244189999133827205)
XLA Ops:
  0.6 141.9 %front.1 = (bf16[512,2048]{1,0:T(8,128)(2,1)}, bf16[512,2048]{1,0:T(8,128)(2,1)}, bf16[512,512]{1,0:T(8,128)(2,1)}, bf16[512,512]{1,0:T(8,128)(2,1)}, bf16[1024,...) custom-call(bf16[512,2048]{1,0:T(8,128)(2,1)} %x_hbm.3, ...), custom_call_target="tpu_custom_call" | custom-call | tf_op jit(solution)/shard_map/front/pallas_call | solution.py:768
  142.5 76.0 %grad_attend.1 = (bf16[512,1536]{1,0:T(8,128)(2,1)}, bf16[512,2048]{1,0:T(8,128)(2,1)}, f32[256,2048]{1,0:T(8,128)}) custom-call(bf16[512,2048]{1,0:T(8,128)(2,1)} %get-tuple-element.40.g_attn_hbm, bf16[512,2048]{1,0:T(8,128)(2,1)} %wout_hbm.3, bf16[512,512]{1,0:T(8,128)(2,1)} %get-tuple-element.41.q_hbm, bf16[512,512]{1,0:T(8,128)(2,1)} %get-tuple-element.42.q_next_hbm, ...), custom_call_target="tpu_custom_call" | custom-call | tf_op jit(solution)/shard_map/grad_attend/pallas_call | solution.py:1096
  218.5 71.7 %last.1 = (f32[512,2048]{1,0:T(8,128)S(1)}, f32[512,2048]{1,0:T(8,128)S(1)}, f32[256,2048]{1,0:T(8,128)S(1)}, f32[2048,256]{1,0:T(8,128)S(1)}, f32[3,256,512]{2,...) custom-call(bf16[512,1536]{1,0:T(8,128)(2,1)} %get-tuple-element.49., ...), custom_call_target="tpu_custom_call" | custom-call | tf_op jit(solution)/shard_map/last/pallas_call | solution.py:1315
  290.2 2.0 copy.35
  292.3 0.6 copy.40
  292.9 0.6 copy.44
  293.5 0.6 copy.37
  294.1 0.6 copy.38
  294.7 0.6 copy.42
  295.3 0.8 copy.41
  296.1 1.1 copy.39
  297.2 1.3 copy.43
  298.5 1.3 copy.45
  299.8 2.0 copy.36

commit v8 on v7

--- a/solution.py
+++ b/solution.py
@@ -1226,7 +1226,7 @@
         bias = jnp.sum(g_qkv_v[:, 2 * j * width : (2 * j + 1) * width].astype(F32), axis=0, keepdims=True)
         small[5:6, j * width : (j + 1) * width] = bias
     give_small(0)
-    for item in loads[2:]:
+    for item in loads[2:9]:
         item.wait()
 
     def back(s):
@@ -1246,7 +1246,7 @@
         acc[0] += fold(e * hat)
         acc[1] += fold(e)
 
-    behind = 4
+    behind = 3
 
     def ahead(s):
         line.tick(s)
@@ -1290,6 +1290,8 @@
             w_out_out[...] = value.T
 
     scatter.finish(write)
+    for item in loads[9:]:
+        item.wait()
     final = take_small(1)
     gains_out[0:1] = final[0:1]
     gains_out[1:2] = early[0:1]

time: 302 us -> 302 us (level)
  no operation moved by 1% of the time
where the time goes in v8:
time: 302 us; the launch traced here: 301 us
  Pallas kernels  289 us (96%)
  local copies, waits for them, and re-layouts  11.6 us (4%)
    pallas_call x1, Pallas kernels, front(): pl.pallas_call(front_kernel, out_shape=(shape((rows, depth), BF16), shape...  142 us
    pallas_call x1, Pallas kernels, grad_attend(): pl.pallas_call(grad_attend_kernel, out_shape=(shape((rows, 3 * width), BF...  76 us
    pallas_call x1, Pallas kernels, last(): pl.pallas_call(last_kernel, out_shape=(result((rows, depth), F32), result...  71.3 us
    unnamed x11, local copies, waits for them, and re-layouts  11.6 us

profile of v8, /device:TPU:0, one launch (start us, length us, event | category | flops | bytes accessed | tf_op | source)
XLA Modules:
  0.0 301.5 jit_solution(17349740554176319818)
XLA Ops:
  0.6 141.9 %front.1 = (bf16[512,2048]{1,0:T(8,128)(2,1)}, bf16[512,2048]{1,0:T(8,128)(2,1)}, bf16[512,512]{1,0:T(8,128)(2,1)}, bf16[512,512]{1,0:T(8,128)(2,1)}, bf16[1024,...) custom-call(bf16[512,2048]{1,0:T(8,128)(2,1)} %x_hbm.3, ...), custom_call_target="tpu_custom_call" | custom-call | tf_op jit(solution)/shard_map/front/pallas_call | solution.py:768
  142.5 76.0 %grad_attend.1 = (bf16[512,1536]{1,0:T(8,128)(2,1)}, bf16[512,2048]{1,0:T(8,128)(2,1)}, f32[256,2048]{1,0:T(8,128)}) custom-call(bf16[512,2048]{1,0:T(8,128)(2,1)} %get-tuple-element.40.g_attn_hbm, bf16[512,2048]{1,0:T(8,128)(2,1)} %wout_hbm.3, bf16[512,512]{1,0:T(8,128)(2,1)} %get-tuple-element.41.q_hbm, bf16[512,512]{1,0:T(8,128)(2,1)} %get-tuple-element.42.q_next_hbm, ...), custom_call_target="tpu_custom_call" | custom-call | tf_op jit(solution)/shard_map/grad_attend/pallas_call | solution.py:1096
  218.5 71.3 %last.1 = (f32[512,2048]{1,0:T(8,128)S(1)}, f32[512,2048]{1,0:T(8,128)S(1)}, f32[256,2048]{1,0:T(8,128)S(1)}, f32[2048,256]{1,0:T(8,128)S(1)}, f32[3,256,512]{2,...) custom-call(bf16[512,1536]{1,0:T(8,128)(2,1)} %get-tuple-element.49., ...), custom_call_target="tpu_custom_call" | custom-call | tf_op jit(solution)/shard_map/last/pallas_call | solution.py:1317
  289.9 2.0 copy.35
  291.9 0.6 copy.40
  292.5 0.6 copy.44
  293.1 0.6 copy.37
  293.7 0.6 copy.38
  294.3 0.6 copy.42
  294.9 0.8 copy.41
  295.7 1.1 copy.39
  296.8 1.3 copy.43
  298.1 1.3 copy.45
  299.5 2.0 copy.36
